TPU v7x, 32 devices: a whole 2x2x4 slice. The times are simulated.
32 devices in a mesh: event: 4 (over y, core), gx: 2 (over x), gy: 4 (over z).
Axes of the slice: x: 2, y: 2, z: 4, core: 2. Of those that a mesh axis runs over, the one named last changes fastest.
Arguments:
- adjoint_now: float32 [4, 3, 32, 32, 128], P('event', None, 'gx', 'gy'), may hold values from -6 to 6
- adjoint_old: float32 [4, 3, 32, 32, 128], P('event', None, 'gx', 'gy'), may hold values from -6 to 6
- bulk_memory: float32 [4, 3, 32, 32, 128], P('event', None, 'gx', 'gy'), may hold values from -4 to 4
- shear_memory: float32 [4, 3, 3, 32, 32, 128], P('event', None, None, 'gx', 'gy'), may hold values from -4 to 4
- forward_strain: float32 [4, 2, 4, 32, 32, 128], P('event', None, None, 'gx', 'gy'), may hold values from -6 to 6
- bulk_modulus: float32 [32, 32, 128], P('gx', 'gy'), may hold values from 0.5 to 1.5
- shear_modulus: float32 [32, 32, 128], P('gx', 'gy'), may hold values from 0.2 to 0.8
- buoyancy: float32 [32, 32, 128], P('gx', 'gy'), may hold values from 0.5 to 2
- bulk_atten: float32 [32, 32, 128], P('gx', 'gy'), may hold values from 0.05 to 0.5
- shear_atten: float32 [32, 32, 128], P('gx', 'gy'), may hold values from 0.05 to 0.5
- relax_time: float32 [3], replicated, may hold values from 0.3 to 30
- mechanism_weight: float32 [3], replicated, may hold values from 0.5 to 2
- event_slowness: float32 [4, 3], P('event'), may hold values from -1.5 to 1.5
- event_amplitude: float32 [4, 3], P('event'), may hold values from -4 to 4
- event_onset: float32 [4], P('event'), may hold values from -1.5 to 1.5
- boundary_cells: int32 [2, 4, 1024], P('gx', 'gy'), may hold values from 0 to 16383, as said below
- boundary_count: int32 [2, 4], P('gx', 'gy'), may hold values from 1 to 1024, as said below
Outputs:
- adjoint_next: float32 [4, 3, 32, 32, 128], P('event', None, 'gx', 'gy')
- adjoint_before: float32 [4, 3, 32, 32, 128], P('event', None, 'gx', 'gy')
- bulk_next: float32 [4, 3, 32, 32, 128], P('event', None, 'gx', 'gy')
- shear_next: float32 [4, 3, 3, 32, 32, 128], P('event', None, None, 'gx', 'gy')
- grad_bulk: float32 [32, 32, 128], P('gx', 'gy')
- grad_shear: float32 [32, 32, 128], P('gx', 'gy')
Inputs may be any that keep to these rules, and one draw needn't show every extreme that they name: `boundary_cells`: within one device the 1024 cell numbers are distinct. `boundary_count`: devices on the lateral edge of the grid hold 512 to 1024 live cells, and one of them exactly 1024; the others at most 256.
All inputs are finite; a program needn't handle non-finite values.
Results may differ from a plain program's by a relative error of at most 0.0001.
Values sent between devices are 32-bit elements; how exact they have to be, the bound alone decides.
No kernel may reach another device: no remote copies, remote signals or barrier semaphores. Data moves between devices by JAX's collectives and lax.ppermute only.
A program may use at most 64 MiB of HBM per device.

v0:
```python
import jax
import jax.numpy as jnp
from jax import lax
from jax.sharding import PartitionSpec as P

STEPS = 2


time_step = 0.3


def with_halo(block, sides, width):
    for axis, dim in sides:
        count = lax.axis_size(axis)
        forward = [(i, i + 1) for i in range(count - 1)]
        backward = [(target, source) for source, target in forward]
        low = lax.ppermute(
            lax.slice_in_dim(block, block.shape[dim] - width, None, axis=dim), axis, forward
        )
        high = lax.ppermute(lax.slice_in_dim(block, 0, width, axis=dim), axis, backward)
        block = jnp.concatenate([low, block, high], axis=dim)
    return block


def central_div(padded):
    dx = padded[0, 2:, 1:-1] - padded[0, :-2, 1:-1]
    dy = padded[1, 1:-1, 2:] - padded[1, 1:-1, :-2]
    deep = jnp.pad(padded[2, 1:-1, 1:-1], ((0, 0), (0, 0), (1, 1)))
    dz = deep[..., 2:] - deep[..., :-2]
    return 0.5 * (dx + dy + dz)


def laplace(padded):
    centre = padded[:, 1:-1, 1:-1, :]
    total = padded[:, 2:, 1:-1, :] + padded[:, :-2, 1:-1, :]
    total = total + padded[:, 1:-1, 2:, :] + padded[:, 1:-1, :-2, :]
    deep = jnp.pad(centre, ((0, 0), (0, 0), (0, 0), (1, 1)))
    total = total + deep[..., 2:] + deep[..., :-2]
    return total - 6.0 * centre


def gradient(padded):
    along_x = 0.5 * (padded[2:, 1:-1] - padded[:-2, 1:-1])
    along_y = 0.5 * (padded[1:-1, 2:] - padded[1:-1, :-2])
    deep = jnp.pad(padded[1:-1, 1:-1], ((0, 0), (0, 0), (1, 1)))
    along_z = 0.5 * (deep[..., 2:] - deep[..., :-2])
    return jnp.stack([along_x, along_y, along_z], 0)


def ricker(tau):
    return (1.0 - 2.0 * tau * tau) * jnp.exp(-tau * tau)


def body(
    adjoint_now,
    adjoint_old,
    bulk_memory,
    shear_memory,
    forward_strain,
    bulk_modulus,
    shear_modulus,
    buoyancy,
    bulk_atten,
    shear_atten,
    relax_time,
    mechanism_weight,
    event_slowness,
    event_amplitude,
    event_onset,
    boundary_cells,
    boundary_count,
):
    wave = adjoint_now[0]
    older = adjoint_old[0]
    zeta = bulk_memory[0]
    memo = shear_memory[0]
    strain = forward_strain[0]
    width_x, width_y, depth = bulk_modulus.shape
    decay = jnp.exp(-time_step / relax_time)
    gain = (1.0 - decay) * mechanism_weight
    flat = boundary_cells[0, 0]
    slots = jnp.arange(flat.shape[0], dtype=jnp.int32)
    live = (slots < boundary_count[0, 0]).astype(jnp.float32)
    whole_x = lax.axis_index("gx") * width_x + flat // (width_y * depth)
    whole_y = lax.axis_index("gy") * width_y + flat // depth % width_y
    pos_x = whole_x.astype(jnp.float32) / (width_x * lax.axis_size("gx"))
    pos_y = whole_y.astype(jnp.float32) / (width_y * lax.axis_size("gy"))
    pos_z = (flat % depth).astype(jnp.float32) / depth
    slow = event_slowness[0]
    delay = slow[0] * pos_x + slow[1] * pos_y + slow[2] * pos_z
    grad_bulk = jnp.zeros((width_x, width_y, depth), jnp.float32)
    grad_shear = jnp.zeros((width_x, width_y, depth), jnp.float32)
    for step in range(STEPS):
        tau = step * time_step - event_onset[0] - delay
        pulse = ricker(tau) * live
        drive = jnp.zeros((3, width_x * width_y * depth), jnp.float32)
        drive = (
            drive.at[:, flat]
            .add(event_amplitude[0][:, None] * pulse[None, :])
            .reshape(3, width_x, width_y, depth)
        )
        zeta_sum = jnp.sum(zeta, 0)
        padded = with_halo(wave, (("gx", 1), ("gy", 2)), 1)
        diver = central_div(padded)
        lapl = laplace(padded)
        pressure = bulk_modulus * diver - zeta_sum
        pressure_pad = with_halo(pressure, (("gx", 0), ("gy", 1)), 1)
        push = gradient(pressure_pad)
        force = push + shear_modulus * lapl - jnp.sum(memo, 0) + drive
        fresh = 2.0 * wave - older + time_step * time_step * buoyancy * force
        zeta = (
            decay[:, None, None, None] * zeta
            + gain[:, None, None, None] * (bulk_atten * bulk_modulus * diver)[None]
        )
        memo = (
            decay[:, None, None, None, None] * memo
            + gain[:, None, None, None, None] * (shear_atten * shear_modulus * lapl)[None]
        )
        grad_bulk = grad_bulk + bulk_modulus * diver * strain[step, 0]
        grad_shear = grad_shear + shear_modulus * jnp.sum(lapl * strain[step, 1:], 0)
        older = wave
        wave = fresh
    grad_bulk, grad_shear = lax.psum((grad_bulk, grad_shear), "event")
    return (wave[None], older[None], zeta[None], memo[None], grad_bulk, grad_shear)


def solution(mesh):
    return jax.shard_map(
        body,
        mesh=mesh,
        in_specs=(
            P("event", None, "gx", "gy", None),
            P("event", None, "gx", "gy", None),
            P("event", None, "gx", "gy", None),
            P("event", None, None, "gx", "gy", None),
            P("event", None, None, "gx", "gy", None),
            P("gx", "gy", None),
            P("gx", "gy", None),
            P("gx", "gy", None),
            P("gx", "gy", None),
            P("gx", "gy", None),
            P(),
            P(),
            P("event", None),
            P("event", None),
            P("event"),
            P("gx", "gy", None),
            P("gx", "gy"),
        ),
        out_specs=(
            P("event", None, "gx", "gy", None),
            P("event", None, "gx", "gy", None),
            P("event", None, "gx", "gy", None),
            P("event", None, None, "gx", "gy", None),
            P("gx", "gy", None),
            P("gx", "gy", None),
        ),
        check_vma=False,
    )
```

profile of v0, /device:TPU:8, one launch (start us, length us, event | category | flops | bytes accessed | tf_op | source)
XLA Modules:
  0.0 147.0 jit_solution(3246108637304603102)
XLA Ops:
  7.9 3.4 %collective-permute-start.1 = (f32[3,1,8,128]{3,2,1,0:T(8,128)S(1)}, f32[3,1,8,128]{3,2,1,0:T(8,128)S(1)}, u32[]{:S(2)}, u32[]{:S(2)}) collective-permute-start(f32[3,1,8,128]{3,2,1,0:T(8,128)S(1)} %get-tuple-element.30), channel_id=1, source_target_pairs={{0,4},{1,5},{2,6},{3,7},{8,12},{9,13},{10,14},{11,15},{16,20},{17,... | collective-permute-start | bytes 36872 | tf_op jit(solution)/shard_map/ppermute | solution.py:17
  11.3 1.3 collective-permute-start
  14.3 1.4 fusion.103
  18.9 1.1 pad_maximum_fusion.37
  20.1 2.4 %collective-permute-start.2 = (f32[3,18,1,128]{3,2,1,0:T(1,128)S(1)}, f32[3,18,1,128]{3,2,1,0:T(1,128)S(1)}, u32[]{:S(2)}, u32[]{:S(2)}) collective-permute-start(f32[3,18,1,128]{3,2,1,0:T(1,128)S(1)} %get-tuple-element.23), channel_id=1, source_target_pairs={{1,0},{2,1},{3,2},{5,4},{6,5},{7,6},{9,8},{10,9},{11,10},{13,12},{... | collective-permute-start | bytes 82952 | tf_op jit(solution)/shard_map/ppermute | solution.py:20
  22.4 3.5 %collective-permute-start.3 = (f32[3,18,1,128]{3,2,1,0:T(1,128)S(1)}, f32[3,18,1,128]{3,2,1,0:T(1,128)S(1)}, u32[]{:S(2)}, u32[]{:S(2)}) collective-permute-start(f32[3,18,1,128]{3,2,1,0:T(1,128)S(1)} %get-tuple-element.24), channel_id=1, source_target_pairs={{0,1},{1,2},{2,3},{4,5},{5,6},{6,7},{8,9},{9,10},{10,11},{12,13},{... | collective-permute-start | bytes 82952 | tf_op jit(solution)/shard_map/ppermute | solution.py:17
  28.2 1.1 multiply_subtract_fusion.1
  29.3 4.5 %collective-permute-start.5 = (f32[1,8,128]{2,1,0:T(8,128)S(1)}, f32[1,8,128]{2,1,0:T(8,128)S(1)}, u32[]{:S(2)}, u32[]{:S(2)}) collective-permute-start(f32[1,8,128]{2,1,0:T(8,128)S(1)} %get-tuple-element.46), channel_id=1, source_target_pairs={{0,4},{1,5},{2,6},{3,7},{8,12},{9,13},{10,14},{11,15},{16,20},{17,... | collective-permute-start | bytes 12296 | tf_op jit(solution)/shard_map/ppermute | solution.py:17
  33.8 1.3 collective-permute-start.4
  35.8 3.5 %collective-permute-done.4 = f32[1,8,128]{2,1,0:T(8,128)S(1)} collective-permute-done((f32[1,8,128]{2,1,0:T(8,128)S(1)}, f32[1,8,128]{2,1,0:T(8,128)S(1)}, u32[]{:S(2)}, u32[]{:S(2)}) %collective-permute-start.4) | collective-permute-done | bytes 4128 | tf_op jit(solution)/shard_map/ppermute | solution.py:20
  39.3 1.9 %collective-permute-start.6 = (f32[18,1,128]{2,1,0:T(1,128)S(1)}, f32[18,1,128]{2,1,0:T(1,128)S(1)}, u32[]{:S(2)}, u32[]{:S(2)}) collective-permute-start(f32[18,1,128]{2,1,0:T(1,128)S(1)} %get-tuple-element.40), channel_id=1, source_target_pairs={{1,0},{2,1},{3,2},{5,4},{6,5},{7,6},{9,8},{10,9},{11,10},{13,12},{... | collective-permute-start | bytes 27656 | tf_op jit(solution)/shard_map/ppermute | solution.py:20
  41.2 3.9 %collective-permute-start.7 = (f32[18,1,128]{2,1,0:T(1,128)S(1)}, f32[18,1,128]{2,1,0:T(1,128)S(1)}, u32[]{:S(2)}, u32[]{:S(2)}) collective-permute-start(f32[18,1,128]{2,1,0:T(1,128)S(1)} %get-tuple-element.41), channel_id=1, source_target_pairs={{0,1},{1,2},{2,3},{4,5},{5,6},{6,7},{8,9},{9,10},{10,11},{12,13},{... | collective-permute-start | bytes 27656 | tf_op jit(solution)/shard_map/ppermute | solution.py:17
  45.2 1.1 reduce_sum.55
  46.4 10.4 %scatter_custom_fusion = f32[3,16384]{0,1:T(8,128)} fusion(s32[1024]{0:T(1024)S(1)} %bitcast.104, f32[]{:T(128)} %constant.76.clone.1, f32[1024]{0:T(1024)S(1)} %get-tuple-element.17, f32[3]{0:T(128)} %bitcast.106), kind=kCustom, calls=%fused_computation.4 | custom fusion | flops 6144 | bytes 200720 | tf_op jit(solution)/shard_map/scatter-add | solution.py:99
  56.8 5.2 %copy.25 = f32[3,16,8,128]{3,2,1,0:T(8,128)S(1)} copy(f32[3,16,8,128]{0,3,2,1:T(8,128)} %bitcast.95) | data formatting | bytes 393216 | tf_op jit(solution)/shard_map/reshape | solution.py:100
  62.4 1.7 %collective-permute-start.9 = (f32[3,1,8,128]{3,2,1,0:T(8,128)S(1)}, f32[3,1,8,128]{3,2,1,0:T(8,128)S(1)}, u32[]{:S(2)}, u32[]{:S(2)}) collective-permute-start(f32[3,1,8,128]{3,2,1,0:T(8,128)S(1)} %get-tuple-element.28), channel_id=1, source_target_pairs={{0,4},{1,5},{2,6},{3,7},{8,12},{9,13},{10,14},{11,15},{16,20},{17,... | collective-permute-start | bytes 36872 | tf_op jit(solution)/shard_map/ppermute | solution.py:17
  64.1 1.3 collective-permute-start.8
  65.5 10.3 %scatter_custom_fusion.1 = f32[3,16384]{0,1:T(8,128)} fusion(s32[1024]{0:T(1024)S(1)} %bitcast.105, f32[]{:T(128)} %constant.76.clone.1, f32[1024]{0:T(1024)S(1)} %fusion.90, f32[3]{0:T(128)S(1)} %bitcast.107), kind=kCustom, calls=%fused_computation.2 | custom fusion | flops 6144 | bytes 201220 | tf_op jit(solution)/shard_map/scatter-add | solution.py:99
  75.8 5.3 %copy.26 = f32[3,16,8,128]{3,2,1,0:T(8,128)S(1)} copy(f32[3,16,8,128]{0,3,2,1:T(8,128)} %bitcast.94) | data formatting | bytes 393216 | tf_op jit(solution)/shard_map/reshape | solution.py:100
  81.2 1.9 %collective-permute-start.10 = (f32[3,18,1,128]{3,2,1,0:T(1,128)S(1)}, f32[3,18,1,128]{3,2,1,0:T(1,128)S(1)}, u32[]{:S(2)}, u32[]{:S(2)}) collective-permute-start(f32[3,18,1,128]{3,2,1,0:T(1,128)S(1)} %get-tuple-element.21), channel_id=1, source_target_pairs={{1,0},{2,1},{3,2},{5,4},{6,5},{7,6},{9,8},{10,9},{11,10},{13,12},{... | collective-permute-start | bytes 82952 | tf_op jit(solution)/shard_map/ppermute | solution.py:20
  83.1 3.9 %collective-permute-start.11 = (f32[3,18,1,128]{3,2,1,0:T(1,128)S(1)}, f32[3,18,1,128]{3,2,1,0:T(1,128)S(1)}, u32[]{:S(2)}, u32[]{:S(2)}) collective-permute-start(f32[3,18,1,128]{3,2,1,0:T(1,128)S(1)} %get-tuple-element.22), channel_id=1, source_target_pairs={{0,1},{1,2},{2,3},{4,5},{5,6},{6,7},{8,9},{9,10},{10,11},{12,13},{... | collective-permute-start | bytes 82952 | tf_op jit(solution)/shard_map/ppermute | solution.py:17
  87.1 1.8 %collective-permute-done.11 = f32[3,18,1,128]{3,2,1,0:T(1,128)S(1)} collective-permute-done((f32[3,18,1,128]{3,2,1,0:T(1,128)S(1)}, f32[3,18,1,128]{3,2,1,0:T(1,128)S(1)}, u32[]{:S(2)}, u32[]{:S(2)}) %collective-permute-start.11) | collective-permute-done | bytes 27680 | tf_op jit(solution)/shard_map/ppermute | solution.py:17
  89.8 4.5 %collective-permute-start.13 = (f32[1,8,128]{2,1,0:T(8,128)S(1)}, f32[1,8,128]{2,1,0:T(8,128)S(1)}, u32[]{:S(2)}, u32[]{:S(2)}) collective-permute-start(f32[1,8,128]{2,1,0:T(8,128)S(1)} %get-tuple-element.43), channel_id=1, source_target_pairs={{0,4},{1,5},{2,6},{3,7},{8,12},{9,13},{10,14},{11,15},{16,20},{17,... | collective-permute-start | bytes 12296 | tf_op jit(solution)/shard_map/ppermute | solution.py:17
  94.3 1.3 collective-permute-start.12
  97.2 2.6 %collective-permute-done.12 = f32[1,8,128]{2,1,0:T(8,128)S(1)} collective-permute-done((f32[1,8,128]{2,1,0:T(8,128)S(1)}, f32[1,8,128]{2,1,0:T(8,128)S(1)}, u32[]{:S(2)}, u32[]{:S(2)}) %collective-permute-start.12) | collective-permute-done | bytes 4128 | tf_op jit(solution)/shard_map/ppermute | solution.py:20
  99.8 1.9 %collective-permute-start.14 = (f32[18,1,128]{2,1,0:T(1,128)S(1)}, f32[18,1,128]{2,1,0:T(1,128)S(1)}, u32[]{:S(2)}, u32[]{:S(2)}) collective-permute-start(f32[18,1,128]{2,1,0:T(1,128)S(1)} %get-tuple-element.36), channel_id=1, source_target_pairs={{1,0},{2,1},{3,2},{5,4},{6,5},{7,6},{9,8},{10,9},{11,10},{13,12},{... | collective-permute-start | bytes 27656 | tf_op jit(solution)/shard_map/ppermute | solution.py:20
  101.8 3.9 %collective-permute-start.15 = (f32[18,1,128]{2,1,0:T(1,128)S(1)}, f32[18,1,128]{2,1,0:T(1,128)S(1)}, u32[]{:S(2)}, u32[]{:S(2)}) collective-permute-start(f32[18,1,128]{2,1,0:T(1,128)S(1)} %get-tuple-element.37), channel_id=1, source_target_pairs={{0,1},{1,2},{2,3},{4,5},{5,6},{6,7},{8,9},{9,10},{10,11},{12,13},{... | collective-permute-start | bytes 27656 | tf_op jit(solution)/shard_map/ppermute | solution.py:17
  105.9 1.4 collective-permute-done.15
  108.2 1.0 multiply_add_fusion
  109.2 28.0 %all-reduce.9.cloned.1.call-done = (f32[16,8,128]{2,1,0:T(8,128)}, f32[16,8,128]{2,1,0:T(8,128)}) async-done(((f32[16,8,128]{2,1,0:T(8,128)}, f32[16,8,128]{2,1,0:T(8,128)}), (f32[16,8,128]{2,1,0:T(8,128)}, f32[16,8,128]{2,1,0:T(8,128)})) %all-reduce.9.cloned.1.call-update) | async-done | bytes 131088 | tf_op jit(solution)/shard_map/psum | solution.py:123
  137.2 1.5 %copy.31 = f32[16,8,128]{2,1,0:T(8,128)} copy(f32[16,8,128]{2,1,0:T(8,128)} %get-tuple-element.55) | data formatting | bytes 131072
  138.7 1.5 %copy.32 = f32[16,8,128]{2,1,0:T(8,128)} copy(f32[16,8,128]{2,1,0:T(8,128)} %get-tuple-element.56) | data formatting | bytes 131072
  (68 shorter events, 9.4 us)
Async XLA Ops:
  7.2 130.0 %all-reduce.9.cloned.1.call-start = ((), (), s32[]{:S(2)}) async-start(), calls=%async_computation | async-start | bytes 262144 | tf_op jit(solution)/shard_map/psum | solution.py:123
  7.9 11.0 %collective-permute-start.1 = (f32[3,1,8,128]{3,2,1,0:T(8,128)S(1)}, f32[3,1,8,128]{3,2,1,0:T(8,128)S(1)}, u32[]{:S(2)}, u32[]{:S(2)}) collective-permute-start(f32[3,1,8,128]{3,2,1,0:T(8,128)S(1)} %get-tuple-element.30), channel_id=1, source_target_pairs={{0,4},{1,5},{2,6},{3,7},{8,12},{9,13},{10,14},{11,15},{16,20},{17,... | collective-permute-start | bytes 36872 | tf_op jit(solution)/shard_map/ppermute | solution.py:17
  11.3 7.6 %collective-permute-start = (f32[3,1,8,128]{3,2,1,0:T(8,128)S(1)}, f32[3,1,8,128]{3,2,1,0:T(8,128)S(1)}, u32[]{:S(2)}, u32[]{:S(2)}) collective-permute-start(f32[3,1,8,128]{3,2,1,0:T(8,128)S(1)} %get-tuple-element.31), channel_id=1, source_target_pairs={{4,0},{5,1},{6,2},{7,3},{12,8},{13,9},{14,10},{15,11},{20,16},{21,... | collective-permute-start | bytes 36872 | tf_op jit(solution)/shard_map/ppermute | solution.py:20
  20.1 7.5 %collective-permute-start.2 = (f32[3,18,1,128]{3,2,1,0:T(1,128)S(1)}, f32[3,18,1,128]{3,2,1,0:T(1,128)S(1)}, u32[]{:S(2)}, u32[]{:S(2)}) collective-permute-start(f32[3,18,1,128]{3,2,1,0:T(1,128)S(1)} %get-tuple-element.23), channel_id=1, source_target_pairs={{1,0},{2,1},{3,2},{5,4},{6,5},{7,6},{9,8},{10,9},{11,10},{13,12},{... | collective-permute-start | bytes 82952 | tf_op jit(solution)/shard_map/ppermute | solution.py:20
  22.4 5.8 %collective-permute-start.3 = (f32[3,18,1,128]{3,2,1,0:T(1,128)S(1)}, f32[3,18,1,128]{3,2,1,0:T(1,128)S(1)}, u32[]{:S(2)}, u32[]{:S(2)}) collective-permute-start(f32[3,18,1,128]{3,2,1,0:T(1,128)S(1)} %get-tuple-element.24), channel_id=1, source_target_pairs={{0,1},{1,2},{2,3},{4,5},{5,6},{6,7},{8,9},{9,10},{10,11},{12,13},{... | collective-permute-start | bytes 82952 | tf_op jit(solution)/shard_map/ppermute | solution.py:17
  29.3 6.5 %collective-permute-start.5 = (f32[1,8,128]{2,1,0:T(8,128)S(1)}, f32[1,8,128]{2,1,0:T(8,128)S(1)}, u32[]{:S(2)}, u32[]{:S(2)}) collective-permute-start(f32[1,8,128]{2,1,0:T(8,128)S(1)} %get-tuple-element.46), channel_id=1, source_target_pairs={{0,4},{1,5},{2,6},{3,7},{8,12},{9,13},{10,14},{11,15},{16,20},{17,... | collective-permute-start | bytes 12296 | tf_op jit(solution)/shard_map/ppermute | solution.py:17
  33.8 5.5 %collective-permute-start.4 = (f32[1,8,128]{2,1,0:T(8,128)S(1)}, f32[1,8,128]{2,1,0:T(8,128)S(1)}, u32[]{:S(2)}, u32[]{:S(2)}) collective-permute-start(f32[1,8,128]{2,1,0:T(8,128)S(1)} %get-tuple-element.47), channel_id=1, source_target_pairs={{4,0},{5,1},{6,2},{7,3},{12,8},{13,9},{14,10},{15,11},{20,16},{21,... | collective-permute-start | bytes 12296 | tf_op jit(solution)/shard_map/ppermute | solution.py:20
  39.3 22.7 %collective-permute-start.6 = (f32[18,1,128]{2,1,0:T(1,128)S(1)}, f32[18,1,128]{2,1,0:T(1,128)S(1)}, u32[]{:S(2)}, u32[]{:S(2)}) collective-permute-start(f32[18,1,128]{2,1,0:T(1,128)S(1)} %get-tuple-element.40), channel_id=1, source_target_pairs={{1,0},{2,1},{3,2},{5,4},{6,5},{7,6},{9,8},{10,9},{11,10},{13,12},{... | collective-permute-start | bytes 27656 | tf_op jit(solution)/shard_map/ppermute | solution.py:20
  41.2 20.8 %collective-permute-start.7 = (f32[18,1,128]{2,1,0:T(1,128)S(1)}, f32[18,1,128]{2,1,0:T(1,128)S(1)}, u32[]{:S(2)}, u32[]{:S(2)}) collective-permute-start(f32[18,1,128]{2,1,0:T(1,128)S(1)} %get-tuple-element.41), channel_id=1, source_target_pairs={{0,1},{1,2},{2,3},{4,5},{5,6},{6,7},{8,9},{9,10},{10,11},{12,13},{... | collective-permute-start | bytes 27656 | tf_op jit(solution)/shard_map/ppermute | solution.py:17
  46.3 15.9 %copy-start.1 = (f32[1,3,16,8,128]{4,3,2,1,0:T(8,128)S(1)}, f32[1,3,16,8,128]{4,3,2,1,0:T(8,128)}, u32[]{:S(2)}) copy-start(f32[1,3,16,8,128]{4,3,2,1,0:T(8,128)} %param.17) | copy-start | bytes 589828
  46.3 15.9 %copy-start.4 = (f32[16,8,128]{2,1,0:T(8,128)S(1)}, f32[16,8,128]{2,1,0:T(8,128)}, u32[]{:S(2)}) copy-start(f32[16,8,128]{2,1,0:T(8,128)} %param.23) | copy-start | bytes 196612
  46.3 15.9 %copy-start.7 = (f32[1,3,16,8,128]{4,3,2,1,0:T(8,128)S(1)}, f32[1,3,16,8,128]{4,3,2,1,0:T(8,128)}, u32[]{:S(2)}) copy-start(f32[1,3,16,8,128]{4,3,2,1,0:T(8,128)} %param.18) | copy-start | bytes 589828
  46.4 19.0 %copy-start.11 = (f32[3]{0:T(128)S(1)}, f32[3]{0:T(128)}, u32[]{:S(2)}) copy-start(f32[3]{0:T(128)} %param.28) | copy-start | bytes 40
  46.4 19.0 %copy-start.12 = (f32[3]{0:T(128)S(1)}, f32[3]{0:T(128)}, u32[]{:S(2)}) copy-start(f32[3]{0:T(128)} %param.27) | copy-start | bytes 40
  46.4 19.1 %copy-start.8 = (f32[16,8,128]{2,1,0:T(8,128)S(1)}, f32[16,8,128]{2,1,0:T(8,128)}, u32[]{:S(2)}) copy-start(f32[16,8,128]{2,1,0:T(8,128)} %param.26) | copy-start | bytes 196612
  46.4 19.1 %copy-start.10 = (f32[1,3]{1,0:T(1,128)S(1)}, f32[1,3]{1,0:T(1,128)}, u32[]{:S(2)}) copy-start(f32[1,3]{1,0:T(1,128)} %param.30) | copy-start | bytes 40
  62.4 45.0 %copy-start = (f32[3,16,8,128]{3,2,1,0:T(8,128)}, f32[3,16,8,128]{3,2,1,0:T(8,128)S(1)}, u32[]{:S(2)}) copy-start(f32[3,16,8,128]{3,2,1,0:T(8,128)S(1)} %get-tuple-element.13) | copy-start | bytes 589828
  62.4 18.7 %collective-permute-start.9 = (f32[3,1,8,128]{3,2,1,0:T(8,128)S(1)}, f32[3,1,8,128]{3,2,1,0:T(8,128)S(1)}, u32[]{:S(2)}, u32[]{:S(2)}) collective-permute-start(f32[3,1,8,128]{3,2,1,0:T(8,128)S(1)} %get-tuple-element.28), channel_id=1, source_target_pairs={{0,4},{1,5},{2,6},{3,7},{8,12},{9,13},{10,14},{11,15},{16,20},{17,... | collective-permute-start | bytes 36872 | tf_op jit(solution)/shard_map/ppermute | solution.py:17
  64.1 17.0 %collective-permute-start.8 = (f32[3,1,8,128]{3,2,1,0:T(8,128)S(1)}, f32[3,1,8,128]{3,2,1,0:T(8,128)S(1)}, u32[]{:S(2)}, u32[]{:S(2)}) collective-permute-start(f32[3,1,8,128]{3,2,1,0:T(8,128)S(1)} %get-tuple-element.29), channel_id=1, source_target_pairs={{4,0},{5,1},{6,2},{7,3},{12,8},{13,9},{14,10},{15,11},{20,16},{21,... | collective-permute-start | bytes 36872 | tf_op jit(solution)/shard_map/ppermute | solution.py:20
  65.5 23.4 %copy-start.5 = (f32[16,8,128]{2,1,0:T(8,128)S(1)}, f32[16,8,128]{2,1,0:T(8,128)}, u32[]{:S(2)}) copy-start(f32[16,8,128]{2,1,0:T(8,128)} %param.22) | copy-start | bytes 196612
  65.5 23.4 %copy-start.6 = (f32[1,2,4,16,8,128]{5,4,3,2,1,0:T(8,128)S(1)}, f32[1,2,4,16,8,128]{5,4,3,2,1,0:T(8,128)}, u32[]{:S(2)}) copy-start(f32[1,2,4,16,8,128]{5,4,3,2,1,0:T(8,128)} %param.21) | copy-start | bytes 1572868
  65.5 24.1 %copy-start.9 = (f32[16,8,128]{2,1,0:T(8,128)S(1)}, f32[16,8,128]{2,1,0:T(8,128)}, u32[]{:S(2)}) copy-start(f32[16,8,128]{2,1,0:T(8,128)} %param.25) | copy-start | bytes 196612
  65.5 24.1 %copy-start.3 = (f32[1,3,16,8,128]{4,3,2,1,0:T(8,128)S(1)}, f32[1,3,16,8,128]{4,3,2,1,0:T(8,128)}, u32[]{:S(2)}) copy-start(f32[1,3,16,8,128]{4,3,2,1,0:T(8,128)} %param.19) | copy-start | bytes 589828
  75.8 29.9 %copy-start.2 = (f32[1,3,3,16,8,128]{5,4,3,2,1,0:T(8,128)S(1)}, f32[1,3,3,16,8,128]{5,4,3,2,1,0:T(8,128)}, u32[]{:S(2)}) copy-start(f32[1,3,3,16,8,128]{5,4,3,2,1,0:T(8,128)} %param.20) | copy-start | bytes 1769476
  81.2 5.9 %collective-permute-start.10 = (f32[3,18,1,128]{3,2,1,0:T(1,128)S(1)}, f32[3,18,1,128]{3,2,1,0:T(1,128)S(1)}, u32[]{:S(2)}, u32[]{:S(2)}) collective-permute-start(f32[3,18,1,128]{3,2,1,0:T(1,128)S(1)} %get-tuple-element.21), channel_id=1, source_target_pairs={{1,0},{2,1},{3,2},{5,4},{6,5},{7,6},{9,8},{10,9},{11,10},{13,12},{... | collective-permute-start | bytes 82952 | tf_op jit(solution)/shard_map/ppermute | solution.py:20
  83.1 5.8 %collective-permute-start.11 = (f32[3,18,1,128]{3,2,1,0:T(1,128)S(1)}, f32[3,18,1,128]{3,2,1,0:T(1,128)S(1)}, u32[]{:S(2)}, u32[]{:S(2)}) collective-permute-start(f32[3,18,1,128]{3,2,1,0:T(1,128)S(1)} %get-tuple-element.22), channel_id=1, source_target_pairs={{0,1},{1,2},{2,3},{4,5},{5,6},{6,7},{8,9},{9,10},{10,11},{12,13},{... | collective-permute-start | bytes 82952 | tf_op jit(solution)/shard_map/ppermute | solution.py:17
  89.8 7.5 %collective-permute-start.13 = (f32[1,8,128]{2,1,0:T(8,128)S(1)}, f32[1,8,128]{2,1,0:T(8,128)S(1)}, u32[]{:S(2)}, u32[]{:S(2)}) collective-permute-start(f32[1,8,128]{2,1,0:T(8,128)S(1)} %get-tuple-element.43), channel_id=1, source_target_pairs={{0,4},{1,5},{2,6},{3,7},{8,12},{9,13},{10,14},{11,15},{16,20},{17,... | collective-permute-start | bytes 12296 | tf_op jit(solution)/shard_map/ppermute | solution.py:17
  94.3 5.5 %collective-permute-start.12 = (f32[1,8,128]{2,1,0:T(8,128)S(1)}, f32[1,8,128]{2,1,0:T(8,128)S(1)}, u32[]{:S(2)}, u32[]{:S(2)}) collective-permute-start(f32[1,8,128]{2,1,0:T(8,128)S(1)} %get-tuple-element.44), channel_id=1, source_target_pairs={{4,0},{5,1},{6,2},{7,3},{12,8},{13,9},{14,10},{15,11},{20,16},{21,... | collective-permute-start | bytes 12296 | tf_op jit(solution)/shard_map/ppermute | solution.py:20
  99.8 6.0 %collective-permute-start.14 = (f32[18,1,128]{2,1,0:T(1,128)S(1)}, f32[18,1,128]{2,1,0:T(1,128)S(1)}, u32[]{:S(2)}, u32[]{:S(2)}) collective-permute-start(f32[18,1,128]{2,1,0:T(1,128)S(1)} %get-tuple-element.36), channel_id=1, source_target_pairs={{1,0},{2,1},{3,2},{5,4},{6,5},{7,6},{9,8},{10,9},{11,10},{13,12},{... | collective-permute-start | bytes 27656 | tf_op jit(solution)/shard_map/ppermute | solution.py:20
  101.8 5.6 %collective-permute-start.15 = (f32[18,1,128]{2,1,0:T(1,128)S(1)}, f32[18,1,128]{2,1,0:T(1,128)S(1)}, u32[]{:S(2)}, u32[]{:S(2)}) collective-permute-start(f32[18,1,128]{2,1,0:T(1,128)S(1)} %get-tuple-element.37), channel_id=1, source_target_pairs={{0,1},{1,2},{2,3},{4,5},{5,6},{6,7},{8,9},{9,10},{10,11},{12,13},{... | collective-permute-start | bytes 27656 | tf_op jit(solution)/shard_map/ppermute | solution.py:17
Sparse Core Ops, SparseCore 0:
  106.0 31.1 all-reduce.8
where the time goes:
time: 150 us; the launch traced here: 147 us
  starting transfers between devices  42.7 us (28%)
  waiting for transfers between devices  37.9 us (25%)
  other arithmetic  32.1 us (21%)
  between operations  17.8 us (12%)
  local copies, waits for them, and re-layouts  16.5 us (11%)
    ppermute x8, starting transfers between devices, with_halo(): lax.ppermute(lax.slice_in_dim(block, block.shape[dim] - width, None, axis...  29.4 us
    psum x1, waiting for transfers between devices, body(): grad_bulk, grad_shear = lax.psum((grad_bulk, grad_shear), 'event')  28 us
    scatter-add x2, other arithmetic, body(): drive = drive.at[:, flat].add(event_amplitude[0][:, None] * pulse[None, :...  20.7 us
    ppermute x8, starting transfers between devices, with_halo(): lax.ppermute(lax.slice_in_dim(block, 0, width, axis=dim), axis, backward)  13.3 us
    reshape x2, local copies, waits for them, and re-layouts, body(): drive = drive.at[:, flat].add(event_amplitude[0][:, None] * pulse[None, :...  10.5 us
    ppermute x8, waiting for transfers between devices, with_halo(): lax.ppermute(lax.slice_in_dim(block, 0, width, axis=dim), axis, backward)  6.1 us
    ppermute x8, waiting for transfers between devices, with_halo(): lax.ppermute(lax.slice_in_dim(block, block.shape[dim] - width, None, axis...  3.82 us
    unnamed x28, local copies, waits for them, and re-layouts  3.02 us
  transfers between devices with their start and end apart: 17, of which 6 were waited for; matrix products, arithmetic and copies ran while one was open for 28% of the time, Pallas kernels for 0%

commit v1 on v0

v1 whole, which is shorter than its diff:
```python
import functools

import jax
import jax.numpy as jnp
from jax import lax
from jax.experimental import pallas as pl
from jax.experimental.pallas import tpu as pltpu
from jax.sharding import PartitionSpec as P

TIME_STEP = 0.3
DT2 = TIME_STEP * TIME_STEP
TILE = (8, 128)

X_LIST = (
    [("wx", d) for d in (1, 2, 3, 4)]
    + [("wy", d) for d in (1, 2, 3)]
    + [("wz", d) for d in (1, 2, 3)]
    + [("kappa", d) for d in (1, 2, 3)]
    + [("zsum", d) for d in (1, 2, 3)]
    + [(f"base{c}", d) for c in range(3) for d in (1, 2)]
    + [("bb", d) for d in (1, 2)]
    + [("bbmu", d) for d in (1, 2)]
    + [("z1", 1), ("atten", 1)]
)
X_AT = {key: at for at, key in enumerate(X_LIST)}
D_LIST = [(t, 1) for t in range(4)] + [(t, 2) for t in range(3)] + [(0, 3)]


def roll(tile, shift, axis):
    return pltpu.roll(tile, shift % TILE[axis], axis)


def row_of():
    return lax.broadcasted_iota(jnp.int32, TILE, 0)


def lane_of():
    return lax.broadcasted_iota(jnp.int32, TILE, 1)


def zplus(f):
    return jnp.where(lane_of() == TILE[1] - 1, 0.0, roll(f, -1, 1))


def zminus(f):
    return jnp.where(lane_of() == 0, 0.0, roll(f, 1, 1))


def yplus(block, halo):
    b, h = roll(block, -1, 0), roll(halo, -1, 0)
    last = row_of() == TILE[0] - 1
    return jnp.where(last, h, b), jnp.where(last, b, h)


def yminus(block, halo):
    b, h = roll(block, 1, 0), roll(halo, 1, 0)
    first = row_of() == 0
    return jnp.where(first, h, b), jnp.where(first, b, h)


def decay_gain(relax_ref, weight_ref):
    decay, gain = [], []
    for l in range(relax_ref.shape[0]):
        d = jnp.exp(-TIME_STEP / jnp.full(TILE, relax_ref[l], jnp.float32))
        decay.append(d)
        gain.append((1.0 - d) * weight_ref[l])
    return decay, gain


def wave_phase(slow_ref, onset_ref, counts):
    nx, ny, cx = counts
    i, j = lax.axis_index("gx"), lax.axis_index("gy")
    py = (j * TILE[0] + row_of()).astype(jnp.float32) / float(ny * TILE[0])
    pz = lane_of().astype(jnp.float32) / float(TILE[1])
    common = slow_ref[0, 1] * py + slow_ref[0, 2] * pz + onset_ref[0]

    def at(x):
        px = jnp.full(TILE, i * cx + x, jnp.int32).astype(jnp.float32) / float(nx * cx)
        return slow_ref[0, 0] * px + common

    return at


def pulse_of(tau):
    square = tau * tau
    return (1.0 - 2.0 * square) * jnp.exp(-square)


def pack_kernel(
    counts, np_, w_ref, v_ref, bm_ref, sm_ref, kappa_ref, mu_ref, buoy_ref, at_ref, relax_ref, weight_ref,
    slow_ref, amp_ref, onset_ref, cells_ref, count_ref, *outs,
):
    nx, ny, cx = counts
    y_refs = outs[:2]
    x_refs = outs[2 : 2 + np_]
    d_refs = outs[2 + np_ : 2 + 3 * np_]
    mask_ref, base_ref, zsum_ref, z1_ref = outs[2 + 3 * np_ :]
    i, j = lax.axis_index("gx"), lax.axis_index("gy")
    rows = cx * TILE[0]
    slots = cells_ref.shape[2]
    cells = cells_ref[0]
    slot = lax.broadcasted_iota(jnp.int32, (1, slots), 1)
    live = slot < count_ref[0, 0]
    row_id = jnp.where(live, cells >> 7, -1)
    lane_id = cells & (TILE[1] - 1)
    wide = lax.broadcasted_iota(jnp.int32, (rows, slots), 0)
    hot_row = jnp.where(wide == row_id, 1.0, 0.0).astype(jnp.bfloat16)
    deep = lax.broadcasted_iota(jnp.int32, (TILE[1], slots), 0)
    hot_lane = jnp.where(deep == lane_id, 1.0, 0.0).astype(jnp.bfloat16)
    mask = lax.dot_general(
        hot_row, hot_lane, (((1,), (1,)), ((), ())), preferred_element_type=jnp.float32
    )
    mask_ref[...] = mask.reshape(cx, TILE[0], TILE[1])

    decay, _ = decay_gain(relax_ref, weight_ref)
    phase = wave_phase(slow_ref, onset_ref, counts)
    row = row_of()
    keep = ((row >> 2) ^ (j & 1)) == 1
    two_three = (row == 2) | (row == 3)
    four_five = (row == 4) | (row == 5)

    def pair(first, second):
        return jnp.where(
            two_three, roll(second, 2, 0), jnp.where(four_five, roll(second, -2, 0), first)
        )

    for x in range(cx):
        w = [w_ref[0, c, x] for c in range(3)]
        kappa, mu, atten = kappa_ref[x], mu_ref[x], at_ref[x]
        bb = DT2 * buoy_ref[x]
        bbmu = bb * mu
        pulse = pulse_of(-phase(x)) * mask_ref[x]
        base = []
        for c in range(3):
            total = sm_ref[0, 0, c, x] + sm_ref[0, 1, c, x] + sm_ref[0, 2, c, x]
            value = 2.0 * w[c] - v_ref[0, c, x] + bb * (amp_ref[0, c] * pulse - total)
            base_ref[c, x] = value
            base.append(value)
        bm = [bm_ref[0, l, x] for l in range(3)]
        zsum = bm[0] + bm[1] + bm[2]
        z1 = decay[0] * bm[0] + decay[1] * bm[1] + decay[2] * bm[2]
        zsum_ref[x] = zsum
        z1_ref[x] = z1
        third = jnp.where(
            row == 2,
            roll(z1, 2, 0),
            jnp.where(
                row == 3,
                roll(atten, 3, 0),
                jnp.where(row == 4, roll(atten, -3, 0), jnp.where(row == 5, roll(z1, -2, 0), bbmu)),
            ),
        )
        tiles = [
            (w[0], w[1]),
            (w[2], kappa),
            (zsum, third),
            (pair(base[0], base[1]), pair(base[2], bb)),
        ]
        for t, (a, b) in enumerate(tiles):
            b = roll(b, 4, 0)
            y_refs[0][t, x] = jnp.where(keep, a, b)
            y_refs[1][t, x] = jnp.where(keep, b, a)

    for p in range(np_):
        for (name, d), at in X_AT.items():
            x = jnp.where(((i ^ p) & 1) == 0, cx - d, d - 1)
            if name[0] == "w":
                value = w_ref[0, "xyz".index(name[1]), x]
            elif name == "kappa":
                value = kappa_ref[x]
            elif name == "zsum":
                value = zsum_ref[x]
            elif name == "z1":
                value = z1_ref[x]
            elif name == "atten":
                value = at_ref[x]
            elif name == "bb":
                value = DT2 * buoy_ref[x]
            elif name == "bbmu":
                value = DT2 * buoy_ref[x] * mu_ref[x]
            else:
                value = base_ref[int(name[4]), x]
            x_refs[p][at] = value
        for q in range(2):
            for at, (t, d) in enumerate(D_LIST):
                x = jnp.where(((i ^ p) & 1) == 0, cx - d, d - 1)
                d_refs[2 * p + q][at] = y_refs[q][t, x]


def first_kernel(
    counts, np_, w_ref, kappa_ref, mu_ref, buoy_ref, at_ref, strain_ref, relax_ref, weight_ref, base_ref, zsum_ref,
    z1_ref, *rest,
):
    nx, ny, cx = counts
    y_refs = rest[:2]
    x_refs = rest[2 : 2 + np_]
    d_refs = rest[2 + np_ : 2 + 3 * np_]
    (term_ref, w1_ref, d0_ref, l0_ref, d1_ref, l1_ref, pb_ref, ph_ref) = rest[2 + 3 * np_ : 10 + 3 * np_]
    (side_ref, halo_ref, p0b, p0h, d0b, d0h, w1b, w1h) = rest[10 + 3 * np_ :]
    i, j = lax.axis_index("gx"), lax.axis_index("gy")
    row = row_of()

    n = len(X_LIST)
    low_there, high_there = i > 0, i < nx - 1
    even = (i & 1) == 0

    def from_sides(pick):
        if np_ == 1:
            value = pick(0)
            return value, value
        first, second = pick(0), pick(1)
        return jnp.where(even, second, first), jnp.where(even, first, second)

    for at in range(n):
        low, high = from_sides(lambda p: x_refs[p][at])
        side_ref[at] = jnp.where(low_there, low, 0.0)
        side_ref[n + at] = jnp.where(high_there, high, 0.0)

    there = jnp.where(row < 4, (j < ny - 1).astype(jnp.int32), (j > 0).astype(jnp.int32))
    mine = (row >> 2) ^ (j & 1)
    pick0, pick1 = jnp.where(mine == 0, there, 0), jnp.where(mine == 1, there, 0)
    swap0, swap1 = roll(pick0, 4, 0), roll(pick1, 4, 0)

    def unpack(t, x, r0, r1, ok):
        if ok is not None:
            r0, r1 = jnp.where(ok, r0, 0.0), jnp.where(ok, r1, 0.0)
        a = jnp.where(pick0 == 1, r0, jnp.where(pick1 == 1, r1, 0.0))
        b = roll(jnp.where(swap0 == 1, r0, jnp.where(swap1 == 1, r1, 0.0)), 4, 0)

        def second(f, near, far):
            return jnp.where(row < 4, roll(f, -near, 0), roll(f, far, 0))

        if t == 0:
            put(("wx", x), a)
            put(("wy", x), b)
        elif t == 1:
            put(("wz", x), a)
            put(("kappa", x), b)
        elif t == 2:
            put(("zsum", x), a)
            if -2 < x < cx + 1:
                put(("bbmu", x), b)
            if 0 <= x < cx:
                put(("z1", x), second(b, 2, 2))
                put(("atten", x), second(b, 3, 3))
        else:
            put(("base0", x), a)
            put(("base1", x), second(a, 2, 2))
            put(("base2", x), b)
            put(("bb", x), second(b, 2, 2))

    names = ["wx", "wy", "wz", "kappa", "zsum", "bbmu", "z1", "atten", "base0", "base1", "base2", "bb"]

    def put(key, value):
        halo_ref[names.index(key[0]), 3 + key[1]] = value

    def halo(name, x):
        return halo_ref[names.index(name), 3 + x]

    for x in range(cx):
        for t in range(4):
            unpack(t, x, y_refs[0][t, x], y_refs[1][t, x], None)
    for at, (t, d) in enumerate(D_LIST):
        low0, high0 = from_sides(lambda p: d_refs[2 * p][at])
        low1, high1 = from_sides(lambda p: d_refs[2 * p + 1][at])
        unpack(t, -d, low0, low1, low_there)
        unpack(t, cx - 1 + d, high0, high1, high_there)

    def block(name, x):
        if x < 0:
            return side_ref[X_AT[(name, -x)]]
        if x >= cx:
            return side_ref[n + X_AT[(name, x - cx + 1)]]
        if name[0] == "w":
            return w_ref[0, "xyz".index(name[1]), x]
        if name == "kappa":
            return kappa_ref[x]
        if name == "zsum":
            return zsum_ref[x]
        if name == "z1":
            return z1_ref[x]
        if name == "atten":
            return at_ref[x]
        if name == "bb":
            return DT2 * buoy_ref[x]
        if name == "bbmu":
            return DT2 * buoy_ref[x] * mu_ref[x]
        return base_ref[int(name[4]), x]

    def divergence(get_b, get_h, x, with_halo):
        yb, yh = get_b(1, x), get_h(1, x)
        up, down = yplus(yb, yh), yminus(yb, yh)
        z = get_b(2, x)
        db = 0.5 * (get_b(0, x + 1) - get_b(0, x - 1) + (up[0] - down[0]) + (zplus(z) - zminus(z)))
        if not with_halo:
            return db, None
        z = get_h(2, x)
        dh = 0.5 * (get_h(0, x + 1) - get_h(0, x - 1) + (up[1] - down[1]) + (zplus(z) - zminus(z)))
        return db, dh

    def w_b(c, x):
        return block("w" + "xyz"[c], x)

    def w_h(c, x):
        return halo("w" + "xyz"[c], x)

    for x in range(-3, cx + 3):
        inner = -3 < x < cx + 2
        db, dh = divergence(w_b, w_h, x, inner)
        p0b[3 + x] = block("kappa", x) * db - block("zsum", x)
        if -2 < x < cx + 1:
            d0b[1 + x] = db
        if inner:
            p0h[2 + x] = halo("kappa", x) * dh - halo("zsum", x)
            if 0 <= x < cx:
                d0h[x] = dh
                d0_ref[x] = db

    def lap(get_b, get_h, c, x, with_halo):
        b, h = get_b(c, x), get_h(c, x)
        up, down = yplus(b, h), yminus(b, h)
        lb = get_b(c, x + 1) + get_b(c, x - 1) + (up[0] + down[0]) + (zplus(b) + zminus(b)) - 6.0 * b
        if not with_halo:
            return lb, None
        lh = get_h(c, x + 1) + get_h(c, x - 1) + (up[1] + down[1]) + (zplus(h) + zminus(h)) - 6.0 * h
        return lb, lh

    for x in range(-2, cx + 2):
        near = -2 < x < cx + 1
        inside = 0 <= x < cx
        bb, bbmu = block("bb", x), block("bbmu", x)
        if near:
            pb, ph = p0b[3 + x], p0h[2 + x]
            up, down = yplus(pb, ph), yminus(pb, ph)
            grad_b = [0.5 * (p0b[4 + x] - p0b[2 + x]), 0.5 * (up[0] - down[0]), 0.5 * (zplus(pb) - zminus(pb))]
            grad_h = [0.5 * (p0h[3 + x] - p0h[1 + x]), 0.5 * (up[1] - down[1]), 0.5 * (zplus(ph) - zminus(ph))]
            hbb, hbbmu = halo("bb", x), halo("bbmu", x)
        else:
            grad_b = [0.5 * (p0b[4 + x] - p0b[2 + x])]
        for c in range(3 if near else 1):
            with_halo = inside or (near and c < 2)
            lb, lh = lap(w_b, w_h, c, x, with_halo)
            value = block(f"base{c}", x) + bb * grad_b[c] + bbmu * lb
            w1b[c, 2 + x] = value
            if inside:
                l0_ref[c, x] = lb
                w1_ref[0, c, x] = value
            if with_halo:
                w1h[c, 1 + x] = halo(f"base{c}", x) + hbb * grad_h[c] + hbbmu * lh

    def w1_b(c, x):
        return w1b[c, 2 + x]

    def w1_h(c, x):
        return w1h[c, 1 + x]

    _, gain = decay_gain(relax_ref, weight_ref)
    gains = gain[0] + gain[1] + gain[2]
    for x in range(-1, cx + 1):
        inside = 0 <= x < cx
        db, dh = divergence(w1_b, w1_h, x, inside)
        kappa = block("kappa", x)
        stress = kappa * db
        pb_ref[1 + x] = stress - (block("z1", x) + gains * (block("atten", x) * kappa * d0b[1 + x]))
        if not inside:
            continue
        hk = halo("kappa", x)
        ph_ref[x] = hk * dh - (halo("z1", x) + gains * (halo("atten", x) * hk * d0h[x]))
        d1_ref[x] = db
        term_ref[0, x] = kappa * d0b[1 + x] * strain_ref[0, 0, 0, x] + stress * strain_ref[0, 1, 0, x]
        total0, total1 = None, None
        for c in range(3):
            lb, _ = lap(w1_b, w1_h, c, x, False)
            l1_ref[c, x] = lb
            part0 = l0_ref[c, x] * strain_ref[0, 0, 1 + c, x]
            part1 = lb * strain_ref[0, 1, 1 + c, x]
            total0 = part0 if total0 is None else total0 + part0
            total1 = part1 if total1 is None else total1 + part1
        mu = mu_ref[x]
        term_ref[1, x] = mu * total0 + mu * total1


def last_kernel(
    counts, w_ref, bm_ref, sm_ref, kappa_ref, mu_ref, buoy_ref, bat_ref, sat_ref, relax_ref, weight_ref, slow_ref,
    amp_ref, onset_ref, mask_ref, w1_ref, d0_ref, l0_ref, d1_ref, l1_ref, pb_ref, ph_ref, w2_ref, bn_ref, sn_ref,
):
    nx, ny, cx = counts
    decay, gain = decay_gain(relax_ref, weight_ref)
    phase = wave_phase(slow_ref, onset_ref, counts)
    for x in range(cx):
        bulk = bat_ref[x] * kappa_ref[x]
        q0, q1 = bulk * d0_ref[x], bulk * d1_ref[x]
        for l in range(3):
            now = decay[l] * bm_ref[0, l, x] + gain[l] * q0
            bn_ref[0, l, x] = decay[l] * now + gain[l] * q1
        pb = pb_ref[1 + x]
        ph = ph_ref[x]
        up, down = yplus(pb, ph), yminus(pb, ph)
        grad = [
            0.5 * (pb_ref[2 + x] - pb_ref[x]),
            0.5 * (up[0] - down[0]),
            0.5 * (zplus(pb) - zminus(pb)),
        ]
        mu = mu_ref[x]
        shear = sat_ref[x] * mu
        pulse = pulse_of(TIME_STEP - phase(x)) * mask_ref[x]
        bb = DT2 * buoy_ref[x]
        for c in range(3):
            l1 = l1_ref[c, x]
            q0, q1 = shear * l0_ref[c, x], shear * l1
            total = None
            for l in range(3):
                now = decay[l] * sm_ref[0, l, c, x] + gain[l] * q0
                sn_ref[0, l, c, x] = decay[l] * now + gain[l] * q1
                total = now if total is None else total + now
            force = grad[c] + mu * l1 - total + amp_ref[0, c] * pulse
            w2_ref[0, c, x] = 2.0 * w1_ref[0, c, x] - w_ref[0, c, x] + bb * force


def matched(value, mesh_shape, along_x, along_y, p, q):
    nx, ny = mesh_shape
    pairs = []
    for a in range(nx):
        for b in range(ny):
            c, d = a, b
            if along_x:
                c = a + 1 if a % 2 == p else a - 1
            if along_y:
                d = b + 1 if b % 2 == q else b - 1
            if not (0 <= c < nx and 0 <= d < ny):
                c, d = a, b
            pairs.append((a * ny + b, c * ny + d))
    return lax.ppermute(value, ("gx", "gy"), pairs)


def event_sum(value):
    count = lax.axis_size("event")
    if count & (count - 1):
        return lax.psum(value, "event")
    step = 1
    while step < count:
        value = value + lax.ppermute(value, "event", [(e, e ^ step) for e in range(count)])
        step *= 2
    return value


def vmem():
    return pl.BlockSpec(memory_space=pltpu.VMEM)


def smem():
    return pl.BlockSpec(memory_space=pltpu.SMEM)


def body(
    adjoint_now, adjoint_old, bulk_memory, shear_memory, forward_strain, bulk_modulus, shear_modulus, buoyancy,
    bulk_atten, shear_atten, relax_time, mechanism_weight, event_slowness, event_amplitude, event_onset,
    boundary_cells, boundary_count,
):
    nx, ny = lax.axis_size("gx"), lax.axis_size("gy")
    cx = bulk_modulus.shape[0]
    counts = (nx, ny, cx)
    np_ = 1 if nx == 2 else 2
    f32 = jnp.float32

    def field(*lead):
        return jax.ShapeDtypeStruct((*lead, *TILE), f32)

    params = pltpu.CompilerParams(vmem_limit_bytes=24 * 1024 * 1024)
    packed = pl.pallas_call(
        functools.partial(pack_kernel, counts, np_),
        out_shape=[field(4, cx)] * 2
        + [field(len(X_LIST))] * np_
        + [field(len(D_LIST))] * (2 * np_)
        + [field(cx), field(3, cx), field(cx), field(cx)],
        in_specs=[vmem()] * 8 + [smem()] * 5 + [vmem(), smem()],
        out_specs=[vmem()] * (2 + 3 * np_ + 4),
        compiler_params=params,
        name="pack",
    )(
        adjoint_now, adjoint_old, bulk_memory, shear_memory, bulk_modulus, shear_modulus, buoyancy, bulk_atten,
        relax_time, mechanism_weight, event_slowness, event_amplitude, event_onset, boundary_cells, boundary_count,
    )
    shape = (nx, ny)
    ys = [matched(packed[q], shape, False, True, 0, q) for q in range(2)]
    xs = [matched(packed[2 + p], shape, True, False, p, 0) for p in range(np_)]
    ds = [
        matched(packed[2 + np_ + 2 * p + q], shape, True, True, p, q) for p in range(np_) for q in range(2)
    ]
    mask, base, zsum, z1 = packed[2 + 3 * np_ :]

    first = pl.pallas_call(
        functools.partial(first_kernel, counts, np_),
        out_shape=[
            field(2, cx), field(1, 3, cx), field(cx), field(3, cx), field(cx), field(3, cx), field(cx + 2), field(cx),
        ],
        in_specs=[vmem()] * 6 + [smem()] * 2 + [vmem()] * (3 + 2 + 3 * np_),
        out_specs=[vmem()] * 8,
        scratch_shapes=[
            pltpu.VMEM((2 * len(X_LIST), *TILE), f32),
            pltpu.VMEM((12, cx + 6, *TILE), f32),
            pltpu.VMEM((cx + 6, *TILE), f32),
            pltpu.VMEM((cx + 4, *TILE), f32),
            pltpu.VMEM((cx + 2, *TILE), f32),
            pltpu.VMEM((cx, *TILE), f32),
            pltpu.VMEM((3, cx + 4, *TILE), f32),
            pltpu.VMEM((3, cx + 2, *TILE), f32),
        ],
        compiler_params=params,
        name="first",
    )(
        adjoint_now, bulk_modulus, shear_modulus, buoyancy, bulk_atten, forward_strain, relax_time, mechanism_weight,
        base, zsum, z1, *ys, *xs, *ds,
    )
    term, w1, d0, l0, d1, l1, pb, ph = first
    total = event_sum(term)

    w2, bulk_next, shear_next = pl.pallas_call(
        functools.partial(last_kernel, counts),
        out_shape=[field(1, 3, cx), field(1, 3, cx), field(1, 3, 3, cx)],
        in_specs=[vmem()] * 8 + [smem()] * 5 + [vmem()] * 8,
        out_specs=[vmem()] * 3,
        compiler_params=params,
        cost_estimate=pl.CostEstimate(flops=3_000_000, bytes_accessed=4_000_000, transcendentals=0),
        name="last",
    )(
        adjoint_now, bulk_memory, shear_memory, bulk_modulus, shear_modulus, buoyancy, bulk_atten, shear_atten,
        relax_time, mechanism_weight, event_slowness, event_amplitude, event_onset, mask, w1, d0, l0, d1, l1, pb, ph,
    )
    return w2, w1, bulk_next, shear_next, total[0], total[1]


def solution(mesh):
    wide = P("event", None, "gx", "gy", None)
    wider = P("event", None, None, "gx", "gy", None)
    grid = P("gx", "gy", None)
    return jax.shard_map(
        body,
        mesh=mesh,
        in_specs=(
            wide, wide, wide, wider, wider, grid, grid, grid, grid, grid, P(), P(), P("event", None),
            P("event", None), P("event"), grid, P("gx", "gy"),
        ),
        out_specs=(wide, wide, wide, wider, grid, grid),
        check_vma=False,
    )
```

time: 150 us -> 34.4 us (0.23); the launches traced: 147 us -> 33.9 us
  starting transfers between devices: 42.7 us -> 10.3 us
  other arithmetic: 32.1 us -> 0.03 us
  waiting for transfers between devices: 37.9 us -> 8.24 us
  between operations: 17.8 us -> 2.16 us
  local copies, waits for them, and re-layouts: 16.5 us -> 8.59 us
  Pallas kernels: 0 us -> 4.66 us
    ppermute x16 -> x7, starting transfers between devices: 42.7 us -> 10.3 us  [the longest x5 8.67 us: matched(): return lax.ppermute(value, ('gx', 'gy'), pairs)]
    psum x1 -> x0, waiting for transfers between devices: 28 us -> none  [body(): grad_bulk, grad_shear = lax.psum((grad_bulk, grad_shear), 'event')]
    scatter-add x2 -> x0, other arithmetic: 20.7 us -> none  [body(): drive = drive.at[:, flat].add(event_amplitude[0][:, None] * pulse[None, :...]
    reshape x2 -> x0, local copies, waits for them, and re-layouts: 10.5 us -> none  [body(): drive = drive.at[:, flat].add(event_amplitude[0][:, None] * pulse[None, :...]
    unnamed x28 -> x44, local copies, waits for them, and re-layouts: 3.02 us -> 7.94 us
    pallas_call x0 -> x3, Pallas kernels: none -> 4.66 us  [the longest x1 1.89 us: body(): pl.pallas_call(functools.partial(first_kernel, counts, np_), out_shape=[f...]
    add x5 -> x2, other arithmetic: 3.37 us -> 0.03 us  [event_sum(): value + lax.ppermute(value, 'event', [(e, e ^ step) for e in range(count)])]
    reduce_sum x5 -> x0, other arithmetic: 2.49 us -> none  [the longest x2 1.26 us: body(): force = push + shear_modulus * lapl - jnp.sum(memo, 0) + drive]
  transfers between devices with their start and end apart: 17 -> 7, of which waited for: 6 -> 4; matrix products, arithmetic and copies ran while one was open for 28% -> 0% of each run, Pallas kernels for 0% -> 5%
where the time goes in v1:
time: 34.4 us; the launch traced here: 33.9 us
  starting transfers between devices  10.3 us (30%)
  local copies, waits for them, and re-layouts  8.59 us (25%)
  waiting for transfers between devices  8.24 us (24%)
  Pallas kernels  4.66 us (14%)
  between operations  2.16 us (6%)
    ppermute x5, starting transfers between devices, matched(): return lax.ppermute(value, ('gx', 'gy'), pairs)  8.67 us
    unnamed x44, local copies, waits for them, and re-layouts  7.94 us
    ppermute x5, waiting for transfers between devices, matched(): return lax.ppermute(value, ('gx', 'gy'), pairs)  4.68 us
    ppermute x2, waiting for transfers between devices, event_sum(): lax.ppermute(value, 'event', [(e, e ^ step) for e in range(count)])  3.55 us
    pallas_call x1, Pallas kernels, body(): pl.pallas_call(functools.partial(first_kernel, counts, np_), out_shape=[f...  1.89 us
    pallas_call x1, Pallas kernels, body(): pl.pallas_call(functools.partial(last_kernel, counts), out_shape=[field(1...  1.81 us
    ppermute x2, starting transfers between devices, event_sum(): lax.ppermute(value, 'event', [(e, e ^ step) for e in range(count)])  1.59 us
    pallas_call x1, Pallas kernels, body(): pl.pallas_call(functools.partial(pack_kernel, counts, np_), out_shape=[fi...  0.97 us
  transfers between devices with their start and end apart: 7, of which 4 were waited for; matrix products, arithmetic and copies ran while one was open for 0% of the time, Pallas kernels for 5%

profile of v1, /device:TPU:8, one launch (start us, length us, event | category | flops | bytes accessed | tf_op | source)
XLA Modules:
  0.0 33.9 jit_solution(15366492359633513180)
XLA Ops:
  0.6 0.0 copy-start.21
  1.3 0.0 copy-start.17
  2.0 0.0 copy-start
  2.1 1.1 %copy-done = f32[1,3,3,16,8,128]{5,4,3,2,1,0:T(8,128)S(1)} copy-done((f32[1,3,3,16,8,128]{5,4,3,2,1,0:T(8,128)S(1)}, f32[1,3,3,16,8,128]{5,4,3,2,1,0:T(8,128)}, u32[]{:S(2)}) %copy-start) | copy-done | bytes 589848
  3.1 0.9 %copy-done.2 = f32[1,3,16,8,128]{4,3,2,1,0:T(8,128)S(1)} copy-done((f32[1,3,16,8,128]{4,3,2,1,0:T(8,128)S(1)}, f32[1,3,16,8,128]{4,3,2,1,0:T(8,128)}, u32[]{:S(2)}) %copy-start.2) | copy-done | bytes 196632
  4.0 0.9 %copy-done.3 = f32[1,3,16,8,128]{4,3,2,1,0:T(8,128)S(1)} copy-done((f32[1,3,16,8,128]{4,3,2,1,0:T(8,128)S(1)}, f32[1,3,16,8,128]{4,3,2,1,0:T(8,128)}, u32[]{:S(2)}) %copy-start.3) | copy-done | bytes 196632
  5.0 0.8 %copy-done.5 = f32[16,8,128]{2,1,0:T(8,128)S(1)} copy-done((f32[16,8,128]{2,1,0:T(8,128)S(1)}, f32[16,8,128]{2,1,0:T(8,128)}, u32[]{:S(2)}) %copy-start.5) | copy-done | bytes 65560
  5.8 0.8 %copy-done.7 = f32[16,8,128]{2,1,0:T(8,128)S(1)} copy-done((f32[16,8,128]{2,1,0:T(8,128)S(1)}, f32[16,8,128]{2,1,0:T(8,128)}, u32[]{:S(2)}) %copy-start.7) | copy-done | bytes 65560
  6.7 0.8 %copy-done.9 = f32[16,8,128]{2,1,0:T(8,128)S(1)} copy-done((f32[16,8,128]{2,1,0:T(8,128)S(1)}, f32[16,8,128]{2,1,0:T(8,128)}, u32[]{:S(2)}) %copy-start.9) | copy-done | bytes 65560
  7.5 0.8 %copy-done.11 = f32[16,8,128]{2,1,0:T(8,128)S(1)} copy-done((f32[16,8,128]{2,1,0:T(8,128)S(1)}, f32[16,8,128]{2,1,0:T(8,128)}, u32[]{:S(2)}) %copy-start.11) | copy-done | bytes 65560
  8.3 0.9 %copy-done.14 = f32[1,3,16,8,128]{4,3,2,1,0:T(8,128)S(1)} copy-done((f32[1,3,16,8,128]{4,3,2,1,0:T(8,128)S(1)}, f32[1,3,16,8,128]{4,3,2,1,0:T(8,128)}, u32[]{:S(2)}) %copy-start.14) | copy-done | bytes 196632
  9.3 0.7 %copy-done.19 = s32[1,1,1024]{2,1,0:T(1,128)S(1)} copy-done((s32[1,1,1024]{2,1,0:T(1,128)S(1)}, s32[1,1,1024]{2,1,0:T(1,128)}, u32[]{:S(2)}) %copy-start.19) | copy-done | bytes 4120
  10.0 1.0 %pack.1 = (f32[4,16,8,128]{3,2,1,0:T(8,128)S(1)}, f32[4,16,8,128]{3,2,1,0:T(8,128)S(1)}, f32[28,8,128]{2,1,0:T(8,128)S(1)}, f32[8,8,128]{2,1,0:T(8,128)S(1)}, f3...) custom-call(f32[1,3,16,8,128]{4,3,2,1,0:T(8,128)S(1)} %copy-done.2, ...), custom_call_target="tpu_custom_call" | custom-call | tf_op jit(solution)/shard_map/pack/pallas_call | solution.py:470
  10.9 0.1 collective-permute-start
  11.0 5.0 %collective-permute-start.1 = (f32[4,16,8,128]{3,2,1,0:T(8,128)S(1)}, f32[4,16,8,128]{3,2,1,0:T(8,128)S(1)}, u32[]{:S(2)}, u32[]{:S(2)}) collective-permute-start(f32[4,16,8,128]{3,2,1,0:T(8,128)S(1)} %get-tuple-element.31), channel_id=1, source_target_pairs={{0,0},{1,2},{2,1},{3,3},{4,4},{5,6},{6,5},{7,7},{8,8},{9,10},{10,9... | collective-permute-start | bytes 786440 | tf_op jit(solution)/shard_map/ppermute | solution.py:433
  16.1 1.5 %collective-permute-start.2 = (f32[28,8,128]{2,1,0:T(8,128)S(1)}, f32[28,8,128]{2,1,0:T(8,128)S(1)}, u32[]{:S(2)}, u32[]{:S(2)}) collective-permute-start(f32[28,8,128]{2,1,0:T(8,128)S(1)} %get-tuple-element.32), channel_id=1, source_target_pairs={{0,4},{1,5},{2,6},{3,7},{4,0},{5,1},{6,2},{7,3},{8,12},{9,13},{10,... | collective-permute-start | bytes 344072 | tf_op jit(solution)/shard_map/ppermute | solution.py:433
  17.6 0.0 collective-permute-start.3
  17.6 2.0 %collective-permute-start.4 = (f32[8,8,128]{2,1,0:T(8,128)S(1)}, f32[8,8,128]{2,1,0:T(8,128)S(1)}, u32[]{:S(2)}, u32[]{:S(2)}) collective-permute-start(f32[8,8,128]{2,1,0:T(8,128)S(1)} %get-tuple-element.34), channel_id=1, source_target_pairs={{0,0},{1,6},{2,5},{3,3},{4,4},{5,2},{6,1},{7,7},{8,8},{9,14},{10,1... | collective-permute-start | bytes 98312 | tf_op jit(solution)/shard_map/ppermute | solution.py:433
  19.6 3.0 %collective-permute-done.3.rest_3_ = f32[8,8,128]{2,1,0:T(8,128)S(1)} collective-permute-done((f32[8,8,128]{2,1,0:T(8,128)S(1)}, f32[8,8,128]{2,1,0:T(8,128)S(1)}, u32[]{:S(2)}, u32[]{:S(2)}) %collective-permute-start.3) | collective-permute-done | bytes 32800 | tf_op jit(solution)/shard_map/ppermute | solution.py:433
  22.6 1.7 %collective-permute-done.4.rest_4_ = f32[8,8,128]{2,1,0:T(8,128)S(1)} collective-permute-done((f32[8,8,128]{2,1,0:T(8,128)S(1)}, f32[8,8,128]{2,1,0:T(8,128)S(1)}, u32[]{:S(2)}, u32[]{:S(2)}) %collective-permute-start.4) | collective-permute-done | bytes 32800 | tf_op jit(solution)/shard_map/ppermute | solution.py:433
  24.3 0.0 collective-permute-done.2.rest_2_
  24.3 0.0 collective-permute-done.rest_0_
  24.3 0.0 collective-permute-done.1.rest_1_
  24.4 0.0 copy-start.1
  24.4 0.0 copy-start.16
  24.4 1.9 %first.1 = (f32[2,16,8,128]{3,2,1,0:T(8,128)S(1)}, f32[1,3,16,8,128]{4,3,2,1,0:T(8,128)}, f32[16,8,128]{2,1,0:T(8,128)S(1)}, f32[3,16,8,128]{3,2,1,0:T(8,128)S(1...) custom-call(f32[1,3,16,8,128]{4,3,2,1,0:T(8,128)S(1)} %copy-done.2, ...), custom_call_target="tpu_custom_call" | custom-call | tf_op jit(solution)/shard_map/first/pallas_call | solution.py:492
  26.3 0.0 collective-permute-start.5
  26.3 1.3 %collective-permute-done.5 = f32[2,16,8,128]{3,2,1,0:T(8,128)S(1)} collective-permute-done((f32[2,16,8,128]{3,2,1,0:T(8,128)S(1)}, f32[2,16,8,128]{3,2,1,0:T(8,128)S(1)}, u32[]{:S(2)}, u32[]{:S(2)}) %collective-permute-start.5) | collective-permute-done | bytes 131104 | tf_op jit(solution)/shard_map/ppermute | solution.py:442
  27.6 1.6 %collective-permute-start.6 = (f32[2,16,8,128]{3,2,1,0:T(8,128)S(1)}, f32[2,16,8,128]{3,2,1,0:T(8,128)S(1)}, u32[]{:S(2)}, u32[]{:S(2)}) collective-permute-start(f32[2,16,8,128]{3,2,1,0:T(8,128)S(1)} %add.6), channel_id=1, source_target_pairs={{0,16},{8,24},{16,0},{24,8},{1,17},{9,25},{17,1},{25,9},{2,18},{10... | collective-permute-start | bytes 393224 | tf_op jit(solution)/shard_map/ppermute | solution.py:442
  29.2 1.8 %last.1 = (f32[1,3,16,8,128]{4,3,2,1,0:T(8,128)}, f32[1,3,16,8,128]{4,3,2,1,0:T(8,128)}, f32[1,3,3,16,8,128]{5,4,3,2,1,0:T(8,128)}) custom-call(f32[1,3,16,8,128]{4,3,2,1,0:T(8,128)S(1)} %copy-done.2, f32[1,3,16,8,128]{4,3,2,1,0:T(8,128)S(1)} %copy-done.4, f32[1,3,3,16,8,128]{5,4,3,2,1,0:T(8,128)S(1)} %copy-done.1, f32[16,8,128]{2,1,0:T(8,128)S(1)} %copy-done.6, ...), custom_call_target="tpu_custom_call" | custom-call | flops 3000000 | bytes 4000000 | tf_op jit(solution)/shard_map/last/pallas_call | solution.py:518
  31.1 2.2 %collective-permute-done.6 = f32[2,16,8,128]{3,2,1,0:T(8,128)S(1)} collective-permute-done((f32[2,16,8,128]{3,2,1,0:T(8,128)S(1)}, f32[2,16,8,128]{3,2,1,0:T(8,128)S(1)}, u32[]{:S(2)}, u32[]{:S(2)}) %collective-permute-start.6) | collective-permute-done | bytes 131104 | tf_op jit(solution)/shard_map/ppermute | solution.py:442
  33.3 0.7 %slice_bitcast_fusion = (f32[16,8,128]{2,1,0:T(8,128)}, f32[16,8,128]{2,1,0:T(8,128)}) fusion(f32[2,16,8,128]{3,2,1,0:T(8,128)S(1)} %add.7), kind=kLoop, calls=%fused_computation | loop fusion | bytes 262144 | tf_op jit(solution)/shard_map/squeeze | solution.py:530
  (32 shorter events, 0.1 us)
Async XLA Ops:
  0.6 1.4 %copy-start.21 = (f32[1,3]{1,0:T(1,128)S(1)}, f32[1,3]{1,0:T(1,128)}, u32[]{:S(2)}) copy-start(f32[1,3]{1,0:T(1,128)} %amp_ref.3) | copy-start | bytes 40
  1.3 0.7 %copy-start.17 = (f32[3]{0:T(128)S(1)}, f32[3]{0:T(128)}, u32[]{:S(2)}) copy-start(f32[3]{0:T(128)} %relax_ref.5) | copy-start | bytes 40
  1.3 0.7 %copy-start.18 = (f32[3]{0:T(128)S(1)}, f32[3]{0:T(128)}, u32[]{:S(2)}) copy-start(f32[3]{0:T(128)} %weight_ref.5) | copy-start | bytes 40
  1.3 0.7 %copy-start.20 = (f32[1,3]{1,0:T(1,128)S(1)}, f32[1,3]{1,0:T(1,128)}, u32[]{:S(2)}) copy-start(f32[1,3]{1,0:T(1,128)} %slow_ref.3) | copy-start | bytes 40
  2.0 1.1 %copy-start = (f32[1,3,3,16,8,128]{5,4,3,2,1,0:T(8,128)S(1)}, f32[1,3,3,16,8,128]{5,4,3,2,1,0:T(8,128)}, u32[]{:S(2)}) copy-start(f32[1,3,3,16,8,128]{5,4,3,2,1,0:T(8,128)} %sm_ref.3) | copy-start | bytes 1769476
  3.1 0.9 %copy-start.2 = (f32[1,3,16,8,128]{4,3,2,1,0:T(8,128)S(1)}, f32[1,3,16,8,128]{4,3,2,1,0:T(8,128)}, u32[]{:S(2)}) copy-start(f32[1,3,16,8,128]{4,3,2,1,0:T(8,128)} %w_ref.5) | copy-start | bytes 589828
  4.0 0.9 %copy-start.3 = (f32[1,3,16,8,128]{4,3,2,1,0:T(8,128)S(1)}, f32[1,3,16,8,128]{4,3,2,1,0:T(8,128)}, u32[]{:S(2)}) copy-start(f32[1,3,16,8,128]{4,3,2,1,0:T(8,128)} %bm_ref.3) | copy-start | bytes 589828
  5.0 0.8 %copy-start.5 = (f32[16,8,128]{2,1,0:T(8,128)S(1)}, f32[16,8,128]{2,1,0:T(8,128)}, u32[]{:S(2)}) copy-start(f32[16,8,128]{2,1,0:T(8,128)} %kappa_ref.5) | copy-start | bytes 196612
  5.8 0.8 %copy-start.7 = (f32[16,8,128]{2,1,0:T(8,128)S(1)}, f32[16,8,128]{2,1,0:T(8,128)}, u32[]{:S(2)}) copy-start(f32[16,8,128]{2,1,0:T(8,128)} %mu_ref.5) | copy-start | bytes 196612
  6.6 0.8 %copy-start.9 = (f32[16,8,128]{2,1,0:T(8,128)S(1)}, f32[16,8,128]{2,1,0:T(8,128)}, u32[]{:S(2)}) copy-start(f32[16,8,128]{2,1,0:T(8,128)} %buoy_ref.5) | copy-start | bytes 196612
  7.5 0.8 %copy-start.11 = (f32[16,8,128]{2,1,0:T(8,128)S(1)}, f32[16,8,128]{2,1,0:T(8,128)}, u32[]{:S(2)}) copy-start(f32[16,8,128]{2,1,0:T(8,128)} %bat_ref.1) | copy-start | bytes 196612
  8.3 0.9 %copy-start.14 = (f32[1,3,16,8,128]{4,3,2,1,0:T(8,128)S(1)}, f32[1,3,16,8,128]{4,3,2,1,0:T(8,128)}, u32[]{:S(2)}) copy-start(f32[1,3,16,8,128]{4,3,2,1,0:T(8,128)} %v_ref.1) | copy-start | bytes 589828
  9.3 0.7 %copy-start.19 = (s32[1,1,1024]{2,1,0:T(1,128)S(1)}, s32[1,1,1024]{2,1,0:T(1,128)}, u32[]{:S(2)}) copy-start(s32[1,1,1024]{2,1,0:T(1,128)} %cells_ref.1) | copy-start | bytes 12292
  9.9 14.4 %copy-start.6 = (f32[16,8,128]{2,1,0:T(8,128)S(1)}, f32[16,8,128]{2,1,0:T(8,128)}, u32[]{:S(2)}) copy-start(f32[16,8,128]{2,1,0:T(8,128)} %kappa_ref.5) | copy-start | bytes 196612
  9.9 14.4 %copy-start.8 = (f32[16,8,128]{2,1,0:T(8,128)S(1)}, f32[16,8,128]{2,1,0:T(8,128)}, u32[]{:S(2)}) copy-start(f32[16,8,128]{2,1,0:T(8,128)} %mu_ref.5) | copy-start | bytes 196612
  9.9 14.4 %copy-start.10 = (f32[16,8,128]{2,1,0:T(8,128)S(1)}, f32[16,8,128]{2,1,0:T(8,128)}, u32[]{:S(2)}) copy-start(f32[16,8,128]{2,1,0:T(8,128)} %buoy_ref.5) | copy-start | bytes 196612
  9.9 14.4 %copy-start.12 = (f32[16,8,128]{2,1,0:T(8,128)S(1)}, f32[16,8,128]{2,1,0:T(8,128)}, u32[]{:S(2)}) copy-start(f32[16,8,128]{2,1,0:T(8,128)} %bat_ref.1) | copy-start | bytes 196612
  10.0 14.4 %copy-start.13 = (f32[1,2,4,16,8,128]{5,4,3,2,1,0:T(8,128)S(1)}, f32[1,2,4,16,8,128]{5,4,3,2,1,0:T(8,128)}, u32[]{:S(2)}) copy-start(f32[1,2,4,16,8,128]{5,4,3,2,1,0:T(8,128)} %strain_ref.1) | copy-start | bytes 1572868
  10.9 13.4 %collective-permute-start = (f32[4,16,8,128]{3,2,1,0:T(8,128)S(1)}, f32[4,16,8,128]{3,2,1,0:T(8,128)S(1)}, u32[]{:S(2)}, u32[]{:S(2)}) collective-permute-start(f32[4,16,8,128]{3,2,1,0:T(8,128)S(1)} %get-tuple-element.30), channel_id=1, source_target_pairs={{0,1},{1,0},{2,3},{3,2},{4,5},{5,4},{6,7},{7,6},{8,9},{9,8},{10,11... | collective-permute-start | bytes 786440 | tf_op jit(solution)/shard_map/ppermute | solution.py:433
  11.0 13.3 %collective-permute-start.1 = (f32[4,16,8,128]{3,2,1,0:T(8,128)S(1)}, f32[4,16,8,128]{3,2,1,0:T(8,128)S(1)}, u32[]{:S(2)}, u32[]{:S(2)}) collective-permute-start(f32[4,16,8,128]{3,2,1,0:T(8,128)S(1)} %get-tuple-element.31), channel_id=1, source_target_pairs={{0,0},{1,2},{2,1},{3,3},{4,4},{5,6},{6,5},{7,7},{8,8},{9,10},{10,9... | collective-permute-start | bytes 786440 | tf_op jit(solution)/shard_map/ppermute | solution.py:433
  16.1 8.2 %collective-permute-start.2 = (f32[28,8,128]{2,1,0:T(8,128)S(1)}, f32[28,8,128]{2,1,0:T(8,128)S(1)}, u32[]{:S(2)}, u32[]{:S(2)}) collective-permute-start(f32[28,8,128]{2,1,0:T(8,128)S(1)} %get-tuple-element.32), channel_id=1, source_target_pairs={{0,4},{1,5},{2,6},{3,7},{4,0},{5,1},{6,2},{7,3},{8,12},{9,13},{10,... | collective-permute-start | bytes 344072 | tf_op jit(solution)/shard_map/ppermute | solution.py:433
  17.6 5.0 %collective-permute-start.3 = (f32[8,8,128]{2,1,0:T(8,128)S(1)}, f32[8,8,128]{2,1,0:T(8,128)S(1)}, u32[]{:S(2)}, u32[]{:S(2)}) collective-permute-start(f32[8,8,128]{2,1,0:T(8,128)S(1)} %get-tuple-element.33), channel_id=1, source_target_pairs={{0,5},{1,4},{2,7},{3,6},{4,1},{5,0},{6,3},{7,2},{8,13},{9,12},{10,... | collective-permute-start | bytes 98312 | tf_op jit(solution)/shard_map/ppermute | solution.py:433
  17.6 6.7 %collective-permute-start.4 = (f32[8,8,128]{2,1,0:T(8,128)S(1)}, f32[8,8,128]{2,1,0:T(8,128)S(1)}, u32[]{:S(2)}, u32[]{:S(2)}) collective-permute-start(f32[8,8,128]{2,1,0:T(8,128)S(1)} %get-tuple-element.34), channel_id=1, source_target_pairs={{0,0},{1,6},{2,5},{3,3},{4,4},{5,2},{6,1},{7,7},{8,8},{9,14},{10,1... | collective-permute-start | bytes 98312 | tf_op jit(solution)/shard_map/ppermute | solution.py:433
  24.4 4.9 %copy-start.1 = (f32[1,3,3,16,8,128]{5,4,3,2,1,0:T(8,128)S(1)}, f32[1,3,3,16,8,128]{5,4,3,2,1,0:T(8,128)}, u32[]{:S(2)}) copy-start(f32[1,3,3,16,8,128]{5,4,3,2,1,0:T(8,128)} %sm_ref.3) | copy-start | bytes 1769476
  24.4 4.9 %copy-start.16 = (f32[16,8,128]{2,1,0:T(8,128)S(1)}, f32[16,8,128]{2,1,0:T(8,128)}, u32[]{:S(2)}) copy-start(f32[16,8,128]{2,1,0:T(8,128)} %sat_ref.1) | copy-start | bytes 196612
  26.3 3.0 %copy-start.4 = (f32[1,3,16,8,128]{4,3,2,1,0:T(8,128)S(1)}, f32[1,3,16,8,128]{4,3,2,1,0:T(8,128)}, u32[]{:S(2)}) copy-start(f32[1,3,16,8,128]{4,3,2,1,0:T(8,128)} %bm_ref.3) | copy-start | bytes 589828
  26.3 3.0 %copy-start.15 = (f32[1,3,16,8,128]{4,3,2,1,0:T(8,128)S(1)}, f32[1,3,16,8,128]{4,3,2,1,0:T(8,128)}, u32[]{:S(2)}) copy-start(f32[1,3,16,8,128]{4,3,2,1,0:T(8,128)} %get-tuple-element.21.w1_ref) | copy-start | bytes 589828
  26.3 1.3 %collective-permute-start.5 = (f32[2,16,8,128]{3,2,1,0:T(8,128)S(1)}, f32[2,16,8,128]{3,2,1,0:T(8,128)S(1)}, u32[]{:S(2)}, u32[]{:S(2)}) collective-permute-start(f32[2,16,8,128]{3,2,1,0:T(8,128)S(1)} %get-tuple-element.45), channel_id=1, source_target_pairs={{0,8},{8,0},{16,24},{24,16},{1,9},{9,1},{17,25},{25,17},{2,10},{10... | collective-permute-start | bytes 393224 | tf_op jit(solution)/shard_map/ppermute | solution.py:442
  27.6 5.6 %collective-permute-start.6 = (f32[2,16,8,128]{3,2,1,0:T(8,128)S(1)}, f32[2,16,8,128]{3,2,1,0:T(8,128)S(1)}, u32[]{:S(2)}, u32[]{:S(2)}) collective-permute-start(f32[2,16,8,128]{3,2,1,0:T(8,128)S(1)} %add.6), channel_id=1, source_target_pairs={{0,16},{8,24},{16,0},{24,8},{1,17},{9,25},{17,1},{25,9},{2,18},{10... | collective-permute-start | bytes 393224 | tf_op jit(solution)/shard_map/ppermute | solution.py:442

commit v2 on v1

--- a/solution.py
+++ b/solution.py
@@ -23,6 +23,7 @@
     + [("z1", 1), ("atten", 1)]
 )
 X_AT = {key: at for at, key in enumerate(X_LIST)}
+PACK_ARGS = 15
 D_LIST = [(t, 1) for t in range(4)] + [(t, 2) for t in range(3)] + [(0, 3)]
 
 
@@ -87,17 +88,24 @@
 
 
 def pack_kernel(
-    counts, np_, w_ref, v_ref, bm_ref, sm_ref, kappa_ref, mu_ref, buoy_ref, at_ref, relax_ref, weight_ref,
-    slow_ref, amp_ref, onset_ref, cells_ref, count_ref, *outs,
+    counts, np_, *refs,
 ):
     nx, ny, cx = counts
+    count_ref, onset_ref, given, rest = refs[0], refs[1], refs[2:PACK_ARGS], refs[PACK_ARGS:]
+    outs, held, sems = rest[: 7 + 3 * np_], rest[7 + 3 * np_ : -1], rest[-1]
+    copies = [pltpu.make_async_copy(a, b, sems.at[k]) for k, (a, b) in enumerate(zip(given, held))]
+    for copy in copies:
+        copy.start()
+    (cells_ref, relax_ref, weight_ref, slow_ref, amp_ref, buoy_ref, mu_ref, kappa_ref, at_ref, w_ref, v_ref, bm_ref,
+     sm_ref) = held
     y_refs = outs[:2]
     x_refs = outs[2 : 2 + np_]
     d_refs = outs[2 + np_ : 2 + 3 * np_]
-    mask_ref, base_ref, zsum_ref, z1_ref = outs[2 + 3 * np_ :]
+    pulse_ref, coef_ref, base_ref, zsum_ref, z1_ref = outs[2 + 3 * np_ :]
     i, j = lax.axis_index("gx"), lax.axis_index("gy")
     rows = cx * TILE[0]
     slots = cells_ref.shape[2]
+    copies[0].wait()
     cells = cells_ref[0]
     slot = lax.broadcasted_iota(jnp.int32, (1, slots), 1)
     live = slot < count_ref[0, 0]
@@ -110,9 +118,15 @@
     mask = lax.dot_general(
         hot_row, hot_lane, (((1,), (1,)), ((), ())), preferred_element_type=jnp.float32
     )
-    mask_ref[...] = mask.reshape(cx, TILE[0], TILE[1])
-
-    decay, _ = decay_gain(relax_ref, weight_ref)
+    mask = mask.reshape(cx, TILE[0], TILE[1])
+
+    for copy in copies[1:]:
+        copy.wait()
+    decay, gain = decay_gain(relax_ref, weight_ref)
+    for l in range(3):
+        coef_ref[l] = decay[l]
+        coef_ref[3 + l] = gain[l]
+        coef_ref[6 + l] = jnp.full(TILE, amp_ref[0, l], jnp.float32)
     phase = wave_phase(slow_ref, onset_ref, counts)
     row = row_of()
     keep = ((row >> 2) ^ (j & 1)) == 1
@@ -129,7 +143,8 @@
         kappa, mu, atten = kappa_ref[x], mu_ref[x], at_ref[x]
         bb = DT2 * buoy_ref[x]
         bbmu = bb * mu
-        pulse = pulse_of(-phase(x)) * mask_ref[x]
+        pulse = pulse_of(-phase(x)) * mask[x]
+        pulse_ref[x] = pulse_of(TIME_STEP - phase(x)) * mask[x]
         base = []
         for c in range(3):
             total = sm_ref[0, 0, c, x] + sm_ref[0, 1, c, x] + sm_ref[0, 2, c, x]
@@ -188,7 +203,7 @@
 
 
 def first_kernel(
-    counts, np_, w_ref, kappa_ref, mu_ref, buoy_ref, at_ref, strain_ref, relax_ref, weight_ref, base_ref, zsum_ref,
+    counts, np_, w_ref, kappa_ref, mu_ref, buoy_ref, at_ref, strain_ref, coef_ref, base_ref, zsum_ref,
     z1_ref, *rest,
 ):
     nx, ny, cx = counts
@@ -354,8 +369,7 @@
     def w1_h(c, x):
         return w1h[c, 1 + x]
 
-    _, gain = decay_gain(relax_ref, weight_ref)
-    gains = gain[0] + gain[1] + gain[2]
+    gains = coef_ref[3] + coef_ref[4] + coef_ref[5]
     for x in range(-1, cx + 1):
         inside = 0 <= x < cx
         db, dh = divergence(w1_b, w1_h, x, inside)
@@ -381,12 +395,10 @@
 
 
 def last_kernel(
-    counts, w_ref, bm_ref, sm_ref, kappa_ref, mu_ref, buoy_ref, bat_ref, sat_ref, relax_ref, weight_ref, slow_ref,
-    amp_ref, onset_ref, mask_ref, w1_ref, d0_ref, l0_ref, d1_ref, l1_ref, pb_ref, ph_ref, w2_ref, bn_ref, sn_ref,
+    counts, w_ref, bm_ref, sm_ref, kappa_ref, mu_ref, buoy_ref, bat_ref, sat_ref, coef_ref, pulse_ref, w1_ref, d0_ref, l0_ref, d1_ref, l1_ref, pb_ref, ph_ref, w2_ref, bn_ref, sn_ref,
 ):
     nx, ny, cx = counts
-    decay, gain = decay_gain(relax_ref, weight_ref)
-    phase = wave_phase(slow_ref, onset_ref, counts)
+    decay, gain, amp = ([coef_ref[3 * k + l] for l in range(3)] for k in range(3))
     for x in range(cx):
         bulk = bat_ref[x] * kappa_ref[x]
         q0, q1 = bulk * d0_ref[x], bulk * d1_ref[x]
@@ -403,7 +415,7 @@
         ]
         mu = mu_ref[x]
         shear = sat_ref[x] * mu
-        pulse = pulse_of(TIME_STEP - phase(x)) * mask_ref[x]
+        pulse = pulse_ref[x]
         bb = DT2 * buoy_ref[x]
         for c in range(3):
             l1 = l1_ref[c, x]
@@ -413,7 +425,7 @@
                 now = decay[l] * sm_ref[0, l, c, x] + gain[l] * q0
                 sn_ref[0, l, c, x] = decay[l] * now + gain[l] * q1
                 total = now if total is None else total + now
-            force = grad[c] + mu * l1 - total + amp_ref[0, c] * pulse
+            force = grad[c] + mu * l1 - total + amp[c] * pulse
             w2_ref[0, c, x] = 2.0 * w1_ref[0, c, x] - w_ref[0, c, x] + bb * force
 
 
@@ -448,10 +460,6 @@
     return pl.BlockSpec(memory_space=pltpu.VMEM)
 
 
-def smem():
-    return pl.BlockSpec(memory_space=pltpu.SMEM)
-
-
 def body(
     adjoint_now, adjoint_old, bulk_memory, shear_memory, forward_strain, bulk_modulus, shear_modulus, buoyancy,
     bulk_atten, shear_atten, relax_time, mechanism_weight, event_slowness, event_amplitude, event_onset,
@@ -467,19 +475,32 @@
         return jax.ShapeDtypeStruct((*lead, *TILE), f32)
 
     params = pltpu.CompilerParams(vmem_limit_bytes=24 * 1024 * 1024)
+    pack_args = (
+        boundary_count, event_onset, boundary_cells, relax_time, mechanism_weight, event_slowness, event_amplitude,
+        buoyancy, shear_modulus, bulk_modulus, bulk_atten, adjoint_now, adjoint_old, bulk_memory, shear_memory,
+    )
     packed = pl.pallas_call(
         functools.partial(pack_kernel, counts, np_),
         out_shape=[field(4, cx)] * 2
         + [field(len(X_LIST))] * np_
         + [field(len(D_LIST))] * (2 * np_)
-        + [field(cx), field(3, cx), field(cx), field(cx)],
-        in_specs=[vmem()] * 8 + [smem()] * 5 + [vmem(), smem()],
-        out_specs=[vmem()] * (2 + 3 * np_ + 4),
+        + [field(cx), field(9), field(3, cx), field(cx), field(cx)],
+        in_specs=[
+            pl.BlockSpec(memory_space=pltpu.HBM if given.size > 1 else pltpu.SMEM) for given in pack_args
+        ],
+        out_specs=[vmem()] * (2 + 3 * np_ + 5),
+        scratch_shapes=[
+            (pltpu.SMEM if k in (1, 2, 3, 4) else pltpu.VMEM)(given.shape, given.dtype)
+            for k, given in enumerate(pack_args[2:])
+        ]
+        + [pltpu.SemaphoreType.DMA((PACK_ARGS - 2,))],
         compiler_params=params,
         name="pack",
     )(
-        adjoint_now, adjoint_old, bulk_memory, shear_memory, bulk_modulus, shear_modulus, buoyancy, bulk_atten,
-        relax_time, mechanism_weight, event_slowness, event_amplitude, event_onset, boundary_cells, boundary_count,
+        *(
+            pltpu.with_memory_space_constraint(given, pltpu.HBM) if given.size > 1 else given
+            for given in pack_args
+        )
     )
     shape = (nx, ny)
     ys = [matched(packed[q], shape, False, True, 0, q) for q in range(2)]
@@ -487,14 +508,14 @@
     ds = [
         matched(packed[2 + np_ + 2 * p + q], shape, True, True, p, q) for p in range(np_) for q in range(2)
     ]
-    mask, base, zsum, z1 = packed[2 + 3 * np_ :]
+    pulse, coef, base, zsum, z1 = packed[2 + 3 * np_ :]
 
     first = pl.pallas_call(
         functools.partial(first_kernel, counts, np_),
         out_shape=[
             field(2, cx), field(1, 3, cx), field(cx), field(3, cx), field(cx), field(3, cx), field(cx + 2), field(cx),
         ],
-        in_specs=[vmem()] * 6 + [smem()] * 2 + [vmem()] * (3 + 2 + 3 * np_),
+        in_specs=[vmem()] * (12 + 3 * np_),
         out_specs=[vmem()] * 8,
         scratch_shapes=[
             pltpu.VMEM((2 * len(X_LIST), *TILE), f32),
@@ -509,8 +530,7 @@
         compiler_params=params,
         name="first",
     )(
-        adjoint_now, bulk_modulus, shear_modulus, buoyancy, bulk_atten, forward_strain, relax_time, mechanism_weight,
-        base, zsum, z1, *ys, *xs, *ds,
+        adjoint_now, bulk_modulus, shear_modulus, buoyancy, bulk_atten, forward_strain, coef, base, zsum, z1, *ys, *xs, *ds,
     )
     term, w1, d0, l0, d1, l1, pb, ph = first
     total = event_sum(term)
@@ -518,14 +538,14 @@
     w2, bulk_next, shear_next = pl.pallas_call(
         functools.partial(last_kernel, counts),
         out_shape=[field(1, 3, cx), field(1, 3, cx), field(1, 3, 3, cx)],
-        in_specs=[vmem()] * 8 + [smem()] * 5 + [vmem()] * 8,
+        in_specs=[vmem()] * 17,
         out_specs=[vmem()] * 3,
         compiler_params=params,
         cost_estimate=pl.CostEstimate(flops=3_000_000, bytes_accessed=4_000_000, transcendentals=0),
         name="last",
     )(
         adjoint_now, bulk_memory, shear_memory, bulk_modulus, shear_modulus, buoyancy, bulk_atten, shear_atten,
-        relax_time, mechanism_weight, event_slowness, event_amplitude, event_onset, mask, w1, d0, l0, d1, l1, pb, ph,
+        coef, pulse, w1, d0, l0, d1, l1, pb, ph,
     )
     return w2, w1, bulk_next, shear_next, total[0], total[1]
 

time: 34.4 us -> 26.6 us (0.77)
  local copies, waits for them, and re-layouts: 8.59 us -> 0.7 us
  waiting for transfers between devices: 8.24 us -> 8.84 us
    unnamed x44 -> x20, local copies, waits for them, and re-layouts: 7.94 us -> 0.05 us
    pallas_call x1, Pallas kernels: 0.97 us -> 1.89 us  [body(): pl.pallas_call(functools.partial(pack_kernel, counts, np_), out_shape=[fi...]
    ppermute x2, waiting for transfers between devices: 3.55 us -> 4.16 us  [event_sum(): lax.ppermute(value, 'event', [(e, e ^ step) for e in range(count)])]
    pallas_call x1, Pallas kernels: 1.81 us -> 1.21 us  [body(): pl.pallas_call(functools.partial(last_kernel, counts), out_shape=[field(1...]
    pallas_call x1, Pallas kernels: 1.89 us -> 1.37 us  [body(): pl.pallas_call(functools.partial(first_kernel, counts, np_), out_shape=[f...]
where the time goes in v2:
time: 26.6 us; the launch traced here: 26.4 us
  starting transfers between devices  10.3 us (39%)
  waiting for transfers between devices  8.84 us (33%)
  Pallas kernels  4.47 us (17%)
  between operations  2.09 us (8%)
  local copies, waits for them, and re-layouts  0.7 us (3%)
    ppermute x5, starting transfers between devices, matched(): return lax.ppermute(value, ('gx', 'gy'), pairs)  8.67 us
    ppermute x5, waiting for transfers between devices, matched(): return lax.ppermute(value, ('gx', 'gy'), pairs)  4.68 us
    ppermute x2, waiting for transfers between devices, event_sum(): lax.ppermute(value, 'event', [(e, e ^ step) for e in range(count)])  4.16 us
    pallas_call x1, Pallas kernels, body(): pl.pallas_call(functools.partial(pack_kernel, counts, np_), out_shape=[fi...  1.89 us
    ppermute x2, starting transfers between devices, event_sum(): lax.ppermute(value, 'event', [(e, e ^ step) for e in range(count)])  1.59 us
    pallas_call x1, Pallas kernels, body(): pl.pallas_call(functools.partial(first_kernel, counts, np_), out_shape=[f...  1.37 us
    pallas_call x1, Pallas kernels, body(): pl.pallas_call(functools.partial(last_kernel, counts), out_shape=[field(1...  1.21 us
    squeeze x1, local copies, waits for them, and re-layouts, body(): return (w2, w1, bulk_next, shear_next, total[0], total[1])  0.66 us
  transfers between devices with their start and end apart: 7, of which 4 were waited for; matrix products, arithmetic and copies ran while one was open for 0% of the time, Pallas kernels for 5%

profile of v2, /device:TPU:8, one launch (start us, length us, event | category | flops | bytes accessed | tf_op | source)
XLA Modules:
  0.0 26.4 jit_solution(11276769288757986472)
XLA Ops:
  1.9 0.0 copy-start.1
  1.9 0.0 copy-start.3
  1.9 0.0 copy-start.4
  2.0 0.0 copy-start.5
  2.0 0.0 copy-start.6
  2.0 0.0 copy-start.7
  2.0 1.9 %pack.1 = (f32[4,16,8,128]{3,2,1,0:T(8,128)S(1)}, f32[4,16,8,128]{3,2,1,0:T(8,128)S(1)}, f32[28,8,128]{2,1,0:T(8,128)S(1)}, f32[8,8,128]{2,1,0:T(8,128)S(1)}, f3...) custom-call(s32[1,1]{1,0:T(1,128)S(6)} %copy.24.refs_0_, ...), custom_call_target="tpu_custom_call" | custom-call | tf_op jit(solution)/shard_map/pack/pallas_call | solution.py:482
  3.9 0.1 collective-permute-start
  4.0 5.0 %collective-permute-start.1 = (f32[4,16,8,128]{3,2,1,0:T(8,128)S(1)}, f32[4,16,8,128]{3,2,1,0:T(8,128)S(1)}, u32[]{:S(2)}, u32[]{:S(2)}) collective-permute-start(f32[4,16,8,128]{3,2,1,0:T(8,128)S(1)} %get-tuple-element.33), channel_id=1, source_target_pairs={{0,0},{1,2},{2,1},{3,3},{4,4},{5,6},{6,5},{7,7},{8,8},{9,10},{10,9... | collective-permute-start | bytes 786440 | tf_op jit(solution)/shard_map/ppermute | solution.py:445
  9.0 1.5 %collective-permute-start.2 = (f32[28,8,128]{2,1,0:T(8,128)S(1)}, f32[28,8,128]{2,1,0:T(8,128)S(1)}, u32[]{:S(2)}, u32[]{:S(2)}) collective-permute-start(f32[28,8,128]{2,1,0:T(8,128)S(1)} %get-tuple-element.34), channel_id=1, source_target_pairs={{0,4},{1,5},{2,6},{3,7},{4,0},{5,1},{6,2},{7,3},{8,12},{9,13},{10,... | collective-permute-start | bytes 344072 | tf_op jit(solution)/shard_map/ppermute | solution.py:445
  10.6 0.0 collective-permute-start.3
  10.6 2.0 %collective-permute-start.4 = (f32[8,8,128]{2,1,0:T(8,128)S(1)}, f32[8,8,128]{2,1,0:T(8,128)S(1)}, u32[]{:S(2)}, u32[]{:S(2)}) collective-permute-start(f32[8,8,128]{2,1,0:T(8,128)S(1)} %get-tuple-element.36), channel_id=1, source_target_pairs={{0,0},{1,6},{2,5},{3,3},{4,4},{5,2},{6,1},{7,7},{8,8},{9,14},{10,1... | collective-permute-start | bytes 98312 | tf_op jit(solution)/shard_map/ppermute | solution.py:445
  12.6 3.0 %collective-permute-done.3.rest_3_ = f32[8,8,128]{2,1,0:T(8,128)S(1)} collective-permute-done((f32[8,8,128]{2,1,0:T(8,128)S(1)}, f32[8,8,128]{2,1,0:T(8,128)S(1)}, u32[]{:S(2)}, u32[]{:S(2)}) %collective-permute-start.3) | collective-permute-done | bytes 32800 | tf_op jit(solution)/shard_map/ppermute | solution.py:445
  15.5 1.7 %collective-permute-done.4.rest_4_ = f32[8,8,128]{2,1,0:T(8,128)S(1)} collective-permute-done((f32[8,8,128]{2,1,0:T(8,128)S(1)}, f32[8,8,128]{2,1,0:T(8,128)S(1)}, u32[]{:S(2)}, u32[]{:S(2)}) %collective-permute-start.4) | collective-permute-done | bytes 32800 | tf_op jit(solution)/shard_map/ppermute | solution.py:445
  17.3 0.0 collective-permute-done.2.rest_2_
  17.3 0.0 collective-permute-done.rest_0_
  17.3 0.0 collective-permute-done.1.rest_1_
  17.3 0.0 copy-done.1
  17.3 0.0 copy-done.3
  17.3 0.0 copy-done.4
  17.3 0.0 copy-done.5
  17.3 0.0 copy-done.6
  17.3 0.0 copy-start
  17.3 0.0 copy-start.9
  17.4 1.4 %first.1 = (f32[2,16,8,128]{3,2,1,0:T(8,128)S(1)}, f32[1,3,16,8,128]{4,3,2,1,0:T(8,128)}, f32[16,8,128]{2,1,0:T(8,128)S(1)}, f32[3,16,8,128]{3,2,1,0:T(8,128)S(1...) custom-call(f32[1,3,16,8,128]{4,3,2,1,0:T(8,128)S(1)} %copy-done.1, ...), custom_call_target="tpu_custom_call" | custom-call | tf_op jit(solution)/shard_map/first/pallas_call | solution.py:513
  18.7 0.0 collective-permute-start.5
  18.7 1.3 %collective-permute-done.5 = f32[2,16,8,128]{3,2,1,0:T(8,128)S(1)} collective-permute-done((f32[2,16,8,128]{3,2,1,0:T(8,128)S(1)}, f32[2,16,8,128]{3,2,1,0:T(8,128)S(1)}, u32[]{:S(2)}, u32[]{:S(2)}) %collective-permute-start.5) | collective-permute-done | bytes 131104 | tf_op jit(solution)/shard_map/ppermute | solution.py:454
  20.1 1.6 %collective-permute-start.6 = (f32[2,16,8,128]{3,2,1,0:T(8,128)S(1)}, f32[2,16,8,128]{3,2,1,0:T(8,128)S(1)}, u32[]{:S(2)}, u32[]{:S(2)}) collective-permute-start(f32[2,16,8,128]{3,2,1,0:T(8,128)S(1)} %add.6), channel_id=1, source_target_pairs={{0,16},{8,24},{16,0},{24,8},{1,17},{9,25},{17,1},{25,9},{2,18},{10... | collective-permute-start | bytes 393224 | tf_op jit(solution)/shard_map/ppermute | solution.py:454
  21.7 0.0 copy-done.9
  21.7 1.2 %last.1 = (f32[1,3,16,8,128]{4,3,2,1,0:T(8,128)}, f32[1,3,16,8,128]{4,3,2,1,0:T(8,128)}, f32[1,3,3,16,8,128]{5,4,3,2,1,0:T(8,128)}) custom-call(f32[1,3,16,8,128]{4,3,2,1,0:T(8,128)S(1)} %copy-done.1, f32[1,3,16,8,128]{4,3,2,1,0:T(8,128)S(1)} %copy-done.2, f32[1,3,3,16,8,128]{5,4,3,2,1,0:T(8,128)S(1)} %copy-done, f32[16,8,128]{2,1,0:T(8,128)S(1)} %copy-done.3, ...), custom_call_target="tpu_custom_call" | custom-call | flops 3000000 | bytes 4000000 | tf_op jit(solution)/shard_map/last/pallas_call | solution.py:538
  22.9 2.8 %collective-permute-done.6 = f32[2,16,8,128]{3,2,1,0:T(8,128)S(1)} collective-permute-done((f32[2,16,8,128]{3,2,1,0:T(8,128)S(1)}, f32[2,16,8,128]{3,2,1,0:T(8,128)S(1)}, u32[]{:S(2)}, u32[]{:S(2)}) %collective-permute-start.6) | collective-permute-done | bytes 131104 | tf_op jit(solution)/shard_map/ppermute | solution.py:454
  25.7 0.7 %slice_bitcast_fusion = (f32[16,8,128]{2,1,0:T(8,128)}, f32[16,8,128]{2,1,0:T(8,128)}) fusion(f32[2,16,8,128]{3,2,1,0:T(8,128)S(1)} %add.7), kind=kLoop, calls=%fused_computation | loop fusion | bytes 262144 | tf_op jit(solution)/shard_map/squeeze | solution.py:550
  (8 shorter events, 0.0 us)
Async XLA Ops:
  1.9 15.3 %copy-start.1 = (f32[1,3,16,8,128]{4,3,2,1,0:T(8,128)S(1)}, f32[1,3,16,8,128]{4,3,2,1,0:T(8,128)}, u32[]{:S(2)}) copy-start(f32[1,3,16,8,128]{4,3,2,1,0:T(8,128)} %w_ref.3) | copy-start | bytes 589828
  1.9 15.3 %copy-start.3 = (f32[16,8,128]{2,1,0:T(8,128)S(1)}, f32[16,8,128]{2,1,0:T(8,128)}, u32[]{:S(2)}) copy-start(f32[16,8,128]{2,1,0:T(8,128)} %kappa_ref.3) | copy-start | bytes 196612
  1.9 15.3 %copy-start.4 = (f32[16,8,128]{2,1,0:T(8,128)S(1)}, f32[16,8,128]{2,1,0:T(8,128)}, u32[]{:S(2)}) copy-start(f32[16,8,128]{2,1,0:T(8,128)} %mu_ref.3) | copy-start | bytes 196612
  2.0 15.3 %copy-start.5 = (f32[16,8,128]{2,1,0:T(8,128)S(1)}, f32[16,8,128]{2,1,0:T(8,128)}, u32[]{:S(2)}) copy-start(f32[16,8,128]{2,1,0:T(8,128)} %buoy_ref.3) | copy-start | bytes 196612
  2.0 15.3 %copy-start.6 = (f32[16,8,128]{2,1,0:T(8,128)S(1)}, f32[16,8,128]{2,1,0:T(8,128)}, u32[]{:S(2)}) copy-start(f32[16,8,128]{2,1,0:T(8,128)} %bat_ref.1) | copy-start | bytes 196612
  2.0 15.3 %copy-start.7 = (f32[1,2,4,16,8,128]{5,4,3,2,1,0:T(8,128)S(1)}, f32[1,2,4,16,8,128]{5,4,3,2,1,0:T(8,128)}, u32[]{:S(2)}) copy-start(f32[1,2,4,16,8,128]{5,4,3,2,1,0:T(8,128)} %strain_ref.1) | copy-start | bytes 1572868
  3.9 13.4 %collective-permute-start = (f32[4,16,8,128]{3,2,1,0:T(8,128)S(1)}, f32[4,16,8,128]{3,2,1,0:T(8,128)S(1)}, u32[]{:S(2)}, u32[]{:S(2)}) collective-permute-start(f32[4,16,8,128]{3,2,1,0:T(8,128)S(1)} %get-tuple-element.32), channel_id=1, source_target_pairs={{0,1},{1,0},{2,3},{3,2},{4,5},{5,4},{6,7},{7,6},{8,9},{9,8},{10,11... | collective-permute-start | bytes 786440 | tf_op jit(solution)/shard_map/ppermute | solution.py:445
  4.0 13.3 %collective-permute-start.1 = (f32[4,16,8,128]{3,2,1,0:T(8,128)S(1)}, f32[4,16,8,128]{3,2,1,0:T(8,128)S(1)}, u32[]{:S(2)}, u32[]{:S(2)}) collective-permute-start(f32[4,16,8,128]{3,2,1,0:T(8,128)S(1)} %get-tuple-element.33), channel_id=1, source_target_pairs={{0,0},{1,2},{2,1},{3,3},{4,4},{5,6},{6,5},{7,7},{8,8},{9,10},{10,9... | collective-permute-start | bytes 786440 | tf_op jit(solution)/shard_map/ppermute | solution.py:445
  9.0 8.2 %collective-permute-start.2 = (f32[28,8,128]{2,1,0:T(8,128)S(1)}, f32[28,8,128]{2,1,0:T(8,128)S(1)}, u32[]{:S(2)}, u32[]{:S(2)}) collective-permute-start(f32[28,8,128]{2,1,0:T(8,128)S(1)} %get-tuple-element.34), channel_id=1, source_target_pairs={{0,4},{1,5},{2,6},{3,7},{4,0},{5,1},{6,2},{7,3},{8,12},{9,13},{10,... | collective-permute-start | bytes 344072 | tf_op jit(solution)/shard_map/ppermute | solution.py:445
  10.6 5.0 %collective-permute-start.3 = (f32[8,8,128]{2,1,0:T(8,128)S(1)}, f32[8,8,128]{2,1,0:T(8,128)S(1)}, u32[]{:S(2)}, u32[]{:S(2)}) collective-permute-start(f32[8,8,128]{2,1,0:T(8,128)S(1)} %get-tuple-element.35), channel_id=1, source_target_pairs={{0,5},{1,4},{2,7},{3,6},{4,1},{5,0},{6,3},{7,2},{8,13},{9,12},{10,... | collective-permute-start | bytes 98312 | tf_op jit(solution)/shard_map/ppermute | solution.py:445
  10.6 6.7 %collective-permute-start.4 = (f32[8,8,128]{2,1,0:T(8,128)S(1)}, f32[8,8,128]{2,1,0:T(8,128)S(1)}, u32[]{:S(2)}, u32[]{:S(2)}) collective-permute-start(f32[8,8,128]{2,1,0:T(8,128)S(1)} %get-tuple-element.36), channel_id=1, source_target_pairs={{0,0},{1,6},{2,5},{3,3},{4,4},{5,2},{6,1},{7,7},{8,8},{9,14},{10,1... | collective-permute-start | bytes 98312 | tf_op jit(solution)/shard_map/ppermute | solution.py:445
  17.3 4.3 %copy-start = (f32[1,3,3,16,8,128]{5,4,3,2,1,0:T(8,128)S(1)}, f32[1,3,3,16,8,128]{5,4,3,2,1,0:T(8,128)}, u32[]{:S(2)}) copy-start(f32[1,3,3,16,8,128]{5,4,3,2,1,0:T(8,128)} %sm_ref.1) | copy-start | bytes 1769476
  17.3 4.3 %copy-start.9 = (f32[16,8,128]{2,1,0:T(8,128)S(1)}, f32[16,8,128]{2,1,0:T(8,128)}, u32[]{:S(2)}) copy-start(f32[16,8,128]{2,1,0:T(8,128)} %sat_ref.1) | copy-start | bytes 196612
  18.7 3.0 %copy-start.2 = (f32[1,3,16,8,128]{4,3,2,1,0:T(8,128)S(1)}, f32[1,3,16,8,128]{4,3,2,1,0:T(8,128)}, u32[]{:S(2)}) copy-start(f32[1,3,16,8,128]{4,3,2,1,0:T(8,128)} %bm_ref.1) | copy-start | bytes 589828
  18.7 3.0 %copy-start.8 = (f32[1,3,16,8,128]{4,3,2,1,0:T(8,128)S(1)}, f32[1,3,16,8,128]{4,3,2,1,0:T(8,128)}, u32[]{:S(2)}) copy-start(f32[1,3,16,8,128]{4,3,2,1,0:T(8,128)} %get-tuple-element.22.w1_ref) | copy-start | bytes 589828
  18.7 1.3 %collective-permute-start.5 = (f32[2,16,8,128]{3,2,1,0:T(8,128)S(1)}, f32[2,16,8,128]{3,2,1,0:T(8,128)S(1)}, u32[]{:S(2)}, u32[]{:S(2)}) collective-permute-start(f32[2,16,8,128]{3,2,1,0:T(8,128)S(1)} %get-tuple-element.47), channel_id=1, source_target_pairs={{0,8},{8,0},{16,24},{24,16},{1,9},{9,1},{17,25},{25,17},{2,10},{10... | collective-permute-start | bytes 393224 | tf_op jit(solution)/shard_map/ppermute | solution.py:454
  20.1 5.6 %collective-permute-start.6 = (f32[2,16,8,128]{3,2,1,0:T(8,128)S(1)}, f32[2,16,8,128]{3,2,1,0:T(8,128)S(1)}, u32[]{:S(2)}, u32[]{:S(2)}) collective-permute-start(f32[2,16,8,128]{3,2,1,0:T(8,128)S(1)} %add.6), channel_id=1, source_target_pairs={{0,16},{8,24},{16,0},{24,8},{1,17},{9,25},{17,1},{25,9},{2,18},{10... | collective-permute-start | bytes 393224 | tf_op jit(solution)/shard_map/ppermute | solution.py:454

commit v3 on v2

--- a/solution.py
+++ b/solution.py
@@ -359,7 +359,7 @@
             w1b[c, 2 + x] = value
             if inside:
                 l0_ref[c, x] = lb
-                w1_ref[0, c, x] = value
+                w1_ref[c, x] = value
             if with_halo:
                 w1h[c, 1 + x] = halo(f"base{c}", x) + hbb * grad_h[c] + hbbmu * lh
 
@@ -395,7 +395,7 @@
 
 
 def last_kernel(
-    counts, w_ref, bm_ref, sm_ref, kappa_ref, mu_ref, buoy_ref, bat_ref, sat_ref, coef_ref, pulse_ref, w1_ref, d0_ref, l0_ref, d1_ref, l1_ref, pb_ref, ph_ref, w2_ref, bn_ref, sn_ref,
+    counts, w_ref, bm_ref, sm_ref, kappa_ref, mu_ref, buoy_ref, bat_ref, sat_ref, coef_ref, pulse_ref, w1_ref, d0_ref, l0_ref, d1_ref, l1_ref, pb_ref, ph_ref, w2_ref, before_ref, bn_ref, sn_ref,
 ):
     nx, ny, cx = counts
     decay, gain, amp = ([coef_ref[3 * k + l] for l in range(3)] for k in range(3))
@@ -426,7 +426,9 @@
                 sn_ref[0, l, c, x] = decay[l] * now + gain[l] * q1
                 total = now if total is None else total + now
             force = grad[c] + mu * l1 - total + amp[c] * pulse
-            w2_ref[0, c, x] = 2.0 * w1_ref[0, c, x] - w_ref[0, c, x] + bb * force
+            w1 = w1_ref[c, x]
+            before_ref[0, c, x] = w1
+            w2_ref[0, c, x] = 2.0 * w1 - w_ref[0, c, x] + bb * force
 
 
 def matched(value, mesh_shape, along_x, along_y, p, q):
@@ -513,7 +515,7 @@
     first = pl.pallas_call(
         functools.partial(first_kernel, counts, np_),
         out_shape=[
-            field(2, cx), field(1, 3, cx), field(cx), field(3, cx), field(cx), field(3, cx), field(cx + 2), field(cx),
+            field(2, cx), field(3, cx), field(cx), field(3, cx), field(cx), field(3, cx), field(cx + 2), field(cx),
         ],
         in_specs=[vmem()] * (12 + 3 * np_),
         out_specs=[vmem()] * 8,
@@ -535,11 +537,11 @@
     term, w1, d0, l0, d1, l1, pb, ph = first
     total = event_sum(term)
 
-    w2, bulk_next, shear_next = pl.pallas_call(
+    w2, before, bulk_next, shear_next = pl.pallas_call(
         functools.partial(last_kernel, counts),
-        out_shape=[field(1, 3, cx), field(1, 3, cx), field(1, 3, 3, cx)],
+        out_shape=[field(1, 3, cx), field(1, 3, cx), field(1, 3, cx), field(1, 3, 3, cx)],
         in_specs=[vmem()] * 17,
-        out_specs=[vmem()] * 3,
+        out_specs=[vmem()] * 4,
         compiler_params=params,
         cost_estimate=pl.CostEstimate(flops=3_000_000, bytes_accessed=4_000_000, transcendentals=0),
         name="last",
@@ -547,7 +549,7 @@
         adjoint_now, bulk_memory, shear_memory, bulk_modulus, shear_modulus, buoyancy, bulk_atten, shear_atten,
         coef, pulse, w1, d0, l0, d1, l1, pb, ph,
     )
-    return w2, w1, bulk_next, shear_next, total[0], total[1]
+    return w2, before, bulk_next, shear_next, total[0], total[1]
 
 
 def solution(mesh):

time: 26.6 us -> 26.1 us (0.981)
  Pallas kernels: 4.47 us -> 3.87 us
    pallas_call x1, Pallas kernels: 1.37 us -> 0.78 us  [body(): pl.pallas_call(functools.partial(first_kernel, counts, np_), out_shape=[f...]
where the time goes in v3:
time: 26.1 us; the launch traced here: 25.9 us
  starting transfers between devices  10.3 us (39%)
  waiting for transfers between devices  8.85 us (34%)
  Pallas kernels  3.87 us (15%)
  between operations  2.1 us (8%)
  local copies, waits for them, and re-layouts  0.7 us (3%)
    ppermute x5, starting transfers between devices, matched(): return lax.ppermute(value, ('gx', 'gy'), pairs)  8.67 us
    ppermute x5, waiting for transfers between devices, matched(): return lax.ppermute(value, ('gx', 'gy'), pairs)  4.68 us
    ppermute x2, waiting for transfers between devices, event_sum(): lax.ppermute(value, 'event', [(e, e ^ step) for e in range(count)])  4.16 us
    pallas_call x1, Pallas kernels, body(): pl.pallas_call(functools.partial(pack_kernel, counts, np_), out_shape=[fi...  1.89 us
    ppermute x2, starting transfers between devices, event_sum(): lax.ppermute(value, 'event', [(e, e ^ step) for e in range(count)])  1.66 us
    pallas_call x1, Pallas kernels, body(): pl.pallas_call(functools.partial(last_kernel, counts), out_shape=[field(1...  1.19 us
    pallas_call x1, Pallas kernels, body(): pl.pallas_call(functools.partial(first_kernel, counts, np_), out_shape=[f...  0.78 us
    squeeze x1, local copies, waits for them, and re-layouts, body(): return (w2, before, bulk_next, shear_next, total[0], total[1])  0.66 us
  transfers between devices with their start and end apart: 7, of which 4 were waited for; matrix products, arithmetic and copies ran while one was open for 0% of the time, Pallas kernels for 5%

profile of v3, /device:TPU:8, one launch (start us, length us, event | category | flops | bytes accessed | tf_op | source)
XLA Modules:
  0.0 25.9 jit_solution(9472196396935270593)
XLA Ops:
  1.9 0.0 copy-start.1
  1.9 0.0 copy-start.3
  1.9 0.0 copy-start.4
  2.0 0.0 copy-start.5
  2.0 0.0 copy-start.6
  2.0 0.0 copy-start.7
  2.0 1.9 %pack.1 = (f32[4,16,8,128]{3,2,1,0:T(8,128)S(1)}, f32[4,16,8,128]{3,2,1,0:T(8,128)S(1)}, f32[28,8,128]{2,1,0:T(8,128)S(1)}, f32[8,8,128]{2,1,0:T(8,128)S(1)}, f3...) custom-call(s32[1,1]{1,0:T(1,128)S(6)} %copy.24.refs_0_, ...), custom_call_target="tpu_custom_call" | custom-call | tf_op jit(solution)/shard_map/pack/pallas_call | solution.py:484
  3.9 0.1 collective-permute-start
  4.0 5.0 %collective-permute-start.1 = (f32[4,16,8,128]{3,2,1,0:T(8,128)S(1)}, f32[4,16,8,128]{3,2,1,0:T(8,128)S(1)}, u32[]{:S(2)}, u32[]{:S(2)}) collective-permute-start(f32[4,16,8,128]{3,2,1,0:T(8,128)S(1)} %get-tuple-element.34), channel_id=1, source_target_pairs={{0,0},{1,2},{2,1},{3,3},{4,4},{5,6},{6,5},{7,7},{8,8},{9,10},{10,9... | collective-permute-start | bytes 786440 | tf_op jit(solution)/shard_map/ppermute | solution.py:447
  9.0 1.5 %collective-permute-start.2 = (f32[28,8,128]{2,1,0:T(8,128)S(1)}, f32[28,8,128]{2,1,0:T(8,128)S(1)}, u32[]{:S(2)}, u32[]{:S(2)}) collective-permute-start(f32[28,8,128]{2,1,0:T(8,128)S(1)} %get-tuple-element.35), channel_id=1, source_target_pairs={{0,4},{1,5},{2,6},{3,7},{4,0},{5,1},{6,2},{7,3},{8,12},{9,13},{10,... | collective-permute-start | bytes 344072 | tf_op jit(solution)/shard_map/ppermute | solution.py:447
  10.6 0.0 collective-permute-start.3
  10.6 2.0 %collective-permute-start.4 = (f32[8,8,128]{2,1,0:T(8,128)S(1)}, f32[8,8,128]{2,1,0:T(8,128)S(1)}, u32[]{:S(2)}, u32[]{:S(2)}) collective-permute-start(f32[8,8,128]{2,1,0:T(8,128)S(1)} %get-tuple-element.37), channel_id=1, source_target_pairs={{0,0},{1,6},{2,5},{3,3},{4,4},{5,2},{6,1},{7,7},{8,8},{9,14},{10,1... | collective-permute-start | bytes 98312 | tf_op jit(solution)/shard_map/ppermute | solution.py:447
  12.6 3.0 %collective-permute-done.3.rest_3_ = f32[8,8,128]{2,1,0:T(8,128)S(1)} collective-permute-done((f32[8,8,128]{2,1,0:T(8,128)S(1)}, f32[8,8,128]{2,1,0:T(8,128)S(1)}, u32[]{:S(2)}, u32[]{:S(2)}) %collective-permute-start.3) | collective-permute-done | bytes 32800 | tf_op jit(solution)/shard_map/ppermute | solution.py:447
  15.5 1.7 %collective-permute-done.4.rest_4_ = f32[8,8,128]{2,1,0:T(8,128)S(1)} collective-permute-done((f32[8,8,128]{2,1,0:T(8,128)S(1)}, f32[8,8,128]{2,1,0:T(8,128)S(1)}, u32[]{:S(2)}, u32[]{:S(2)}) %collective-permute-start.4) | collective-permute-done | bytes 32800 | tf_op jit(solution)/shard_map/ppermute | solution.py:447
  17.3 0.0 collective-permute-done.2.rest_2_
  17.3 0.0 collective-permute-done.rest_0_
  17.3 0.0 collective-permute-done.1.rest_1_
  17.3 0.0 copy-done.1
  17.3 0.0 copy-done.3
  17.3 0.0 copy-done.4
  17.3 0.0 copy-done.5
  17.3 0.0 copy-start
  17.3 0.8 %first.1 = (f32[2,16,8,128]{3,2,1,0:T(8,128)S(1)}, f32[3,16,8,128]{3,2,1,0:T(8,128)S(1)}, f32[16,8,128]{2,1,0:T(8,128)S(1)}, f32[3,16,8,128]{3,2,1,0:T(8,128)S(1...) custom-call(f32[1,3,16,8,128]{4,3,2,1,0:T(8,128)S(1)} %copy-done.1, ...), custom_call_target="tpu_custom_call" | custom-call | tf_op jit(solution)/shard_map/first/pallas_call | solution.py:515
  18.1 0.0 copy-start.2
  18.1 0.0 copy-start.8
  18.1 0.1 collective-permute-start.5
  18.2 1.3 %collective-permute-done.5 = f32[2,16,8,128]{3,2,1,0:T(8,128)S(1)} collective-permute-done((f32[2,16,8,128]{3,2,1,0:T(8,128)S(1)}, f32[2,16,8,128]{3,2,1,0:T(8,128)S(1)}, u32[]{:S(2)}, u32[]{:S(2)}) %collective-permute-start.5) | collective-permute-done | bytes 131104 | tf_op jit(solution)/shard_map/ppermute | solution.py:456
  19.6 1.6 %collective-permute-start.6 = (f32[2,16,8,128]{3,2,1,0:T(8,128)S(1)}, f32[2,16,8,128]{3,2,1,0:T(8,128)S(1)}, u32[]{:S(2)}, u32[]{:S(2)}) collective-permute-start(f32[2,16,8,128]{3,2,1,0:T(8,128)S(1)} %add.6), channel_id=1, source_target_pairs={{0,16},{8,24},{16,0},{24,8},{1,17},{9,25},{17,1},{25,9},{2,18},{10... | collective-permute-start | bytes 393224 | tf_op jit(solution)/shard_map/ppermute | solution.py:456
  21.2 0.0 copy-done.8
  21.2 1.2 %last.1 = (f32[1,3,16,8,128]{4,3,2,1,0:T(8,128)}, f32[1,3,16,8,128]{4,3,2,1,0:T(8,128)}, f32[1,3,16,8,128]{4,3,2,1,0:T(8,128)}, f32[1,3,3,16,8,128]{5,4,3,2,1,0:T(8,128)}) custom-call(f32[1,3,16,8,128]{4,3,2,1,0:T(8,128)S(1)} %copy-done.1, f32[1,3,16,8,128]{4,3,2,1,0:T(8,128)S(1)} %copy-done.2, f32[1,3,3,16,8,128]{5,4,3,2,1,0:T(8,128)S(1)} %copy-done, ...), custom_call_target="tpu_custom_call" | custom-call | flops 3000000 | bytes 4000000 | tf_op jit(solution)/shard_map/last/pallas_call | solution.py:540
  22.4 2.8 %collective-permute-done.6 = f32[2,16,8,128]{3,2,1,0:T(8,128)S(1)} collective-permute-done((f32[2,16,8,128]{3,2,1,0:T(8,128)S(1)}, f32[2,16,8,128]{3,2,1,0:T(8,128)S(1)}, u32[]{:S(2)}, u32[]{:S(2)}) %collective-permute-start.6) | collective-permute-done | bytes 131104 | tf_op jit(solution)/shard_map/ppermute | solution.py:456
  25.2 0.7 %slice_bitcast_fusion = (f32[16,8,128]{2,1,0:T(8,128)}, f32[16,8,128]{2,1,0:T(8,128)}) fusion(f32[2,16,8,128]{3,2,1,0:T(8,128)S(1)} %add.7), kind=kLoop, calls=%fused_computation | loop fusion | bytes 262144 | tf_op jit(solution)/shard_map/squeeze | solution.py:552
  (6 shorter events, 0.0 us)
Async XLA Ops:
  1.9 15.3 %copy-start.1 = (f32[1,3,16,8,128]{4,3,2,1,0:T(8,128)S(1)}, f32[1,3,16,8,128]{4,3,2,1,0:T(8,128)}, u32[]{:S(2)}) copy-start(f32[1,3,16,8,128]{4,3,2,1,0:T(8,128)} %w_ref.3) | copy-start | bytes 589828
  1.9 15.3 %copy-start.3 = (f32[16,8,128]{2,1,0:T(8,128)S(1)}, f32[16,8,128]{2,1,0:T(8,128)}, u32[]{:S(2)}) copy-start(f32[16,8,128]{2,1,0:T(8,128)} %kappa_ref.3) | copy-start | bytes 196612
  1.9 15.3 %copy-start.4 = (f32[16,8,128]{2,1,0:T(8,128)S(1)}, f32[16,8,128]{2,1,0:T(8,128)}, u32[]{:S(2)}) copy-start(f32[16,8,128]{2,1,0:T(8,128)} %mu_ref.3) | copy-start | bytes 196612
  2.0 15.3 %copy-start.5 = (f32[16,8,128]{2,1,0:T(8,128)S(1)}, f32[16,8,128]{2,1,0:T(8,128)}, u32[]{:S(2)}) copy-start(f32[16,8,128]{2,1,0:T(8,128)} %buoy_ref.3) | copy-start | bytes 196612
  2.0 15.3 %copy-start.6 = (f32[16,8,128]{2,1,0:T(8,128)S(1)}, f32[16,8,128]{2,1,0:T(8,128)}, u32[]{:S(2)}) copy-start(f32[16,8,128]{2,1,0:T(8,128)} %bat_ref.1) | copy-start | bytes 196612
  2.0 15.3 %copy-start.7 = (f32[1,2,4,16,8,128]{5,4,3,2,1,0:T(8,128)S(1)}, f32[1,2,4,16,8,128]{5,4,3,2,1,0:T(8,128)}, u32[]{:S(2)}) copy-start(f32[1,2,4,16,8,128]{5,4,3,2,1,0:T(8,128)} %strain_ref.1) | copy-start | bytes 1572868
  3.9 13.4 %collective-permute-start = (f32[4,16,8,128]{3,2,1,0:T(8,128)S(1)}, f32[4,16,8,128]{3,2,1,0:T(8,128)S(1)}, u32[]{:S(2)}, u32[]{:S(2)}) collective-permute-start(f32[4,16,8,128]{3,2,1,0:T(8,128)S(1)} %get-tuple-element.33), channel_id=1, source_target_pairs={{0,1},{1,0},{2,3},{3,2},{4,5},{5,4},{6,7},{7,6},{8,9},{9,8},{10,11... | collective-permute-start | bytes 786440 | tf_op jit(solution)/shard_map/ppermute | solution.py:447
  4.0 13.3 %collective-permute-start.1 = (f32[4,16,8,128]{3,2,1,0:T(8,128)S(1)}, f32[4,16,8,128]{3,2,1,0:T(8,128)S(1)}, u32[]{:S(2)}, u32[]{:S(2)}) collective-permute-start(f32[4,16,8,128]{3,2,1,0:T(8,128)S(1)} %get-tuple-element.34), channel_id=1, source_target_pairs={{0,0},{1,2},{2,1},{3,3},{4,4},{5,6},{6,5},{7,7},{8,8},{9,10},{10,9... | collective-permute-start | bytes 786440 | tf_op jit(solution)/shard_map/ppermute | solution.py:447
  9.0 8.2 %collective-permute-start.2 = (f32[28,8,128]{2,1,0:T(8,128)S(1)}, f32[28,8,128]{2,1,0:T(8,128)S(1)}, u32[]{:S(2)}, u32[]{:S(2)}) collective-permute-start(f32[28,8,128]{2,1,0:T(8,128)S(1)} %get-tuple-element.35), channel_id=1, source_target_pairs={{0,4},{1,5},{2,6},{3,7},{4,0},{5,1},{6,2},{7,3},{8,12},{9,13},{10,... | collective-permute-start | bytes 344072 | tf_op jit(solution)/shard_map/ppermute | solution.py:447
  10.6 5.0 %collective-permute-start.3 = (f32[8,8,128]{2,1,0:T(8,128)S(1)}, f32[8,8,128]{2,1,0:T(8,128)S(1)}, u32[]{:S(2)}, u32[]{:S(2)}) collective-permute-start(f32[8,8,128]{2,1,0:T(8,128)S(1)} %get-tuple-element.36), channel_id=1, source_target_pairs={{0,5},{1,4},{2,7},{3,6},{4,1},{5,0},{6,3},{7,2},{8,13},{9,12},{10,... | collective-permute-start | bytes 98312 | tf_op jit(solution)/shard_map/ppermute | solution.py:447
  10.6 6.7 %collective-permute-start.4 = (f32[8,8,128]{2,1,0:T(8,128)S(1)}, f32[8,8,128]{2,1,0:T(8,128)S(1)}, u32[]{:S(2)}, u32[]{:S(2)}) collective-permute-start(f32[8,8,128]{2,1,0:T(8,128)S(1)} %get-tuple-element.37), channel_id=1, source_target_pairs={{0,0},{1,6},{2,5},{3,3},{4,4},{5,2},{6,1},{7,7},{8,8},{9,14},{10,1... | collective-permute-start | bytes 98312 | tf_op jit(solution)/shard_map/ppermute | solution.py:447
  17.3 3.8 %copy-start = (f32[1,3,3,16,8,128]{5,4,3,2,1,0:T(8,128)S(1)}, f32[1,3,3,16,8,128]{5,4,3,2,1,0:T(8,128)}, u32[]{:S(2)}) copy-start(f32[1,3,3,16,8,128]{5,4,3,2,1,0:T(8,128)} %sm_ref.1) | copy-start | bytes 1769476
  18.1 3.0 %copy-start.2 = (f32[1,3,16,8,128]{4,3,2,1,0:T(8,128)S(1)}, f32[1,3,16,8,128]{4,3,2,1,0:T(8,128)}, u32[]{:S(2)}) copy-start(f32[1,3,16,8,128]{4,3,2,1,0:T(8,128)} %bm_ref.1) | copy-start | bytes 589828
  18.1 3.0 %copy-start.8 = (f32[16,8,128]{2,1,0:T(8,128)S(1)}, f32[16,8,128]{2,1,0:T(8,128)}, u32[]{:S(2)}) copy-start(f32[16,8,128]{2,1,0:T(8,128)} %sat_ref.1) | copy-start | bytes 196612
  18.1 1.4 %collective-permute-start.5 = (f32[2,16,8,128]{3,2,1,0:T(8,128)S(1)}, f32[2,16,8,128]{3,2,1,0:T(8,128)S(1)}, u32[]{:S(2)}, u32[]{:S(2)}) collective-permute-start(f32[2,16,8,128]{3,2,1,0:T(8,128)S(1)} %get-tuple-element.49), channel_id=1, source_target_pairs={{0,8},{8,0},{16,24},{24,16},{1,9},{9,1},{17,25},{25,17},{2,10},{10... | collective-permute-start | bytes 393224 | tf_op jit(solution)/shard_map/ppermute | solution.py:456
  19.6 5.6 %collective-permute-start.6 = (f32[2,16,8,128]{3,2,1,0:T(8,128)S(1)}, f32[2,16,8,128]{3,2,1,0:T(8,128)S(1)}, u32[]{:S(2)}, u32[]{:S(2)}) collective-permute-start(f32[2,16,8,128]{3,2,1,0:T(8,128)S(1)} %add.6), channel_id=1, source_target_pairs={{0,16},{8,24},{16,0},{24,8},{1,17},{9,25},{17,1},{25,9},{2,18},{10... | collective-permute-start | bytes 393224 | tf_op jit(solution)/shard_map/ppermute | solution.py:456

commit v4 on v3

--- a/solution.py
+++ b/solution.py
@@ -20,10 +20,10 @@
     + [(f"base{c}", d) for c in range(3) for d in (1, 2)]
     + [("bb", d) for d in (1, 2)]
     + [("bbmu", d) for d in (1, 2)]
-    + [("z1", 1), ("atten", 1)]
+    + [("z1", 1), ("atten", 1), ("mask", 1), ("mask", 2)]
 )
 X_AT = {key: at for at, key in enumerate(X_LIST)}
-PACK_ARGS = 15
+PACK_ARGS = 14
 D_LIST = [(t, 1) for t in range(4)] + [(t, 2) for t in range(3)] + [(0, 3)]
 
 
@@ -68,16 +68,16 @@
     return decay, gain
 
 
-def wave_phase(slow_ref, onset_ref, counts):
+def wave_phase(slow, onset_ref, counts, y):
     nx, ny, cx = counts
     i, j = lax.axis_index("gx"), lax.axis_index("gy")
-    py = (j * TILE[0] + row_of()).astype(jnp.float32) / float(ny * TILE[0])
+    py = (j * TILE[0] + y).astype(jnp.float32) / float(ny * TILE[0])
     pz = lane_of().astype(jnp.float32) / float(TILE[1])
-    common = slow_ref[0, 1] * py + slow_ref[0, 2] * pz + onset_ref[0]
+    common = slow[1] * py + slow[2] * pz + onset_ref[0]
 
     def at(x):
         px = jnp.full(TILE, i * cx + x, jnp.int32).astype(jnp.float32) / float(nx * cx)
-        return slow_ref[0, 0] * px + common
+        return slow[0] * px + common
 
     return at
 
@@ -91,7 +91,7 @@
     counts, np_, *refs,
 ):
     nx, ny, cx = counts
-    count_ref, onset_ref, given, rest = refs[0], refs[1], refs[2:PACK_ARGS], refs[PACK_ARGS:]
+    count_ref, given, rest = refs[0], refs[1:PACK_ARGS], refs[PACK_ARGS:]
     outs, held, sems = rest[: 7 + 3 * np_], rest[7 + 3 * np_ : -1], rest[-1]
     copies = [pltpu.make_async_copy(a, b, sems.at[k]) for k, (a, b) in enumerate(zip(given, held))]
     for copy in copies:
@@ -101,7 +101,7 @@
     y_refs = outs[:2]
     x_refs = outs[2 : 2 + np_]
     d_refs = outs[2 + np_ : 2 + 3 * np_]
-    pulse_ref, coef_ref, base_ref, zsum_ref, z1_ref = outs[2 + 3 * np_ :]
+    mask_ref, coef_ref, base_ref, zsum_ref, z1_ref = outs[2 + 3 * np_ :]
     i, j = lax.axis_index("gx"), lax.axis_index("gy")
     rows = cx * TILE[0]
     slots = cells_ref.shape[2]
@@ -118,7 +118,7 @@
     mask = lax.dot_general(
         hot_row, hot_lane, (((1,), (1,)), ((), ())), preferred_element_type=jnp.float32
     )
-    mask = mask.reshape(cx, TILE[0], TILE[1])
+    mask_ref[...] = mask.reshape(cx, TILE[0], TILE[1])
 
     for copy in copies[1:]:
         copy.wait()
@@ -127,7 +127,7 @@
         coef_ref[l] = decay[l]
         coef_ref[3 + l] = gain[l]
         coef_ref[6 + l] = jnp.full(TILE, amp_ref[0, l], jnp.float32)
-    phase = wave_phase(slow_ref, onset_ref, counts)
+        coef_ref[9 + l] = jnp.full(TILE, slow_ref[0, l], jnp.float32)
     row = row_of()
     keep = ((row >> 2) ^ (j & 1)) == 1
     two_three = (row == 2) | (row == 3)
@@ -136,6 +136,11 @@
     def pair(first, second):
         return jnp.where(
             two_three, roll(second, 2, 0), jnp.where(four_five, roll(second, -2, 0), first)
+        )
+
+    def spare(field, live, shift):
+        return jnp.where(
+            row == 3, roll(live, shift, 0), jnp.where(row == 4, roll(live, -shift, 0), field)
         )
 
     for x in range(cx):
@@ -143,12 +148,11 @@
         kappa, mu, atten = kappa_ref[x], mu_ref[x], at_ref[x]
         bb = DT2 * buoy_ref[x]
         bbmu = bb * mu
-        pulse = pulse_of(-phase(x)) * mask[x]
-        pulse_ref[x] = pulse_of(TIME_STEP - phase(x)) * mask[x]
+        live = mask_ref[x]
         base = []
         for c in range(3):
             total = sm_ref[0, 0, c, x] + sm_ref[0, 1, c, x] + sm_ref[0, 2, c, x]
-            value = 2.0 * w[c] - v_ref[0, c, x] + bb * (amp_ref[0, c] * pulse - total)
+            value = 2.0 * w[c] - v_ref[0, c, x] - bb * total
             base_ref[c, x] = value
             base.append(value)
         bm = [bm_ref[0, l, x] for l in range(3)]
@@ -166,8 +170,8 @@
             ),
         )
         tiles = [
-            (w[0], w[1]),
-            (w[2], kappa),
+            (spare(w[0], live, 3), w[1]),
+            (w[2], spare(kappa, live, 2)),
             (zsum, third),
             (pair(base[0], base[1]), pair(base[2], bb)),
         ]
@@ -189,6 +193,8 @@
                 value = z1_ref[x]
             elif name == "atten":
                 value = at_ref[x]
+            elif name == "mask":
+                value = mask_ref[x]
             elif name == "bb":
                 value = DT2 * buoy_ref[x]
             elif name == "bbmu":
@@ -203,7 +209,7 @@
 
 
 def first_kernel(
-    counts, np_, w_ref, kappa_ref, mu_ref, buoy_ref, at_ref, strain_ref, coef_ref, base_ref, zsum_ref,
+    counts, np_, w_ref, kappa_ref, mu_ref, buoy_ref, at_ref, strain_ref, onset_ref, coef_ref, mask_ref, base_ref, zsum_ref,
     z1_ref, *rest,
 ):
     nx, ny, cx = counts
@@ -248,9 +254,14 @@
         if t == 0:
             put(("wx", x), a)
             put(("wy", x), b)
+            if -2 < x < cx + 1:
+                put(("mask", x), jnp.where((row == 0) | (row == 7), second(a, 3, 3), 0.0))
         elif t == 1:
             put(("wz", x), a)
             put(("kappa", x), b)
+            if -2 < x < cx + 1:
+                live = jnp.where((row == 1) | (row == 6), second(b, 2, 2), halo("mask", x))
+                put(("mask", x), live)
         elif t == 2:
             put(("zsum", x), a)
             if -2 < x < cx + 1:
@@ -264,7 +275,7 @@
             put(("base2", x), b)
             put(("bb", x), second(b, 2, 2))
 
-    names = ["wx", "wy", "wz", "kappa", "zsum", "bbmu", "z1", "atten", "base0", "base1", "base2", "bb"]
+    names = ["wx", "wy", "wz", "kappa", "zsum", "bbmu", "z1", "atten", "base0", "base1", "base2", "bb", "mask"]
 
     def put(key, value):
         halo_ref[names.index(key[0]), 3 + key[1]] = value
@@ -296,6 +307,8 @@
             return z1_ref[x]
         if name == "atten":
             return at_ref[x]
+        if name == "mask":
+            return mask_ref[x]
         if name == "bb":
             return DT2 * buoy_ref[x]
         if name == "bbmu":
@@ -340,7 +353,13 @@
         lh = get_h(c, x + 1) + get_h(c, x - 1) + (up[1] + down[1]) + (zplus(h) + zminus(h)) - 6.0 * h
         return lb, lh
 
+    amp = [coef_ref[6 + c] for c in range(3)]
+    slow = [coef_ref[9 + c] for c in range(3)]
+    phase_b = wave_phase(slow, onset_ref, counts, row)
+    phase_h = wave_phase(slow, onset_ref, counts, jnp.where(row < 4, row + TILE[0], row - TILE[0]))
+
     for x in range(-2, cx + 2):
+        pulse_b = pulse_of(-phase_b(x)) * block("mask", x)
         near = -2 < x < cx + 1
         inside = 0 <= x < cx
         bb, bbmu = block("bb", x), block("bbmu", x)
@@ -349,19 +368,20 @@
             up, down = yplus(pb, ph), yminus(pb, ph)
             grad_b = [0.5 * (p0b[4 + x] - p0b[2 + x]), 0.5 * (up[0] - down[0]), 0.5 * (zplus(pb) - zminus(pb))]
             grad_h = [0.5 * (p0h[3 + x] - p0h[1 + x]), 0.5 * (up[1] - down[1]), 0.5 * (zplus(ph) - zminus(ph))]
+            pulse_h = pulse_of(-phase_h(x)) * halo("mask", x)
             hbb, hbbmu = halo("bb", x), halo("bbmu", x)
         else:
             grad_b = [0.5 * (p0b[4 + x] - p0b[2 + x])]
         for c in range(3 if near else 1):
             with_halo = inside or (near and c < 2)
             lb, lh = lap(w_b, w_h, c, x, with_halo)
-            value = block(f"base{c}", x) + bb * grad_b[c] + bbmu * lb
+            value = block(f"base{c}", x) + bb * (grad_b[c] + amp[c] * pulse_b) + bbmu * lb
             w1b[c, 2 + x] = value
             if inside:
                 l0_ref[c, x] = lb
                 w1_ref[c, x] = value
             if with_halo:
-                w1h[c, 1 + x] = halo(f"base{c}", x) + hbb * grad_h[c] + hbbmu * lh
+                w1h[c, 1 + x] = halo(f"base{c}", x) + hbb * (grad_h[c] + amp[c] * pulse_h) + hbbmu * lh
 
     def w1_b(c, x):
         return w1b[c, 2 + x]
@@ -395,10 +415,11 @@
 
 
 def last_kernel(
-    counts, w_ref, bm_ref, sm_ref, kappa_ref, mu_ref, buoy_ref, bat_ref, sat_ref, coef_ref, pulse_ref, w1_ref, d0_ref, l0_ref, d1_ref, l1_ref, pb_ref, ph_ref, w2_ref, before_ref, bn_ref, sn_ref,
+    counts, w_ref, bm_ref, sm_ref, kappa_ref, mu_ref, buoy_ref, bat_ref, sat_ref, onset_ref, coef_ref, mask_ref, w1_ref, d0_ref, l0_ref, d1_ref, l1_ref, pb_ref, ph_ref, w2_ref, before_ref, bn_ref, sn_ref,
 ):
     nx, ny, cx = counts
-    decay, gain, amp = ([coef_ref[3 * k + l] for l in range(3)] for k in range(3))
+    decay, gain, amp, slow = ([coef_ref[3 * k + l] for l in range(3)] for k in range(4))
+    phase = wave_phase(slow, onset_ref, counts, row_of())
     for x in range(cx):
         bulk = bat_ref[x] * kappa_ref[x]
         q0, q1 = bulk * d0_ref[x], bulk * d1_ref[x]
@@ -415,7 +436,7 @@
         ]
         mu = mu_ref[x]
         shear = sat_ref[x] * mu
-        pulse = pulse_ref[x]
+        pulse = pulse_of(TIME_STEP - phase(x)) * mask_ref[x]
         bb = DT2 * buoy_ref[x]
         for c in range(3):
             l1 = l1_ref[c, x]
@@ -462,6 +483,10 @@
     return pl.BlockSpec(memory_space=pltpu.VMEM)
 
 
+def smem():
+    return pl.BlockSpec(memory_space=pltpu.SMEM)
+
+
 def body(
     adjoint_now, adjoint_old, bulk_memory, shear_memory, forward_strain, bulk_modulus, shear_modulus, buoyancy,
     bulk_atten, shear_atten, relax_time, mechanism_weight, event_slowness, event_amplitude, event_onset,
@@ -478,7 +503,7 @@
 
     params = pltpu.CompilerParams(vmem_limit_bytes=24 * 1024 * 1024)
     pack_args = (
-        boundary_count, event_onset, boundary_cells, relax_time, mechanism_weight, event_slowness, event_amplitude,
+        boundary_count, boundary_cells, relax_time, mechanism_weight, event_slowness, event_amplitude,
         buoyancy, shear_modulus, bulk_modulus, bulk_atten, adjoint_now, adjoint_old, bulk_memory, shear_memory,
     )
     packed = pl.pallas_call(
@@ -486,16 +511,16 @@
         out_shape=[field(4, cx)] * 2
         + [field(len(X_LIST))] * np_
         + [field(len(D_LIST))] * (2 * np_)
-        + [field(cx), field(9), field(3, cx), field(cx), field(cx)],
+        + [field(cx), field(12), field(3, cx), field(cx), field(cx)],
         in_specs=[
             pl.BlockSpec(memory_space=pltpu.HBM if given.size > 1 else pltpu.SMEM) for given in pack_args
         ],
         out_specs=[vmem()] * (2 + 3 * np_ + 5),
         scratch_shapes=[
             (pltpu.SMEM if k in (1, 2, 3, 4) else pltpu.VMEM)(given.shape, given.dtype)
-            for k, given in enumerate(pack_args[2:])
+            for k, given in enumerate(pack_args[1:])
         ]
-        + [pltpu.SemaphoreType.DMA((PACK_ARGS - 2,))],
+        + [pltpu.SemaphoreType.DMA((PACK_ARGS - 1,))],
         compiler_params=params,
         name="pack",
     )(
@@ -510,18 +535,18 @@
     ds = [
         matched(packed[2 + np_ + 2 * p + q], shape, True, True, p, q) for p in range(np_) for q in range(2)
     ]
-    pulse, coef, base, zsum, z1 = packed[2 + 3 * np_ :]
+    mask, coef, base, zsum, z1 = packed[2 + 3 * np_ :]
 
     first = pl.pallas_call(
         functools.partial(first_kernel, counts, np_),
         out_shape=[
             field(2, cx), field(3, cx), field(cx), field(3, cx), field(cx), field(3, cx), field(cx + 2), field(cx),
         ],
-        in_specs=[vmem()] * (12 + 3 * np_),
+        in_specs=[vmem()] * 6 + [smem()] + [vmem()] * (7 + 3 * np_),
         out_specs=[vmem()] * 8,
         scratch_shapes=[
             pltpu.VMEM((2 * len(X_LIST), *TILE), f32),
-            pltpu.VMEM((12, cx + 6, *TILE), f32),
+            pltpu.VMEM((13, cx + 6, *TILE), f32),
             pltpu.VMEM((cx + 6, *TILE), f32),
             pltpu.VMEM((cx + 4, *TILE), f32),
             pltpu.VMEM((cx + 2, *TILE), f32),
@@ -532,7 +557,7 @@
         compiler_params=params,
         name="first",
     )(
-        adjoint_now, bulk_modulus, shear_modulus, buoyancy, bulk_atten, forward_strain, coef, base, zsum, z1, *ys, *xs, *ds,
+        adjoint_now, bulk_modulus, shear_modulus, buoyancy, bulk_atten, forward_strain, event_onset, coef, mask, base, zsum, z1, *ys, *xs, *ds,
     )
     term, w1, d0, l0, d1, l1, pb, ph = first
     total = event_sum(term)
@@ -540,14 +565,14 @@
     w2, before, bulk_next, shear_next = pl.pallas_call(
         functools.partial(last_kernel, counts),
         out_shape=[field(1, 3, cx), field(1, 3, cx), field(1, 3, cx), field(1, 3, 3, cx)],
-        in_specs=[vmem()] * 17,
+        in_specs=[vmem()] * 8 + [smem()] + [vmem()] * 9,
         out_specs=[vmem()] * 4,
         compiler_params=params,
         cost_estimate=pl.CostEstimate(flops=3_000_000, bytes_accessed=4_000_000, transcendentals=0),
         name="last",
     )(
         adjoint_now, bulk_memory, shear_memory, bulk_modulus, shear_modulus, buoyancy, bulk_atten, shear_atten,
-        coef, pulse, w1, d0, l0, d1, l1, pb, ph,
+        event_onset, coef, mask, w1, d0, l0, d1, l1, pb, ph,
     )
     return w2, before, bulk_next, shear_next, total[0], total[1]
 

time: 26.1 us -> 25.5 us (0.977)
  waiting for transfers between devices: 8.85 us -> 8.18 us
    ppermute x5, waiting for transfers between devices: 4.68 us -> 4.04 us  [matched(): return lax.ppermute(value, ('gx', 'gy'), pairs)]
where the time goes in v4:
time: 25.5 us; the launch traced here: 25.3 us
  starting transfers between devices  10.3 us (40%)
  waiting for transfers between devices  8.18 us (32%)
  Pallas kernels  3.92 us (15%)
  between operations  2.11 us (8%)
  local copies, waits for them, and re-layouts  0.7 us (3%)
    ppermute x5, starting transfers between devices, matched(): return lax.ppermute(value, ('gx', 'gy'), pairs)  8.67 us
    ppermute x2, waiting for transfers between devices, event_sum(): lax.ppermute(value, 'event', [(e, e ^ step) for e in range(count)])  4.14 us
    ppermute x5, waiting for transfers between devices, matched(): return lax.ppermute(value, ('gx', 'gy'), pairs)  4.04 us
    pallas_call x1, Pallas kernels, body(): pl.pallas_call(functools.partial(pack_kernel, counts, np_), out_shape=[fi...  1.84 us
    ppermute x2, starting transfers between devices, event_sum(): lax.ppermute(value, 'event', [(e, e ^ step) for e in range(count)])  1.66 us
    pallas_call x1, Pallas kernels, body(): pl.pallas_call(functools.partial(last_kernel, counts), out_shape=[field(1...  1.22 us
    pallas_call x1, Pallas kernels, body(): pl.pallas_call(functools.partial(first_kernel, counts, np_), out_shape=[f...  0.86 us
    squeeze x1, local copies, waits for them, and re-layouts, body(): return (w2, before, bulk_next, shear_next, total[0], total[1])  0.66 us
  transfers between devices with their start and end apart: 7, of which 4 were waited for; matrix products, arithmetic and copies ran while one was open for 0% of the time, Pallas kernels for 5%

profile of v4, /device:TPU:8, one launch (start us, length us, event | category | flops | bytes accessed | tf_op | source)
XLA Modules:
  0.0 25.3 jit_solution(12312908657572256904)
XLA Ops:
  1.3 0.0 copy-start.1
  1.3 0.0 copy-start.3
  1.3 0.0 copy-start.4
  1.3 0.0 copy-start.5
  1.3 0.0 copy-start.6
  1.3 0.0 copy-start.7
  1.3 1.8 %pack.1 = (f32[4,16,8,128]{3,2,1,0:T(8,128)S(1)}, f32[4,16,8,128]{3,2,1,0:T(8,128)S(1)}, f32[30,8,128]{2,1,0:T(8,128)S(1)}, f32[8,8,128]{2,1,0:T(8,128)S(1)}, f3...) custom-call(s32[1,1]{1,0:T(1,128)S(6)} %copy.24.refs_0_, ...), custom_call_target="tpu_custom_call" | custom-call | tf_op jit(solution)/shard_map/pack/pallas_call | solution.py:509
  3.2 0.1 collective-permute-start
  3.3 5.0 %collective-permute-start.1 = (f32[4,16,8,128]{3,2,1,0:T(8,128)S(1)}, f32[4,16,8,128]{3,2,1,0:T(8,128)S(1)}, u32[]{:S(2)}, u32[]{:S(2)}) collective-permute-start(f32[4,16,8,128]{3,2,1,0:T(8,128)S(1)} %get-tuple-element.34), channel_id=1, source_target_pairs={{0,0},{1,2},{2,1},{3,3},{4,4},{5,6},{6,5},{7,7},{8,8},{9,10},{10,9... | collective-permute-start | bytes 786440 | tf_op jit(solution)/shard_map/ppermute | solution.py:468
  8.3 1.6 %collective-permute-start.2 = (f32[30,8,128]{2,1,0:T(8,128)S(1)}, f32[30,8,128]{2,1,0:T(8,128)S(1)}, u32[]{:S(2)}, u32[]{:S(2)}) collective-permute-start(f32[30,8,128]{2,1,0:T(8,128)S(1)} %get-tuple-element.35), channel_id=1, source_target_pairs={{0,4},{1,5},{2,6},{3,7},{4,0},{5,1},{6,2},{7,3},{8,12},{9,13},{10,... | collective-permute-start | bytes 368648 | tf_op jit(solution)/shard_map/ppermute | solution.py:468
  9.9 0.0 collective-permute-start.3
  9.9 2.0 %collective-permute-start.4 = (f32[8,8,128]{2,1,0:T(8,128)S(1)}, f32[8,8,128]{2,1,0:T(8,128)S(1)}, u32[]{:S(2)}, u32[]{:S(2)}) collective-permute-start(f32[8,8,128]{2,1,0:T(8,128)S(1)} %get-tuple-element.37), channel_id=1, source_target_pairs={{0,0},{1,6},{2,5},{3,3},{4,4},{5,2},{6,1},{7,7},{8,8},{9,14},{10,1... | collective-permute-start | bytes 98312 | tf_op jit(solution)/shard_map/ppermute | solution.py:468
  12.5 2.3 %collective-permute-done.3.rest_3_ = f32[8,8,128]{2,1,0:T(8,128)S(1)} collective-permute-done((f32[8,8,128]{2,1,0:T(8,128)S(1)}, f32[8,8,128]{2,1,0:T(8,128)S(1)}, u32[]{:S(2)}, u32[]{:S(2)}) %collective-permute-start.3) | collective-permute-done | bytes 32800 | tf_op jit(solution)/shard_map/ppermute | solution.py:468
  14.9 1.7 %collective-permute-done.4.rest_4_ = f32[8,8,128]{2,1,0:T(8,128)S(1)} collective-permute-done((f32[8,8,128]{2,1,0:T(8,128)S(1)}, f32[8,8,128]{2,1,0:T(8,128)S(1)}, u32[]{:S(2)}, u32[]{:S(2)}) %collective-permute-start.4) | collective-permute-done | bytes 32800 | tf_op jit(solution)/shard_map/ppermute | solution.py:468
  16.6 0.0 collective-permute-done.2.rest_2_
  16.6 0.0 collective-permute-done.rest_0_
  16.6 0.0 collective-permute-done.1.rest_1_
  16.6 0.0 copy-done.1
  16.6 0.0 copy-done.3
  16.6 0.0 copy-done.4
  16.6 0.0 copy-start
  16.6 0.9 %first.1 = (f32[2,16,8,128]{3,2,1,0:T(8,128)S(1)}, f32[3,16,8,128]{3,2,1,0:T(8,128)S(1)}, f32[16,8,128]{2,1,0:T(8,128)S(1)}, f32[3,16,8,128]{3,2,1,0:T(8,128)S(1...) custom-call(f32[1,3,16,8,128]{4,3,2,1,0:T(8,128)S(1)} %copy-done.1, ...), custom_call_target="tpu_custom_call" | custom-call | tf_op jit(solution)/shard_map/first/pallas_call | solution.py:540
  17.5 0.0 copy-start.2
  17.5 0.0 copy-start.8
  17.5 0.1 collective-permute-start.5
  17.6 1.3 %collective-permute-done.5 = f32[2,16,8,128]{3,2,1,0:T(8,128)S(1)} collective-permute-done((f32[2,16,8,128]{3,2,1,0:T(8,128)S(1)}, f32[2,16,8,128]{3,2,1,0:T(8,128)S(1)}, u32[]{:S(2)}, u32[]{:S(2)}) %collective-permute-start.5) | collective-permute-done | bytes 131104 | tf_op jit(solution)/shard_map/ppermute | solution.py:477
  19.0 1.6 %collective-permute-start.6 = (f32[2,16,8,128]{3,2,1,0:T(8,128)S(1)}, f32[2,16,8,128]{3,2,1,0:T(8,128)S(1)}, u32[]{:S(2)}, u32[]{:S(2)}) collective-permute-start(f32[2,16,8,128]{3,2,1,0:T(8,128)S(1)} %add.6), channel_id=1, source_target_pairs={{0,16},{8,24},{16,0},{24,8},{1,17},{9,25},{17,1},{25,9},{2,18},{10... | collective-permute-start | bytes 393224 | tf_op jit(solution)/shard_map/ppermute | solution.py:477
  20.6 0.0 copy-done
  20.6 0.0 copy-done.8
  20.6 1.2 %last.1 = (f32[1,3,16,8,128]{4,3,2,1,0:T(8,128)}, f32[1,3,16,8,128]{4,3,2,1,0:T(8,128)}, f32[1,3,16,8,128]{4,3,2,1,0:T(8,128)}, f32[1,3,3,16,8,128]{5,4,3,2,1,0:T(8,128)}) custom-call(f32[1,3,16,8,128]{4,3,2,1,0:T(8,128)S(1)} %copy-done.1, f32[1,3,16,8,128]{4,3,2,1,0:T(8,128)S(1)} %copy-done.2, f32[1,3,3,16,8,128]{5,4,3,2,1,0:T(8,128)S(1)} %copy-done, ...), custom_call_target="tpu_custom_call" | custom-call | flops 3000000 | bytes 4000000 | tf_op jit(solution)/shard_map/last/pallas_call | solution.py:565
  21.8 2.8 %collective-permute-done.6 = f32[2,16,8,128]{3,2,1,0:T(8,128)S(1)} collective-permute-done((f32[2,16,8,128]{3,2,1,0:T(8,128)S(1)}, f32[2,16,8,128]{3,2,1,0:T(8,128)S(1)}, u32[]{:S(2)}, u32[]{:S(2)}) %collective-permute-start.6) | collective-permute-done | bytes 131104 | tf_op jit(solution)/shard_map/ppermute | solution.py:477
  24.6 0.7 %slice_bitcast_fusion = (f32[16,8,128]{2,1,0:T(8,128)}, f32[16,8,128]{2,1,0:T(8,128)}) fusion(f32[2,16,8,128]{3,2,1,0:T(8,128)S(1)} %add.7), kind=kLoop, calls=%fused_computation | loop fusion | bytes 262144 | tf_op jit(solution)/shard_map/squeeze | solution.py:577
  (6 shorter events, 0.0 us)
Async XLA Ops:
  1.3 15.3 %copy-start.1 = (f32[1,3,16,8,128]{4,3,2,1,0:T(8,128)S(1)}, f32[1,3,16,8,128]{4,3,2,1,0:T(8,128)}, u32[]{:S(2)}) copy-start(f32[1,3,16,8,128]{4,3,2,1,0:T(8,128)} %w_ref.3) | copy-start | bytes 589828
  1.3 15.3 %copy-start.3 = (f32[16,8,128]{2,1,0:T(8,128)S(1)}, f32[16,8,128]{2,1,0:T(8,128)}, u32[]{:S(2)}) copy-start(f32[16,8,128]{2,1,0:T(8,128)} %kappa_ref.3) | copy-start | bytes 196612
  1.3 15.3 %copy-start.4 = (f32[16,8,128]{2,1,0:T(8,128)S(1)}, f32[16,8,128]{2,1,0:T(8,128)}, u32[]{:S(2)}) copy-start(f32[16,8,128]{2,1,0:T(8,128)} %mu_ref.3) | copy-start | bytes 196612
  1.3 15.3 %copy-start.5 = (f32[16,8,128]{2,1,0:T(8,128)S(1)}, f32[16,8,128]{2,1,0:T(8,128)}, u32[]{:S(2)}) copy-start(f32[16,8,128]{2,1,0:T(8,128)} %buoy_ref.3) | copy-start | bytes 196612
  1.3 15.3 %copy-start.6 = (f32[16,8,128]{2,1,0:T(8,128)S(1)}, f32[16,8,128]{2,1,0:T(8,128)}, u32[]{:S(2)}) copy-start(f32[16,8,128]{2,1,0:T(8,128)} %bat_ref.1) | copy-start | bytes 196612
  1.3 15.3 %copy-start.7 = (f32[1,2,4,16,8,128]{5,4,3,2,1,0:T(8,128)S(1)}, f32[1,2,4,16,8,128]{5,4,3,2,1,0:T(8,128)}, u32[]{:S(2)}) copy-start(f32[1,2,4,16,8,128]{5,4,3,2,1,0:T(8,128)} %strain_ref.1) | copy-start | bytes 1572868
  3.2 13.4 %collective-permute-start = (f32[4,16,8,128]{3,2,1,0:T(8,128)S(1)}, f32[4,16,8,128]{3,2,1,0:T(8,128)S(1)}, u32[]{:S(2)}, u32[]{:S(2)}) collective-permute-start(f32[4,16,8,128]{3,2,1,0:T(8,128)S(1)} %get-tuple-element.33), channel_id=1, source_target_pairs={{0,1},{1,0},{2,3},{3,2},{4,5},{5,4},{6,7},{7,6},{8,9},{9,8},{10,11... | collective-permute-start | bytes 786440 | tf_op jit(solution)/shard_map/ppermute | solution.py:468
  3.3 13.3 %collective-permute-start.1 = (f32[4,16,8,128]{3,2,1,0:T(8,128)S(1)}, f32[4,16,8,128]{3,2,1,0:T(8,128)S(1)}, u32[]{:S(2)}, u32[]{:S(2)}) collective-permute-start(f32[4,16,8,128]{3,2,1,0:T(8,128)S(1)} %get-tuple-element.34), channel_id=1, source_target_pairs={{0,0},{1,2},{2,1},{3,3},{4,4},{5,6},{6,5},{7,7},{8,8},{9,10},{10,9... | collective-permute-start | bytes 786440 | tf_op jit(solution)/shard_map/ppermute | solution.py:468
  8.3 8.3 %collective-permute-start.2 = (f32[30,8,128]{2,1,0:T(8,128)S(1)}, f32[30,8,128]{2,1,0:T(8,128)S(1)}, u32[]{:S(2)}, u32[]{:S(2)}) collective-permute-start(f32[30,8,128]{2,1,0:T(8,128)S(1)} %get-tuple-element.35), channel_id=1, source_target_pairs={{0,4},{1,5},{2,6},{3,7},{4,0},{5,1},{6,2},{7,3},{8,12},{9,13},{10,... | collective-permute-start | bytes 368648 | tf_op jit(solution)/shard_map/ppermute | solution.py:468
  9.9 5.0 %collective-permute-start.3 = (f32[8,8,128]{2,1,0:T(8,128)S(1)}, f32[8,8,128]{2,1,0:T(8,128)S(1)}, u32[]{:S(2)}, u32[]{:S(2)}) collective-permute-start(f32[8,8,128]{2,1,0:T(8,128)S(1)} %get-tuple-element.36), channel_id=1, source_target_pairs={{0,5},{1,4},{2,7},{3,6},{4,1},{5,0},{6,3},{7,2},{8,13},{9,12},{10,... | collective-permute-start | bytes 98312 | tf_op jit(solution)/shard_map/ppermute | solution.py:468
  9.9 6.7 %collective-permute-start.4 = (f32[8,8,128]{2,1,0:T(8,128)S(1)}, f32[8,8,128]{2,1,0:T(8,128)S(1)}, u32[]{:S(2)}, u32[]{:S(2)}) collective-permute-start(f32[8,8,128]{2,1,0:T(8,128)S(1)} %get-tuple-element.37), channel_id=1, source_target_pairs={{0,0},{1,6},{2,5},{3,3},{4,4},{5,2},{6,1},{7,7},{8,8},{9,14},{10,1... | collective-permute-start | bytes 98312 | tf_op jit(solution)/shard_map/ppermute | solution.py:468
  16.6 3.9 %copy-start = (f32[1,3,3,16,8,128]{5,4,3,2,1,0:T(8,128)S(1)}, f32[1,3,3,16,8,128]{5,4,3,2,1,0:T(8,128)}, u32[]{:S(2)}) copy-start(f32[1,3,3,16,8,128]{5,4,3,2,1,0:T(8,128)} %sm_ref.1) | copy-start | bytes 1769476
  17.5 3.0 %copy-start.2 = (f32[1,3,16,8,128]{4,3,2,1,0:T(8,128)S(1)}, f32[1,3,16,8,128]{4,3,2,1,0:T(8,128)}, u32[]{:S(2)}) copy-start(f32[1,3,16,8,128]{4,3,2,1,0:T(8,128)} %bm_ref.1) | copy-start | bytes 589828
  17.5 3.0 %copy-start.8 = (f32[16,8,128]{2,1,0:T(8,128)S(1)}, f32[16,8,128]{2,1,0:T(8,128)}, u32[]{:S(2)}) copy-start(f32[16,8,128]{2,1,0:T(8,128)} %sat_ref.1) | copy-start | bytes 196612
  17.5 1.4 %collective-permute-start.5 = (f32[2,16,8,128]{3,2,1,0:T(8,128)S(1)}, f32[2,16,8,128]{3,2,1,0:T(8,128)S(1)}, u32[]{:S(2)}, u32[]{:S(2)}) collective-permute-start(f32[2,16,8,128]{3,2,1,0:T(8,128)S(1)} %get-tuple-element.49), channel_id=1, source_target_pairs={{0,8},{8,0},{16,24},{24,16},{1,9},{9,1},{17,25},{25,17},{2,10},{10... | collective-permute-start | bytes 393224 | tf_op jit(solution)/shard_map/ppermute | solution.py:477
  19.0 5.6 %collective-permute-start.6 = (f32[2,16,8,128]{3,2,1,0:T(8,128)S(1)}, f32[2,16,8,128]{3,2,1,0:T(8,128)S(1)}, u32[]{:S(2)}, u32[]{:S(2)}) collective-permute-start(f32[2,16,8,128]{3,2,1,0:T(8,128)S(1)} %add.6), channel_id=1, source_target_pairs={{0,16},{8,24},{16,0},{24,8},{1,17},{9,25},{17,1},{25,9},{2,18},{10... | collective-permute-start | bytes 393224 | tf_op jit(solution)/shard_map/ppermute | solution.py:477

commit v5 on v4

--- a/solution.py
+++ b/solution.py
@@ -23,7 +23,7 @@
     + [("z1", 1), ("atten", 1), ("mask", 1), ("mask", 2)]
 )
 X_AT = {key: at for at, key in enumerate(X_LIST)}
-PACK_ARGS = 14
+PACK_ARGS, SMALL, KEPT, PARTS = 14, 5, (6, 7, 8, 9, 10), 2
 D_LIST = [(t, 1) for t in range(4)] + [(t, 2) for t in range(3)] + [(0, 3)]
 
 
@@ -92,8 +92,16 @@
 ):
     nx, ny, cx = counts
     count_ref, given, rest = refs[0], refs[1:PACK_ARGS], refs[PACK_ARGS:]
-    outs, held, sems = rest[: 7 + 3 * np_], rest[7 + 3 * np_ : -1], rest[-1]
-    copies = [pltpu.make_async_copy(a, b, sems.at[k]) for k, (a, b) in enumerate(zip(given, held))]
+    n = 7 + 3 * np_
+    outs, kept, own, sems = rest[:n], rest[n : n + len(KEPT)], rest[n + len(KEPT) : -1], rest[-1]
+    held = (*own[:SMALL], *kept, *own[SMALL:])
+    pairs = list(zip(given[:SMALL], held[:SMALL]))
+    for part in range(PARTS):
+        planes = pl.ds(part * (cx // PARTS), cx // PARTS)
+        for a, b in zip(given[SMALL:], held[SMALL:]):
+            lead = (slice(None),) * (len(a.shape) - 3)
+            pairs.append((a.at[(*lead, planes)], b.at[(*lead, planes)]))
+    copies = [pltpu.make_async_copy(a, b, sems.at[k]) for k, (a, b) in enumerate(pairs)]
     for copy in copies:
         copy.start()
     (cells_ref, relax_ref, weight_ref, slow_ref, amp_ref, buoy_ref, mu_ref, kappa_ref, at_ref, w_ref, v_ref, bm_ref,
@@ -120,7 +128,7 @@
     )
     mask_ref[...] = mask.reshape(cx, TILE[0], TILE[1])
 
-    for copy in copies[1:]:
+    for copy in copies[1:SMALL]:
         copy.wait()
     decay, gain = decay_gain(relax_ref, weight_ref)
     for l in range(3):
@@ -143,7 +151,12 @@
             row == 3, roll(live, shift, 0), jnp.where(row == 4, roll(live, -shift, 0), field)
         )
 
+    size = len(given) - SMALL
     for x in range(cx):
+        if x % (cx // PARTS) == 0:
+            at = SMALL + x // (cx // PARTS) * size
+            for copy in copies[at : at + size]:
+                copy.wait()
         w = [w_ref[0, c, x] for c in range(3)]
         kappa, mu, atten = kappa_ref[x], mu_ref[x], at_ref[x]
         bb = DT2 * buoy_ref[x]
@@ -511,16 +524,18 @@
         out_shape=[field(4, cx)] * 2
         + [field(len(X_LIST))] * np_
         + [field(len(D_LIST))] * (2 * np_)
-        + [field(cx), field(12), field(3, cx), field(cx), field(cx)],
+        + [field(cx), field(12), field(3, cx), field(cx), field(cx)]
+        + [jax.ShapeDtypeStruct(pack_args[k].shape, f32) for k in KEPT],
         in_specs=[
             pl.BlockSpec(memory_space=pltpu.HBM if given.size > 1 else pltpu.SMEM) for given in pack_args
         ],
-        out_specs=[vmem()] * (2 + 3 * np_ + 5),
+        out_specs=[vmem()] * (2 + 3 * np_ + 5 + len(KEPT)),
         scratch_shapes=[
             (pltpu.SMEM if k in (1, 2, 3, 4) else pltpu.VMEM)(given.shape, given.dtype)
             for k, given in enumerate(pack_args[1:])
+            if k + 1 not in KEPT
         ]
-        + [pltpu.SemaphoreType.DMA((PACK_ARGS - 1,))],
+        + [pltpu.SemaphoreType.DMA((SMALL + PARTS * (PACK_ARGS - 1 - SMALL),))],
         compiler_params=params,
         name="pack",
     )(
@@ -535,7 +550,7 @@
     ds = [
         matched(packed[2 + np_ + 2 * p + q], shape, True, True, p, q) for p in range(np_) for q in range(2)
     ]
-    mask, coef, base, zsum, z1 = packed[2 + 3 * np_ :]
+    mask, coef, base, zsum, z1, inverse, shear, bulk, atten, wave = packed[2 + 3 * np_ :]
 
     first = pl.pallas_call(
         functools.partial(first_kernel, counts, np_),
@@ -557,7 +572,7 @@
         compiler_params=params,
         name="first",
     )(
-        adjoint_now, bulk_modulus, shear_modulus, buoyancy, bulk_atten, forward_strain, event_onset, coef, mask, base, zsum, z1, *ys, *xs, *ds,
+        wave, bulk, shear, inverse, atten, forward_strain, event_onset, coef, mask, base, zsum, z1, *ys, *xs, *ds,
     )
     term, w1, d0, l0, d1, l1, pb, ph = first
     total = event_sum(term)
@@ -571,7 +586,7 @@
         cost_estimate=pl.CostEstimate(flops=3_000_000, bytes_accessed=4_000_000, transcendentals=0),
         name="last",
     )(
-        adjoint_now, bulk_memory, shear_memory, bulk_modulus, shear_modulus, buoyancy, bulk_atten, shear_atten,
+        wave, bulk_memory, shear_memory, bulk, shear, inverse, atten, shear_atten,
         event_onset, coef, mask, w1, d0, l0, d1, l1, pb, ph,
     )
     return w2, before, bulk_next, shear_next, total[0], total[1]

time: 25.5 us -> 25.3 us (level)
  no operation moved by 1% of the time
where the time goes in v5:
time: 25.3 us; the launch traced here: 25.1 us
  starting transfers between devices  10.3 us (41%)
  waiting for transfers between devices  8.18 us (32%)
  Pallas kernels  3.83 us (15%)
  between operations  2.03 us (8%)
  local copies, waits for them, and re-layouts  0.68 us (3%)
    ppermute x5, starting transfers between devices, matched(): return lax.ppermute(value, ('gx', 'gy'), pairs)  8.67 us
    ppermute x2, waiting for transfers between devices, event_sum(): lax.ppermute(value, 'event', [(e, e ^ step) for e in range(count)])  4.14 us
    ppermute x5, waiting for transfers between devices, matched(): return lax.ppermute(value, ('gx', 'gy'), pairs)  4.04 us
    pallas_call x1, Pallas kernels, body(): pl.pallas_call(functools.partial(pack_kernel, counts, np_), out_shape=[fi...  1.76 us
    ppermute x2, starting transfers between devices, event_sum(): lax.ppermute(value, 'event', [(e, e ^ step) for e in range(count)])  1.66 us
    pallas_call x1, Pallas kernels, body(): pl.pallas_call(functools.partial(last_kernel, counts), out_shape=[field(1...  1.22 us
    pallas_call x1, Pallas kernels, body(): pl.pallas_call(functools.partial(first_kernel, counts, np_), out_shape=[f...  0.86 us
    squeeze x1, local copies, waits for them, and re-layouts, body(): return (w2, before, bulk_next, shear_next, total[0], total[1])  0.66 us
  transfers between devices with their start and end apart: 7, of which 4 were waited for; matrix products, arithmetic and copies ran while one was open for 0% of the time, Pallas kernels for 5%

profile of v5, /device:TPU:8, one launch (start us, length us, event | category | flops | bytes accessed | tf_op | source)
XLA Modules:
  0.0 25.1 jit_solution(6950439531213438846)
XLA Ops:
  1.3 0.0 copy-start.2
  1.3 1.8 %pack.1 = (f32[4,16,8,128]{3,2,1,0:T(8,128)S(1)}, f32[4,16,8,128]{3,2,1,0:T(8,128)S(1)}, f32[30,8,128]{2,1,0:T(8,128)S(1)}, f32[8,8,128]{2,1,0:T(8,128)S(1)}, f3...) custom-call(s32[1,1]{1,0:T(1,128)S(6)} %copy.24.refs_0_, ...), custom_call_target="tpu_custom_call" | custom-call | tf_op jit(solution)/shard_map/pack/pallas_call | solution.py:522
  3.1 0.1 collective-permute-start
  3.1 5.0 %collective-permute-start.1 = (f32[4,16,8,128]{3,2,1,0:T(8,128)S(1)}, f32[4,16,8,128]{3,2,1,0:T(8,128)S(1)}, u32[]{:S(2)}, u32[]{:S(2)}) collective-permute-start(f32[4,16,8,128]{3,2,1,0:T(8,128)S(1)} %get-tuple-element.44), channel_id=1, source_target_pairs={{0,0},{1,2},{2,1},{3,3},{4,4},{5,6},{6,5},{7,7},{8,8},{9,10},{10,9... | collective-permute-start | bytes 786440 | tf_op jit(solution)/shard_map/ppermute | solution.py:481
  8.2 1.5 %collective-permute-start.2 = (f32[30,8,128]{2,1,0:T(8,128)S(1)}, f32[30,8,128]{2,1,0:T(8,128)S(1)}, u32[]{:S(2)}, u32[]{:S(2)}) collective-permute-start(f32[30,8,128]{2,1,0:T(8,128)S(1)} %get-tuple-element.45), channel_id=1, source_target_pairs={{0,4},{1,5},{2,6},{3,7},{4,0},{5,1},{6,2},{7,3},{8,12},{9,13},{10,... | collective-permute-start | bytes 368648 | tf_op jit(solution)/shard_map/ppermute | solution.py:481
  9.7 0.0 collective-permute-start.3
  9.7 2.0 %collective-permute-start.4 = (f32[8,8,128]{2,1,0:T(8,128)S(1)}, f32[8,8,128]{2,1,0:T(8,128)S(1)}, u32[]{:S(2)}, u32[]{:S(2)}) collective-permute-start(f32[8,8,128]{2,1,0:T(8,128)S(1)} %get-tuple-element.47), channel_id=1, source_target_pairs={{0,0},{1,6},{2,5},{3,3},{4,4},{5,2},{6,1},{7,7},{8,8},{9,14},{10,1... | collective-permute-start | bytes 98312 | tf_op jit(solution)/shard_map/ppermute | solution.py:481
  12.4 2.3 %collective-permute-done.3.rest_3_ = f32[8,8,128]{2,1,0:T(8,128)S(1)} collective-permute-done((f32[8,8,128]{2,1,0:T(8,128)S(1)}, f32[8,8,128]{2,1,0:T(8,128)S(1)}, u32[]{:S(2)}, u32[]{:S(2)}) %collective-permute-start.3) | collective-permute-done | bytes 32800 | tf_op jit(solution)/shard_map/ppermute | solution.py:481
  14.7 1.7 %collective-permute-done.4.rest_4_ = f32[8,8,128]{2,1,0:T(8,128)S(1)} collective-permute-done((f32[8,8,128]{2,1,0:T(8,128)S(1)}, f32[8,8,128]{2,1,0:T(8,128)S(1)}, u32[]{:S(2)}, u32[]{:S(2)}) %collective-permute-start.4) | collective-permute-done | bytes 32800 | tf_op jit(solution)/shard_map/ppermute | solution.py:481
  16.4 0.0 collective-permute-done.2.rest_2_
  16.4 0.0 collective-permute-done.rest_0_
  16.4 0.0 collective-permute-done.1.rest_1_
  16.4 0.0 copy-done.2
  16.5 0.0 copy-start
  16.5 0.9 %first.1 = (f32[2,16,8,128]{3,2,1,0:T(8,128)S(1)}, f32[3,16,8,128]{3,2,1,0:T(8,128)S(1)}, f32[16,8,128]{2,1,0:T(8,128)S(1)}, f32[3,16,8,128]{3,2,1,0:T(8,128)S(1...) custom-call(f32[1,3,16,8,128]{4,3,2,1,0:T(8,128)S(1)} %get-tuple-ele, ...), custom_call_target="tpu_custom_call" | custom-call | tf_op jit(solution)/shard_map/first/pallas_call | solution.py:555
  17.3 0.0 copy-start.1
  17.3 0.0 copy-start.3
  17.4 0.1 collective-permute-start.5
  17.4 1.3 %collective-permute-done.5 = f32[2,16,8,128]{3,2,1,0:T(8,128)S(1)} collective-permute-done((f32[2,16,8,128]{3,2,1,0:T(8,128)S(1)}, f32[2,16,8,128]{3,2,1,0:T(8,128)S(1)}, u32[]{:S(2)}, u32[]{:S(2)}) %collective-permute-start.5) | collective-permute-done | bytes 131104 | tf_op jit(solution)/shard_map/ppermute | solution.py:490
  18.8 1.6 %collective-permute-start.6 = (f32[2,16,8,128]{3,2,1,0:T(8,128)S(1)}, f32[2,16,8,128]{3,2,1,0:T(8,128)S(1)}, u32[]{:S(2)}, u32[]{:S(2)}) collective-permute-start(f32[2,16,8,128]{3,2,1,0:T(8,128)S(1)} %add.6), channel_id=1, source_target_pairs={{0,16},{8,24},{16,0},{24,8},{1,17},{9,25},{17,1},{25,9},{2,18},{10... | collective-permute-start | bytes 393224 | tf_op jit(solution)/shard_map/ppermute | solution.py:490
  20.4 0.0 copy-done
  20.4 0.0 copy-done.1
  20.4 0.0 copy-done.3
  20.4 1.2 %last.1 = (f32[1,3,16,8,128]{4,3,2,1,0:T(8,128)}, f32[1,3,16,8,128]{4,3,2,1,0:T(8,128)}, f32[1,3,16,8,128]{4,3,2,1,0:T(8,128)}, f32[1,3,3,16,8,128]{5,4,3,2,1,0:T(8,128)}) custom-call(f32[1,3,16,8,128]{4,3,2,1,0:T(8,128)S(1)} %get-tuple-element.33.w_ref, f32[1,3,16,8,128]{4,3,2,1,0:T(8,128)S(1)} %copy-done.1, f32[1,3,3,16,8,128]{5,4,3,2,1,0:T(8,128)S(1)} %copy-done, ...), custom_call_target="tpu_custom_call" | custom-call | flops 3000000 | bytes 4000000 | tf_op jit(solution)/shard_map/last/pallas_call | solution.py:580
  21.6 2.8 %collective-permute-done.6 = f32[2,16,8,128]{3,2,1,0:T(8,128)S(1)} collective-permute-done((f32[2,16,8,128]{3,2,1,0:T(8,128)S(1)}, f32[2,16,8,128]{3,2,1,0:T(8,128)S(1)}, u32[]{:S(2)}, u32[]{:S(2)}) %collective-permute-start.6) | collective-permute-done | bytes 131104 | tf_op jit(solution)/shard_map/ppermute | solution.py:490
  24.4 0.7 %slice_bitcast_fusion = (f32[16,8,128]{2,1,0:T(8,128)}, f32[16,8,128]{2,1,0:T(8,128)}) fusion(f32[2,16,8,128]{3,2,1,0:T(8,128)S(1)} %add.7), kind=kLoop, calls=%fused_computation | loop fusion | bytes 262144 | tf_op jit(solution)/shard_map/squeeze | solution.py:592
  (2 shorter events, 0.0 us)
Async XLA Ops:
  1.3 15.2 %copy-start.2 = (f32[1,2,4,16,8,128]{5,4,3,2,1,0:T(8,128)S(1)}, f32[1,2,4,16,8,128]{5,4,3,2,1,0:T(8,128)}, u32[]{:S(2)}) copy-start(f32[1,2,4,16,8,128]{5,4,3,2,1,0:T(8,128)} %strain_ref.1) | copy-start | bytes 1572868
  3.1 13.4 %collective-permute-start = (f32[4,16,8,128]{3,2,1,0:T(8,128)S(1)}, f32[4,16,8,128]{3,2,1,0:T(8,128)S(1)}, u32[]{:S(2)}, u32[]{:S(2)}) collective-permute-start(f32[4,16,8,128]{3,2,1,0:T(8,128)S(1)} %get-tuple-element.43), channel_id=1, source_target_pairs={{0,1},{1,0},{2,3},{3,2},{4,5},{5,4},{6,7},{7,6},{8,9},{9,8},{10,11... | collective-permute-start | bytes 786440 | tf_op jit(solution)/shard_map/ppermute | solution.py:481
  3.1 13.3 %collective-permute-start.1 = (f32[4,16,8,128]{3,2,1,0:T(8,128)S(1)}, f32[4,16,8,128]{3,2,1,0:T(8,128)S(1)}, u32[]{:S(2)}, u32[]{:S(2)}) collective-permute-start(f32[4,16,8,128]{3,2,1,0:T(8,128)S(1)} %get-tuple-element.44), channel_id=1, source_target_pairs={{0,0},{1,2},{2,1},{3,3},{4,4},{5,6},{6,5},{7,7},{8,8},{9,10},{10,9... | collective-permute-start | bytes 786440 | tf_op jit(solution)/shard_map/ppermute | solution.py:481
  8.2 8.3 %collective-permute-start.2 = (f32[30,8,128]{2,1,0:T(8,128)S(1)}, f32[30,8,128]{2,1,0:T(8,128)S(1)}, u32[]{:S(2)}, u32[]{:S(2)}) collective-permute-start(f32[30,8,128]{2,1,0:T(8,128)S(1)} %get-tuple-element.45), channel_id=1, source_target_pairs={{0,4},{1,5},{2,6},{3,7},{4,0},{5,1},{6,2},{7,3},{8,12},{9,13},{10,... | collective-permute-start | bytes 368648 | tf_op jit(solution)/shard_map/ppermute | solution.py:481
  9.7 5.0 %collective-permute-start.3 = (f32[8,8,128]{2,1,0:T(8,128)S(1)}, f32[8,8,128]{2,1,0:T(8,128)S(1)}, u32[]{:S(2)}, u32[]{:S(2)}) collective-permute-start(f32[8,8,128]{2,1,0:T(8,128)S(1)} %get-tuple-element.46), channel_id=1, source_target_pairs={{0,5},{1,4},{2,7},{3,6},{4,1},{5,0},{6,3},{7,2},{8,13},{9,12},{10,... | collective-permute-start | bytes 98312 | tf_op jit(solution)/shard_map/ppermute | solution.py:481
  9.7 6.7 %collective-permute-start.4 = (f32[8,8,128]{2,1,0:T(8,128)S(1)}, f32[8,8,128]{2,1,0:T(8,128)S(1)}, u32[]{:S(2)}, u32[]{:S(2)}) collective-permute-start(f32[8,8,128]{2,1,0:T(8,128)S(1)} %get-tuple-element.47), channel_id=1, source_target_pairs={{0,0},{1,6},{2,5},{3,3},{4,4},{5,2},{6,1},{7,7},{8,8},{9,14},{10,1... | collective-permute-start | bytes 98312 | tf_op jit(solution)/shard_map/ppermute | solution.py:481
  16.5 3.9 %copy-start = (f32[1,3,3,16,8,128]{5,4,3,2,1,0:T(8,128)S(1)}, f32[1,3,3,16,8,128]{5,4,3,2,1,0:T(8,128)}, u32[]{:S(2)}) copy-start(f32[1,3,3,16,8,128]{5,4,3,2,1,0:T(8,128)} %sm_ref.1) | copy-start | bytes 1769476
  17.3 3.0 %copy-start.1 = (f32[1,3,16,8,128]{4,3,2,1,0:T(8,128)S(1)}, f32[1,3,16,8,128]{4,3,2,1,0:T(8,128)}, u32[]{:S(2)}) copy-start(f32[1,3,16,8,128]{4,3,2,1,0:T(8,128)} %bm_ref.1) | copy-start | bytes 589828
  17.3 3.0 %copy-start.3 = (f32[16,8,128]{2,1,0:T(8,128)S(1)}, f32[16,8,128]{2,1,0:T(8,128)}, u32[]{:S(2)}) copy-start(f32[16,8,128]{2,1,0:T(8,128)} %sat_ref.1) | copy-start | bytes 196612
  17.4 1.4 %collective-permute-start.5 = (f32[2,16,8,128]{3,2,1,0:T(8,128)S(1)}, f32[2,16,8,128]{3,2,1,0:T(8,128)S(1)}, u32[]{:S(2)}, u32[]{:S(2)}) collective-permute-start(f32[2,16,8,128]{3,2,1,0:T(8,128)S(1)} %get-tuple-element.59), channel_id=1, source_target_pairs={{0,8},{8,0},{16,24},{24,16},{1,9},{9,1},{17,25},{25,17},{2,10},{10... | collective-permute-start | bytes 393224 | tf_op jit(solution)/shard_map/ppermute | solution.py:490
  18.8 5.6 %collective-permute-start.6 = (f32[2,16,8,128]{3,2,1,0:T(8,128)S(1)}, f32[2,16,8,128]{3,2,1,0:T(8,128)S(1)}, u32[]{:S(2)}, u32[]{:S(2)}) collective-permute-start(f32[2,16,8,128]{3,2,1,0:T(8,128)S(1)} %add.6), channel_id=1, source_target_pairs={{0,16},{8,24},{16,0},{24,8},{1,17},{9,25},{17,1},{25,9},{2,18},{10... | collective-permute-start | bytes 393224 | tf_op jit(solution)/shard_map/ppermute | solution.py:490

commit v6 on v5

--- a/solution.py
+++ b/solution.py
@@ -485,10 +485,10 @@
     count = lax.axis_size("event")
     if count & (count - 1):
         return lax.psum(value, "event")
-    step = 1
-    while step < count:
+    step = count // 2
+    while step > 0:
         value = value + lax.ppermute(value, "event", [(e, e ^ step) for e in range(count)])
-        step *= 2
+        step //= 2
     return value
 
 

time: 25.3 us -> 25.2 us (level)
  the two profiles are of different devices: /device:TPU:8 before, /device:TPU:9 now
where the time goes in v6:
time: 25.2 us; the launch traced here: 25.1 us
  starting transfers between devices  12.5 us (50%)
  waiting for transfers between devices  6 us (24%)
  Pallas kernels  3.83 us (15%)
  between operations  2.02 us (8%)
  local copies, waits for them, and re-layouts  0.68 us (3%)
    ppermute x5, starting transfers between devices, matched(): return lax.ppermute(value, ('gx', 'gy'), pairs)  7.73 us
    ppermute x2, starting transfers between devices, event_sum(): lax.ppermute(value, 'event', [(e, e ^ step) for e in range(count)])  4.75 us
    ppermute x5, waiting for transfers between devices, matched(): return lax.ppermute(value, ('gx', 'gy'), pairs)  3.42 us
    ppermute x2, waiting for transfers between devices, event_sum(): lax.ppermute(value, 'event', [(e, e ^ step) for e in range(count)])  2.58 us
    pallas_call x1, Pallas kernels, body(): pl.pallas_call(functools.partial(pack_kernel, counts, np_), out_shape=[fi...  1.76 us
    pallas_call x1, Pallas kernels, body(): pl.pallas_call(functools.partial(last_kernel, counts), out_shape=[field(1...  1.22 us
    pallas_call x1, Pallas kernels, body(): pl.pallas_call(functools.partial(first_kernel, counts, np_), out_shape=[f...  0.86 us
    squeeze x1, local copies, waits for them, and re-layouts, body(): return (w2, before, bulk_next, shear_next, total[0], total[1])  0.66 us
  transfers between devices with their start and end apart: 7, of which 3 were waited for; matrix products, arithmetic and copies ran while one was open for 0% of the time, Pallas kernels for 5%

profile of v6, /device:TPU:9, one launch (start us, length us, event | category | flops | bytes accessed | tf_op | source)
XLA Modules:
  0.0 25.1 jit_solution(9265688772157827349)
XLA Ops:
  1.3 0.0 copy-start.2
  1.3 1.8 %pack.1 = (f32[4,16,8,128]{3,2,1,0:T(8,128)S(1)}, f32[4,16,8,128]{3,2,1,0:T(8,128)S(1)}, f32[30,8,128]{2,1,0:T(8,128)S(1)}, f32[8,8,128]{2,1,0:T(8,128)S(1)}, f3...) custom-call(s32[1,1]{1,0:T(1,128)S(6)} %copy.24.refs_0_, ...), custom_call_target="tpu_custom_call" | custom-call | tf_op jit(solution)/shard_map/pack/pallas_call | solution.py:522
  3.1 0.1 collective-permute-start
  3.1 4.5 %collective-permute-start.1 = (f32[4,16,8,128]{3,2,1,0:T(8,128)S(1)}, f32[4,16,8,128]{3,2,1,0:T(8,128)S(1)}, u32[]{:S(2)}, u32[]{:S(2)}) collective-permute-start(f32[4,16,8,128]{3,2,1,0:T(8,128)S(1)} %get-tuple-element.44), channel_id=1, source_target_pairs={{0,0},{1,2},{2,1},{3,3},{4,4},{5,6},{6,5},{7,7},{8,8},{9,10},{10,9... | collective-permute-start | bytes 786440 | tf_op jit(solution)/shard_map/ppermute | solution.py:481
  7.6 1.3 %collective-permute-start.2 = (f32[30,8,128]{2,1,0:T(8,128)S(1)}, f32[30,8,128]{2,1,0:T(8,128)S(1)}, u32[]{:S(2)}, u32[]{:S(2)}) collective-permute-start(f32[30,8,128]{2,1,0:T(8,128)S(1)} %get-tuple-element.45), channel_id=1, source_target_pairs={{0,4},{1,5},{2,6},{3,7},{4,0},{5,1},{6,2},{7,3},{8,12},{9,13},{10,... | collective-permute-start | bytes 368648 | tf_op jit(solution)/shard_map/ppermute | solution.py:481
  8.9 0.0 collective-permute-start.3
  8.9 1.9 %collective-permute-start.4 = (f32[8,8,128]{2,1,0:T(8,128)S(1)}, f32[8,8,128]{2,1,0:T(8,128)S(1)}, u32[]{:S(2)}, u32[]{:S(2)}) collective-permute-start(f32[8,8,128]{2,1,0:T(8,128)S(1)} %get-tuple-element.47), channel_id=1, source_target_pairs={{0,0},{1,6},{2,5},{3,3},{4,4},{5,2},{6,1},{7,7},{8,8},{9,14},{10,1... | collective-permute-start | bytes 98312 | tf_op jit(solution)/shard_map/ppermute | solution.py:481
  11.5 1.2 %collective-permute-done.3.rest_3_ = f32[8,8,128]{2,1,0:T(8,128)S(1)} collective-permute-done((f32[8,8,128]{2,1,0:T(8,128)S(1)}, f32[8,8,128]{2,1,0:T(8,128)S(1)}, u32[]{:S(2)}, u32[]{:S(2)}) %collective-permute-start.3) | collective-permute-done | bytes 32800 | tf_op jit(solution)/shard_map/ppermute | solution.py:481
  12.7 2.2 %collective-permute-done.4.rest_4_ = f32[8,8,128]{2,1,0:T(8,128)S(1)} collective-permute-done((f32[8,8,128]{2,1,0:T(8,128)S(1)}, f32[8,8,128]{2,1,0:T(8,128)S(1)}, u32[]{:S(2)}, u32[]{:S(2)}) %collective-permute-start.4) | collective-permute-done | bytes 32800 | tf_op jit(solution)/shard_map/ppermute | solution.py:481
  14.9 0.0 collective-permute-done.2.rest_2_
  14.9 0.0 collective-permute-done.rest_0_
  14.9 0.0 collective-permute-done.1.rest_1_
  14.9 0.0 copy-done.2
  14.9 0.0 copy-start
  14.9 0.9 %first.1 = (f32[2,16,8,128]{3,2,1,0:T(8,128)S(1)}, f32[3,16,8,128]{3,2,1,0:T(8,128)S(1)}, f32[16,8,128]{2,1,0:T(8,128)S(1)}, f32[3,16,8,128]{3,2,1,0:T(8,128)S(1...) custom-call(f32[1,3,16,8,128]{4,3,2,1,0:T(8,128)S(1)} %get-tuple-ele, ...), custom_call_target="tpu_custom_call" | custom-call | tf_op jit(solution)/shard_map/first/pallas_call | solution.py:555
  15.8 0.0 copy-start.1
  15.8 0.0 copy-start.3
  15.8 1.3 %collective-permute-start.5 = (f32[2,16,8,128]{3,2,1,0:T(8,128)S(1)}, f32[2,16,8,128]{3,2,1,0:T(8,128)S(1)}, u32[]{:S(2)}, u32[]{:S(2)}) collective-permute-start(f32[2,16,8,128]{3,2,1,0:T(8,128)S(1)} %get-tuple-element.59), channel_id=1, source_target_pairs={{0,16},{8,24},{16,0},{24,8},{1,17},{9,25},{17,1},{25,9},{2,18},{10... | collective-permute-start | bytes 393224 | tf_op jit(solution)/shard_map/ppermute | solution.py:490
  17.1 2.6 %collective-permute-done.5 = f32[2,16,8,128]{3,2,1,0:T(8,128)S(1)} collective-permute-done((f32[2,16,8,128]{3,2,1,0:T(8,128)S(1)}, f32[2,16,8,128]{3,2,1,0:T(8,128)S(1)}, u32[]{:S(2)}, u32[]{:S(2)}) %collective-permute-start.5) | collective-permute-done | bytes 131104 | tf_op jit(solution)/shard_map/ppermute | solution.py:490
  19.7 3.4 %collective-permute-start.6 = (f32[2,16,8,128]{3,2,1,0:T(8,128)S(1)}, f32[2,16,8,128]{3,2,1,0:T(8,128)S(1)}, u32[]{:S(2)}, u32[]{:S(2)}) collective-permute-start(f32[2,16,8,128]{3,2,1,0:T(8,128)S(1)} %add.6), channel_id=1, source_target_pairs={{0,8},{8,0},{16,24},{24,16},{1,9},{9,1},{17,25},{25,17},{2,10},{10... | collective-permute-start | bytes 393224 | tf_op jit(solution)/shard_map/ppermute | solution.py:490
  23.1 0.0 copy-done
  23.1 0.0 copy-done.1
  23.2 0.0 copy-done.3
  23.2 1.2 %last.1 = (f32[1,3,16,8,128]{4,3,2,1,0:T(8,128)}, f32[1,3,16,8,128]{4,3,2,1,0:T(8,128)}, f32[1,3,16,8,128]{4,3,2,1,0:T(8,128)}, f32[1,3,3,16,8,128]{5,4,3,2,1,0:T(8,128)}) custom-call(f32[1,3,16,8,128]{4,3,2,1,0:T(8,128)S(1)} %get-tuple-element.33.w_ref, f32[1,3,16,8,128]{4,3,2,1,0:T(8,128)S(1)} %copy-done.1, f32[1,3,3,16,8,128]{5,4,3,2,1,0:T(8,128)S(1)} %copy-done, ...), custom_call_target="tpu_custom_call" | custom-call | flops 3000000 | bytes 4000000 | tf_op jit(solution)/shard_map/last/pallas_call | solution.py:580
  24.4 0.0 collective-permute-done.6
  24.4 0.7 %slice_bitcast_fusion = (f32[16,8,128]{2,1,0:T(8,128)}, f32[16,8,128]{2,1,0:T(8,128)}) fusion(f32[2,16,8,128]{3,2,1,0:T(8,128)S(1)} %add.7), kind=kLoop, calls=%fused_computation | loop fusion | bytes 262144 | tf_op jit(solution)/shard_map/squeeze | solution.py:592
  (2 shorter events, 0.0 us)
Async XLA Ops:
  1.3 13.6 %copy-start.2 = (f32[1,2,4,16,8,128]{5,4,3,2,1,0:T(8,128)S(1)}, f32[1,2,4,16,8,128]{5,4,3,2,1,0:T(8,128)}, u32[]{:S(2)}) copy-start(f32[1,2,4,16,8,128]{5,4,3,2,1,0:T(8,128)} %strain_ref.1) | copy-start | bytes 1572868
  3.1 11.8 %collective-permute-start = (f32[4,16,8,128]{3,2,1,0:T(8,128)S(1)}, f32[4,16,8,128]{3,2,1,0:T(8,128)S(1)}, u32[]{:S(2)}, u32[]{:S(2)}) collective-permute-start(f32[4,16,8,128]{3,2,1,0:T(8,128)S(1)} %get-tuple-element.43), channel_id=1, source_target_pairs={{0,1},{1,0},{2,3},{3,2},{4,5},{5,4},{6,7},{7,6},{8,9},{9,8},{10,11... | collective-permute-start | bytes 786440 | tf_op jit(solution)/shard_map/ppermute | solution.py:481
  3.1 11.7 %collective-permute-start.1 = (f32[4,16,8,128]{3,2,1,0:T(8,128)S(1)}, f32[4,16,8,128]{3,2,1,0:T(8,128)S(1)}, u32[]{:S(2)}, u32[]{:S(2)}) collective-permute-start(f32[4,16,8,128]{3,2,1,0:T(8,128)S(1)} %get-tuple-element.44), channel_id=1, source_target_pairs={{0,0},{1,2},{2,1},{3,3},{4,4},{5,6},{6,5},{7,7},{8,8},{9,10},{10,9... | collective-permute-start | bytes 786440 | tf_op jit(solution)/shard_map/ppermute | solution.py:481
  7.6 7.3 %collective-permute-start.2 = (f32[30,8,128]{2,1,0:T(8,128)S(1)}, f32[30,8,128]{2,1,0:T(8,128)S(1)}, u32[]{:S(2)}, u32[]{:S(2)}) collective-permute-start(f32[30,8,128]{2,1,0:T(8,128)S(1)} %get-tuple-element.45), channel_id=1, source_target_pairs={{0,4},{1,5},{2,6},{3,7},{4,0},{5,1},{6,2},{7,3},{8,12},{9,13},{10,... | collective-permute-start | bytes 368648 | tf_op jit(solution)/shard_map/ppermute | solution.py:481
  8.9 3.8 %collective-permute-start.3 = (f32[8,8,128]{2,1,0:T(8,128)S(1)}, f32[8,8,128]{2,1,0:T(8,128)S(1)}, u32[]{:S(2)}, u32[]{:S(2)}) collective-permute-start(f32[8,8,128]{2,1,0:T(8,128)S(1)} %get-tuple-element.46), channel_id=1, source_target_pairs={{0,5},{1,4},{2,7},{3,6},{4,1},{5,0},{6,3},{7,2},{8,13},{9,12},{10,... | collective-permute-start | bytes 98312 | tf_op jit(solution)/shard_map/ppermute | solution.py:481
  8.9 6.0 %collective-permute-start.4 = (f32[8,8,128]{2,1,0:T(8,128)S(1)}, f32[8,8,128]{2,1,0:T(8,128)S(1)}, u32[]{:S(2)}, u32[]{:S(2)}) collective-permute-start(f32[8,8,128]{2,1,0:T(8,128)S(1)} %get-tuple-element.47), channel_id=1, source_target_pairs={{0,0},{1,6},{2,5},{3,3},{4,4},{5,2},{6,1},{7,7},{8,8},{9,14},{10,1... | collective-permute-start | bytes 98312 | tf_op jit(solution)/shard_map/ppermute | solution.py:481
  14.9 8.3 %copy-start = (f32[1,3,3,16,8,128]{5,4,3,2,1,0:T(8,128)S(1)}, f32[1,3,3,16,8,128]{5,4,3,2,1,0:T(8,128)}, u32[]{:S(2)}) copy-start(f32[1,3,3,16,8,128]{5,4,3,2,1,0:T(8,128)} %sm_ref.1) | copy-start | bytes 1769476
  15.8 7.4 %copy-start.1 = (f32[1,3,16,8,128]{4,3,2,1,0:T(8,128)S(1)}, f32[1,3,16,8,128]{4,3,2,1,0:T(8,128)}, u32[]{:S(2)}) copy-start(f32[1,3,16,8,128]{4,3,2,1,0:T(8,128)} %bm_ref.1) | copy-start | bytes 589828
  15.8 7.4 %copy-start.3 = (f32[16,8,128]{2,1,0:T(8,128)S(1)}, f32[16,8,128]{2,1,0:T(8,128)}, u32[]{:S(2)}) copy-start(f32[16,8,128]{2,1,0:T(8,128)} %sat_ref.1) | copy-start | bytes 196612
  15.8 3.9 %collective-permute-start.5 = (f32[2,16,8,128]{3,2,1,0:T(8,128)S(1)}, f32[2,16,8,128]{3,2,1,0:T(8,128)S(1)}, u32[]{:S(2)}, u32[]{:S(2)}) collective-permute-start(f32[2,16,8,128]{3,2,1,0:T(8,128)S(1)} %get-tuple-element.59), channel_id=1, source_target_pairs={{0,16},{8,24},{16,0},{24,8},{1,17},{9,25},{17,1},{25,9},{2,18},{10... | collective-permute-start | bytes 393224 | tf_op jit(solution)/shard_map/ppermute | solution.py:490
  19.7 4.7 %collective-permute-start.6 = (f32[2,16,8,128]{3,2,1,0:T(8,128)S(1)}, f32[2,16,8,128]{3,2,1,0:T(8,128)S(1)}, u32[]{:S(2)}, u32[]{:S(2)}) collective-permute-start(f32[2,16,8,128]{3,2,1,0:T(8,128)S(1)} %add.6), channel_id=1, source_target_pairs={{0,8},{8,0},{16,24},{24,16},{1,9},{9,1},{17,25},{25,17},{2,10},{10... | collective-permute-start | bytes 393224 | tf_op jit(solution)/shard_map/ppermute | solution.py:490
